TPU v7x, 512 devices: a whole 4x4x16 slice. The times are simulated.
512 devices in a mesh: seq: 32 (over y, x, core), ch: 16 (over z).
Axes of the slice: x: 4, y: 4, z: 16, core: 2. Of those that a mesh axis runs over, the one named last changes fastest.
Arguments:
- q_branch: bfloat16 [16384, 4096], P('seq', 'ch'), may hold values from -6 to 6
- k_branch: bfloat16 [16384, 4096], P('seq', 'ch'), may hold values from -6 to 6
- v_branch: bfloat16 [16384, 4096], P('seq', 'ch'), may hold values from -6 to 6
- decay_rates: float32 [16, 4096], P(None, 'ch'), may hold values from 1.2207031e-05 to 0.05
- residues: float32 [16, 4096], P(None, 'ch'), may hold values from -0.237170825 to 0.237170825
- skip_gain: float32 [4096], P('ch'), may hold values from 0.5 to 1.5
- out_weight: bfloat16 [4096, 4096], P(None, 'ch'), may hold values from -0.09375 to 0.09375
Outputs:
- mixed: bfloat16 [16384, 4096], P('seq', 'ch')
All inputs are finite; a program needn't handle non-finite values.
Results may differ from a plain program's by a relative error of at most 0.015.
Values may be sent and summed in bfloat16 or wider, within the bound.
No kernel may reach another device: no remote copies, remote signals or barrier semaphores. Data moves between devices by JAX's collectives and lax.ppermute only.
A program may use at most 64 MiB of HBM per device.

v0:
```python
import jax
import jax.numpy as jnp
from jax import lax
from jax.experimental import pallas as pl
from jax.experimental.pallas import tpu as pltpu
from jax.sharding import Mesh
from jax.sharding import PartitionSpec as P

BLOCKS = 8
LANES = 128
F32 = jnp.float32
BF16 = jnp.bfloat16


def fill_natural(core, own_ref, oth_ref, flat):
    rows = own_ref.shape[0]
    piece = 64
    own_at, oth_at = core * rows, (1 - core) * rows

    @pl.loop(0, rows // piece)
    def _(i):
        at = pl.multiple_of(i * piece, piece)
        for half in range(flat.shape[0]):
            lanes = slice(half * LANES, (half + 1) * LANES)
            flat[half, pl.ds(pl.multiple_of(own_at + at, piece), piece), :] = own_ref[pl.ds(at, piece), lanes].astype(F32)
            flat[half, pl.ds(pl.multiple_of(oth_at + at, piece), piece), :] = oth_ref[pl.ds(at, piece), lanes].astype(F32)


def spread(ref, mode, lanes):
    return jnp.broadcast_to(ref[mode : mode + 1, lanes], (BLOCKS, LANES))


def states_kernel(core_ref, own_ref, oth_ref, rates_ref, total_ref, ends_ref, flat):
    modes, width = rates_ref.shape
    steps = flat.shape[1] // BLOCKS
    fill_natural(core_ref[0], own_ref, oth_ref, flat)
    block = lax.broadcasted_iota(jnp.int32, (BLOCKS, LANES), 0).astype(F32)
    for half in range(width // LANES):
        lanes = slice(half * LANES, (half + 1) * LANES)
        poles = [jnp.exp(-spread(rates_ref, m, lanes)) for m in range(modes)]

        def step(j, held):
            now = flat[half, pl.ds(j, BLOCKS, stride=steps), :]
            return tuple(p * h + now for p, h in zip(poles, held))

        held = lax.fori_loop(0, steps, step, (jnp.zeros((BLOCKS, LANES), F32),) * modes, unroll=8)
        for m in range(modes):
            ends_ref[m, :, lanes] = held[m]
            fade = jnp.exp(-spread(rates_ref, m, lanes) * (steps * (BLOCKS - 1 - block)))
            total_ref[m : m + 1, lanes] = jnp.sum(fade * held[m], axis=0, keepdims=True)


def local_kernel(core_ref, own_ref, oth_ref, q_own_ref, q_oth_ref, rates_ref, resid_ref, skip_ref, ends_ref, conv_ref, gate_ref, flat, flat_q):
    modes, width = rates_ref.shape
    steps = flat.shape[1] // BLOCKS
    fill_natural(core_ref[0], own_ref, oth_ref, flat)
    fill_natural(core_ref[0], q_own_ref, q_oth_ref, flat_q)
    block = lax.broadcasted_iota(jnp.int32, (BLOCKS, LANES), 0)
    for half in range(width // LANES):
        lanes = slice(half * LANES, (half + 1) * LANES)
        poles, weights, first = [], [], []
        for m in range(modes):
            rate = spread(rates_ref, m, lanes)
            poles.append(jnp.exp(-rate))
            weights.append(spread(resid_ref, m, lanes))
            scan = ends_ref[m, :, lanes]
            for shift in (1, 2, 4):
                moved = jnp.where(block >= shift, pltpu.roll(scan, shift, 0), 0.0)
                scan = scan + jnp.exp(-rate * float(steps * shift)) * moved
            first.append(jnp.where(block >= 1, pltpu.roll(scan, 1, 0), 0.0))
        direct = jnp.broadcast_to(skip_ref[0:1, lanes], (BLOCKS, LANES))

        def step(j, held):
            now = flat[half, pl.ds(j, BLOCKS, stride=steps), :]
            held = tuple(p * h + now for p, h in zip(poles, held))
            terms = [w * h for w, h in zip(weights, held)]
            while len(terms) > 1:
                terms = [a + b for a, b in zip(terms[::2], terms[1::2])]
            conv_ref[j, :, lanes] = terms[0] + direct * now
            gate_ref[j, :, lanes] = flat_q[half, pl.ds(j, BLOCKS, stride=steps), :]
            return held

        lax.fori_loop(0, steps, step, tuple(first), unroll=4)


def gate_kernel(place_ref, all_ref, rates_ref, resid_ref, conv_ref, gate_ref, own_ref, oth_ref, flat):
    chips, modes, width = all_ref.shape
    steps = conv_ref.shape[0]
    chip, core = place_ref[0], place_ref[1]
    block = lax.broadcasted_iota(jnp.int32, (BLOCKS, LANES), 0).astype(F32)
    rates = rates_ref[...]
    fade = jnp.exp(-rates * float(steps * BLOCKS))
    before = jnp.zeros((modes, width), F32)
    for c in range(chips - 1):
        before = jnp.where(c < chip, fade * before + all_ref[c], before)
    before = before * resid_ref[...]
    for half in range(width // LANES):
        lanes = slice(half * LANES, (half + 1) * LANES)
        poles, first = [], []
        for m in range(modes):
            rate = spread(rates_ref, m, lanes)
            poles.append(jnp.exp(-rate))
            come = jnp.broadcast_to(before[m : m + 1, lanes], (BLOCKS, LANES))
            first.append(come * jnp.exp(-rate * (steps * block + 1.0)))

        def step(j, held):
            terms = list(held)
            while len(terms) > 1:
                terms = [a + b for a, b in zip(terms[::2], terms[1::2])]
            flat[half, pl.ds(j, BLOCKS, stride=steps), :] = gate_ref[j, :, lanes] * (conv_ref[j, :, lanes] + terms[0])
            return tuple(p * h for p, h in zip(poles, held))

        lax.fori_loop(0, steps, step, tuple(first), unroll=4)
    rows = own_ref.shape[0]
    piece = 64
    own_at, oth_at = core * rows, (1 - core) * rows

    @pl.loop(0, rows // piece)
    def _(i):
        at = pl.multiple_of(i * piece, piece)
        for half in range(flat.shape[0]):
            lanes = slice(half * LANES, (half + 1) * LANES)
            own_ref[pl.ds(at, piece), lanes] = flat[half, pl.ds(pl.multiple_of(own_at + at, piece), piece), :].astype(BF16)
            oth_ref[pl.ds(at, piece), lanes] = flat[half, pl.ds(pl.multiple_of(oth_at + at, piece), piece), :].astype(BF16)


VMEM = pl.BlockSpec(memory_space=pltpu.VMEM)
SMEM = pl.BlockSpec(memory_space=pltpu.SMEM)
PARAMS = pltpu.CompilerParams(vmem_limit_bytes=40 * 1024 * 1024)


def body(q_branch, k_branch, v_branch, decay_rates, residues, skip_gain, out_weight):
    rows, width = k_branch.shape
    modes = decay_rates.shape[0]
    steps = 2 * rows // BLOCKS
    chips = lax.axis_size("y") * lax.axis_size("x")
    depth = lax.axis_size("ch")
    core, z = lax.axis_index("core"), lax.axis_index("ch")
    chip = lax.axis_index("y") * lax.axis_size("x") + lax.axis_index("x")
    core_at = core.reshape(1).astype(jnp.int32)
    place = jnp.stack([chip, core]).astype(jnp.int32)
    shape = lambda s, d=F32: jax.ShapeDtypeStruct(s, d)
    swap = [(0, 1), (1, 0)]

    mixed_in = (k_branch.astype(F32) * v_branch.astype(F32)).astype(BF16)
    x_oth, q_oth = lax.ppermute(jnp.stack([mixed_in, q_branch]), "core", swap)

    total, ends = pl.pallas_call(
        states_kernel,
        out_shape=(shape((modes, width)), shape((modes, BLOCKS, width))),
        in_specs=[SMEM, VMEM, VMEM, VMEM],
        out_specs=(VMEM, VMEM),
        scratch_shapes=[pltpu.VMEM((width // LANES, 2 * rows, LANES), F32)],
        compiler_params=PARAMS,
        name="chip_states",
    )(core_at, mixed_in, x_oth, decay_rates)

    every = lax.all_to_all(
        jnp.broadcast_to(total[None], (chips, modes, width)), ("y", "x"), split_axis=0, concat_axis=0, tiled=True
    )
    conv, gate = pl.pallas_call(
        local_kernel,
        out_shape=(shape((steps, BLOCKS, width)), shape((steps, BLOCKS, width))),
        in_specs=[SMEM] + [VMEM] * 8,
        out_specs=(VMEM, VMEM),
        scratch_shapes=[pltpu.VMEM((width // LANES, 2 * rows, LANES), F32)] * 2,
        compiler_params=PARAMS,
        cost_estimate=pl.CostEstimate(flops=4 * modes * 2 * rows * width, bytes_accessed=4 << 20, transcendentals=0),
        name="chip_convolution",
    )(core_at, mixed_in, x_oth, q_branch, q_oth, decay_rates, residues, skip_gain[None, :], ends)

    own, oth = pl.pallas_call(
        gate_kernel,
        out_shape=(shape((rows, width), BF16), shape((rows, width), BF16)),
        in_specs=[SMEM] + [VMEM] * 5,
        out_specs=(VMEM, VMEM),
        scratch_shapes=[pltpu.VMEM((width // LANES, 2 * rows, LANES), F32)],
        compiler_params=PARAMS,
        name="carry_and_gate",
    )(place, every, decay_rates, residues, conv, gate)

    ring = [(c * depth + i, c * depth + (i + 1 - 2 * c) % depth) for c in range(2) for i in range(depth)]
    hop = lambda array: lax.ppermute(array, ("core", "ch"), ring)

    def project(array, distance):
        source = lax.rem(z + (2 * core - 1) * distance + depth, depth)
        weight = lax.dynamic_slice(out_weight, (source * width, 0), (width, out_weight.shape[1]))
        return jnp.dot(array, weight, preferred_element_type=F32)

    sum_own, sum_oth = project(own, 0), None
    for distance in range(1, depth // 2):
        own, oth = hop(own), hop(oth)
        sum_own = sum_own + project(own, distance)
        part = project(oth, distance)
        sum_oth = part if sum_oth is None else sum_oth + part
    own = hop(own)
    sum_own = sum_own + lax.ppermute(sum_oth, "core", swap) + project(own, depth // 2)
    return sum_own.astype(BF16)


def solution(mesh):
    chips = Mesh(mesh.devices.reshape(4, 4, 2, 16), ("y", "x", "core", "ch"))
    seq = ("y", "x", "core")
    placed = (P(seq, "ch"), P(seq, "ch"), P(seq, "ch"), P(None, "ch"), P(None, "ch"), P("ch"), P(None, "ch"))
    return jax.shard_map(body, mesh=chips, in_specs=placed, out_specs=P(seq, "ch"), check_vma=False)
```

profile of v0, /device:TPU:2, one launch (start us, length us, event | category | flops | bytes accessed | tf_op | source)
XLA Modules:
  0.0 126.0 jit_solution(13677500022443558087)
XLA Ops:
  0.0 1.3 multiply_convert_fusion.own_ref
  1.3 1.0 pad_maximum_fusion
  2.3 1.9 %collective-permute-start = (bf16[2,512,256]{2,1,0:T(8,128)(2,1)S(1)}, bf16[2,512,256]{2,1,0:T(8,128)(2,1)}, u32[]{:S(2)}, u32[]{:S(2)}) collective-permute-start(bf16[2,512,256]{2,1,0:T(8,128)(2,1)S(1)} %pad_maximum_fusion), channel_id=1, source_target_pairs={{0,16},{16,0},{1,17},{17,1},{2,18},{18,2},{3,19},{19,3},{4,20},{20... | collective-permute-start | bytes 1572872 | tf_op jit(solution)/shard_map/ppermute | solution.py:146
  4.2 2.0 %collective-permute-done = bf16[2,512,256]{2,1,0:T(8,128)(2,1)} collective-permute-done((bf16[2,512,256]{2,1,0:T(8,128)(2,1)S(1)}, bf16[2,512,256]{2,1,0:T(8,128)(2,1)}, u32[]{:S(2)}, u32[]{:S(2)}) %collective-permute-start) | collective-permute-done | bytes 524320 | tf_op jit(solution)/shard_map/ppermute | solution.py:146
  6.2 1.1 slice_bitcast_fusion
  7.3 1.8 %chip_states.1 = (f32[16,256]{1,0:T(8,128)S(1)}, f32[16,8,256]{2,1,0:T(8,128)S(1)}) custom-call(s32[1]{0:T(128)} %bitcast.1.core_ref, bf16[512,256]{1,0:T(8,128)(2,1)S(1)} %multiply_convert_fusion.own_ref, bf16[512,256]{1,0:T(8,128)(2,1)S(1)} %get-tuple-element.18.oth_ref, f32[16,256]{1,0:T(8,128)S(1)} %copy-done.6), custom_call_target="tpu_custom_call" | custom-call | tf_op jit(solution)/shard_map/chip_states/pallas_call | solution.py:148
  9.1 0.7 broadcast_in_dim.4
  9.8 9.2 %all-to-all-start = ((f32[16,16,256]{2,1,0:T(8,128)}), f32[16,16,256]{2,1,0:T(8,128)S(1)}, u32[]{:S(2)}, u32[]{:S(2)}) async-start(f32[16,16,256]{2,1,0:T(8,128)} %broadcast_in_dim.4), calls=%async_computation | async-start | bytes 524288 | tf_op jit(solution)/shard_map/all_to_all | solution.py:158
  19.0 0.6 pad_add_fusion.place_ref
  19.7 0.7 copy-done.7
  20.4 0.7 copy-done.9
  21.1 3.9 %chip_convolution.1 = (f32[128,8,256]{2,1,0:T(8,128)S(1)}, f32[128,8,256]{2,1,0:T(8,128)S(1)}) custom-call(s32[1]{0:T(128)} %bitcast.1.core_ref, bf16[512,256]{1,0:T(8,128)(2,1)S(1)} %multiply_convert_fusion.own_ref, bf16[512,256]{1,0:T(8,128)(2,1)S(1)} %get-tuple-element.18.oth_ref, bf16[512,256]{1,0:T(8,128)(2,1)S(1)} %copy-done.1, ...), custom_call_target="tpu_custom_call" | custom-call | flops 16777216 | bytes 4194304 | tf_op jit(solution)/shard_map/chip_convolution/pallas_call | solution.py:161
  25.0 1.0 copy-done.2
  25.9 1.0 copy-done.4
  27.0 1.2 copy-done.3
  28.2 1.2 copy-done.5
  29.5 0.7 copy-done.8
  30.2 0.7 copy-done.10
  30.8 2.2 %carry_and_gate.1 = (bf16[512,256]{1,0:T(8,128)(2,1)S(1)}, bf16[512,256]{1,0:T(8,128)(2,1)S(1)}) custom-call(s32[2]{0:T(128)S(1)} %copy-done.10, f32[16,16,256]{2,1,0:T(8,128)S(1)} %all-to-all-done.all_ref, f32[16,256]{1,0:T(8,128)S(1)} %copy-done.6, f32[16,256]{1,0:T(8,128)S(1)} %copy-done.8, f32[128,8,256]{2,1,0:T(8,128)S(1)} %copy-done.3, ...), custom_call_target="tpu_custom_call" | custom-call | tf_op jit(solution)/shard_map/carry_and_gate/pallas_call | solution.py:172
  33.1 2.0 %collective-permute-start.8 = (bf16[512,256]{1,0:T(8,128)(2,1)S(1)}, bf16[512,256]{1,0:T(8,128)(2,1)S(1)}, u32[]{:S(2)}, u32[]{:S(2)}) collective-permute-start(bf16[512,256]{1,0:T(8,128)(2,1)S(1)} %get-tuple-element.16), channel_id=1, source_target_pairs={{0,1},{1,2},{2,3},{3,4},{4,5},{5,6},{6,7},{7,8},{8,9},{9,10},{10,1... | collective-permute-start | bytes 786440 | tf_op jit(solution)/shard_map/ppermute | solution.py:183
  35.0 3.8 %collective-permute-start.1 = (bf16[512,256]{1,0:T(8,128)(2,1)S(1)}, bf16[512,256]{1,0:T(8,128)(2,1)S(1)}, u32[]{:S(2)}, u32[]{:S(2)}) collective-permute-start(bf16[512,256]{1,0:T(8,128)(2,1)S(1)} %get-tuple-element.15), channel_id=1, source_target_pairs={{0,1},{1,2},{2,3},{3,4},{4,5},{5,6},{6,7},{7,8},{8,9},{9,10},{10,1... | collective-permute-start | bytes 786440 | tf_op jit(solution)/shard_map/ppermute | solution.py:183
  38.9 8.1 %collective-permute-done.8 = bf16[512,256]{1,0:T(8,128)(2,1)S(1)} collective-permute-done((bf16[512,256]{1,0:T(8,128)(2,1)S(1)}, bf16[512,256]{1,0:T(8,128)(2,1)S(1)}, u32[]{:S(2)}, u32[]{:S(2)}) %collective-permute-start.8) | collective-permute-done | bytes 262176 | tf_op jit(solution)/shard_map/ppermute | solution.py:183
  47.0 1.9 %collective-permute-start.9 = (bf16[512,256]{1,0:T(8,128)(2,1)S(1)}, bf16[512,256]{1,0:T(8,128)(2,1)S(1)}, u32[]{:S(2)}, u32[]{:S(2)}) collective-permute-start(bf16[512,256]{1,0:T(8,128)(2,1)S(1)} %collective-permute-done.8), channel_id=1, source_target_pairs={{0,1},{1,2},{2,3},{3,4},{4,5},{5,6},{6,7},{7,8},{8,9},{9,10},{10,1... | collective-permute-start | bytes 786440 | tf_op jit(solution)/shard_map/ppermute | solution.py:183
  48.9 0.8 collective-permute-done.1
  49.8 1.9 %collective-permute-start.2 = (bf16[512,256]{1,0:T(8,128)(2,1)S(1)}, bf16[512,256]{1,0:T(8,128)(2,1)S(1)}, u32[]{:S(2)}, u32[]{:S(2)}) collective-permute-start(bf16[512,256]{1,0:T(8,128)(2,1)S(1)} %collective-permute-done.1), channel_id=1, source_target_pairs={{0,1},{1,2},{2,3},{3,4},{4,5},{5,6},{6,7},{7,8},{8,9},{9,10},{10,1... | collective-permute-start | bytes 786440 | tf_op jit(solution)/shard_map/ppermute | solution.py:183
  51.7 4.7 %collective-permute-done.9 = bf16[512,256]{1,0:T(8,128)(2,1)S(1)} collective-permute-done((bf16[512,256]{1,0:T(8,128)(2,1)S(1)}, bf16[512,256]{1,0:T(8,128)(2,1)S(1)}, u32[]{:S(2)}, u32[]{:S(2)}) %collective-permute-start.9) | collective-permute-done | bytes 262176 | tf_op jit(solution)/shard_map/ppermute | solution.py:183
  56.4 1.9 %collective-permute-start.10 = (bf16[512,256]{1,0:T(8,128)(2,1)S(1)}, bf16[512,256]{1,0:T(8,128)(2,1)S(1)}, u32[]{:S(2)}, u32[]{:S(2)}) collective-permute-start(bf16[512,256]{1,0:T(8,128)(2,1)S(1)} %collective-permute-done.9), channel_id=1, source_target_pairs={{0,1},{1,2},{2,3},{3,4},{4,5},{5,6},{6,7},{7,8},{8,9},{9,10},{10,1... | collective-permute-start | bytes 786440 | tf_op jit(solution)/shard_map/ppermute | solution.py:183
  58.6 0.2 convolution_add_fusion.13
  58.8 0.4 collective-permute-done.2
  59.2 1.9 %collective-permute-start.3 = (bf16[512,256]{1,0:T(8,128)(2,1)S(1)}, bf16[512,256]{1,0:T(8,128)(2,1)S(1)}, u32[]{:S(2)}, u32[]{:S(2)}) collective-permute-start(bf16[512,256]{1,0:T(8,128)(2,1)S(1)} %collective-permute-done.2), channel_id=1, source_target_pairs={{0,1},{1,2},{2,3},{3,4},{4,5},{5,6},{6,7},{7,8},{8,9},{9,10},{10,1... | collective-permute-start | bytes 786440 | tf_op jit(solution)/shard_map/ppermute | solution.py:183
  61.1 4.7 %collective-permute-done.10 = bf16[512,256]{1,0:T(8,128)(2,1)S(1)} collective-permute-done((bf16[512,256]{1,0:T(8,128)(2,1)S(1)}, bf16[512,256]{1,0:T(8,128)(2,1)S(1)}, u32[]{:S(2)}, u32[]{:S(2)}) %collective-permute-start.10) | collective-permute-done | bytes 262176 | tf_op jit(solution)/shard_map/ppermute | solution.py:183
  65.9 1.9 %collective-permute-start.11 = (bf16[512,256]{1,0:T(8,128)(2,1)S(1)}, bf16[512,256]{1,0:T(8,128)(2,1)S(1)}, u32[]{:S(2)}, u32[]{:S(2)}) collective-permute-start(bf16[512,256]{1,0:T(8,128)(2,1)S(1)} %collective-permute-done.10), channel_id=1, source_target_pairs={{0,1},{1,2},{2,3},{3,4},{4,5},{5,6},{6,7},{7,8},{8,9},{9,10},{10,1... | collective-permute-start | bytes 786440 | tf_op jit(solution)/shard_map/ppermute | solution.py:183
  67.8 0.2 fusion.17
  68.0 0.2 convolution_add_fusion.12
  68.3 0.4 collective-permute-done.3
  68.7 1.9 %collective-permute-start.4 = (bf16[512,256]{1,0:T(8,128)(2,1)S(1)}, bf16[512,256]{1,0:T(8,128)(2,1)S(1)}, u32[]{:S(2)}, u32[]{:S(2)}) collective-permute-start(bf16[512,256]{1,0:T(8,128)(2,1)S(1)} %collective-permute-done.3), channel_id=1, source_target_pairs={{0,1},{1,2},{2,3},{3,4},{4,5},{5,6},{6,7},{7,8},{8,9},{9,10},{10,1... | collective-permute-start | bytes 786440 | tf_op jit(solution)/shard_map/ppermute | solution.py:183
  70.6 4.7 %collective-permute-done.11 = bf16[512,256]{1,0:T(8,128)(2,1)S(1)} collective-permute-done((bf16[512,256]{1,0:T(8,128)(2,1)S(1)}, bf16[512,256]{1,0:T(8,128)(2,1)S(1)}, u32[]{:S(2)}, u32[]{:S(2)}) %collective-permute-start.11) | collective-permute-done | bytes 262176 | tf_op jit(solution)/shard_map/ppermute | solution.py:183
  75.4 1.9 %collective-permute-start.12 = (bf16[512,256]{1,0:T(8,128)(2,1)S(1)}, bf16[512,256]{1,0:T(8,128)(2,1)S(1)}, u32[]{:S(2)}, u32[]{:S(2)}) collective-permute-start(bf16[512,256]{1,0:T(8,128)(2,1)S(1)} %collective-permute-done.11), channel_id=1, source_target_pairs={{0,1},{1,2},{2,3},{3,4},{4,5},{5,6},{6,7},{7,8},{8,9},{9,10},{10,1... | collective-permute-start | bytes 786440 | tf_op jit(solution)/shard_map/ppermute | solution.py:183
  77.3 0.2 convolution_add_fusion.6
  77.5 0.2 convolution_add_fusion.11
  77.7 0.4 collective-permute-done.4
  78.2 1.9 %collective-permute-start.5 = (bf16[512,256]{1,0:T(8,128)(2,1)S(1)}, bf16[512,256]{1,0:T(8,128)(2,1)S(1)}, u32[]{:S(2)}, u32[]{:S(2)}) collective-permute-start(bf16[512,256]{1,0:T(8,128)(2,1)S(1)} %collective-permute-done.4), channel_id=1, source_target_pairs={{0,1},{1,2},{2,3},{3,4},{4,5},{5,6},{6,7},{7,8},{8,9},{9,10},{10,1... | collective-permute-start | bytes 786440 | tf_op jit(solution)/shard_map/ppermute | solution.py:183
  80.1 4.7 %collective-permute-done.12 = bf16[512,256]{1,0:T(8,128)(2,1)S(1)} collective-permute-done((bf16[512,256]{1,0:T(8,128)(2,1)S(1)}, bf16[512,256]{1,0:T(8,128)(2,1)S(1)}, u32[]{:S(2)}, u32[]{:S(2)}) %collective-permute-start.12) | collective-permute-done | bytes 262176 | tf_op jit(solution)/shard_map/ppermute | solution.py:183
  84.8 1.9 %collective-permute-start.13 = (bf16[512,256]{1,0:T(8,128)(2,1)S(1)}, bf16[512,256]{1,0:T(8,128)(2,1)S(1)}, u32[]{:S(2)}, u32[]{:S(2)}) collective-permute-start(bf16[512,256]{1,0:T(8,128)(2,1)S(1)} %collective-permute-done.12), channel_id=1, source_target_pairs={{0,1},{1,2},{2,3},{3,4},{4,5},{5,6},{6,7},{7,8},{8,9},{9,10},{10,1... | collective-permute-start | bytes 786440 | tf_op jit(solution)/shard_map/ppermute | solution.py:183
  86.7 0.2 convolution_add_fusion.5
  87.0 0.2 convolution_add_fusion.4
  87.2 0.4 collective-permute-done.5
  87.6 1.9 %collective-permute-start.6 = (bf16[512,256]{1,0:T(8,128)(2,1)S(1)}, bf16[512,256]{1,0:T(8,128)(2,1)S(1)}, u32[]{:S(2)}, u32[]{:S(2)}) collective-permute-start(bf16[512,256]{1,0:T(8,128)(2,1)S(1)} %collective-permute-done.5), channel_id=1, source_target_pairs={{0,1},{1,2},{2,3},{3,4},{4,5},{5,6},{6,7},{7,8},{8,9},{9,10},{10,1... | collective-permute-start | bytes 786440 | tf_op jit(solution)/shard_map/ppermute | solution.py:183
  89.5 4.7 %collective-permute-done.13 = bf16[512,256]{1,0:T(8,128)(2,1)S(1)} collective-permute-done((bf16[512,256]{1,0:T(8,128)(2,1)S(1)}, bf16[512,256]{1,0:T(8,128)(2,1)S(1)}, u32[]{:S(2)}, u32[]{:S(2)}) %collective-permute-start.13) | collective-permute-done | bytes 262176 | tf_op jit(solution)/shard_map/ppermute | solution.py:183
  94.3 1.9 %collective-permute-start.14 = (bf16[512,256]{1,0:T(8,128)(2,1)S(1)}, bf16[512,256]{1,0:T(8,128)(2,1)S(1)}, u32[]{:S(2)}, u32[]{:S(2)}) collective-permute-start(bf16[512,256]{1,0:T(8,128)(2,1)S(1)} %collective-permute-done.13), channel_id=1, source_target_pairs={{0,1},{1,2},{2,3},{3,4},{4,5},{5,6},{6,7},{7,8},{8,9},{9,10},{10,1... | collective-permute-start | bytes 786440 | tf_op jit(solution)/shard_map/ppermute | solution.py:183
  96.2 0.2 convolution_add_fusion.3
  96.4 0.2 convolution_add_fusion.2
  96.7 7.1 %collective-permute-done.14 = bf16[512,256]{1,0:T(8,128)(2,1)S(1)} collective-permute-done((bf16[512,256]{1,0:T(8,128)(2,1)S(1)}, bf16[512,256]{1,0:T(8,128)(2,1)S(1)}, u32[]{:S(2)}, u32[]{:S(2)}) %collective-permute-start.14) | collective-permute-done | bytes 262176 | tf_op jit(solution)/shard_map/ppermute | solution.py:183
  103.8 0.2 convolution_add_fusion.1
  104.0 1.9 %collective-permute-start.15 = (f32[512,256]{1,0:T(8,128)S(1)}, f32[512,256]{1,0:T(8,128)S(1)}, u32[]{:S(2)}, u32[]{:S(2)}) collective-permute-start(f32[512,256]{1,0:T(8,128)S(1)} %convolution_add_fusion.1), channel_id=1, source_target_pairs={{0,16},{16,0},{1,17},{17,1},{2,18},{18,2},{3,19},{19,3},{4,20},{20... | collective-permute-start | bytes 1572872 | tf_op jit(solution)/shard_map/ppermute | solution.py:197
  105.9 0.2 convolution_add_fusion.10
  106.2 1.9 %collective-permute-start.7 = (bf16[512,256]{1,0:T(8,128)(2,1)S(1)}, bf16[512,256]{1,0:T(8,128)(2,1)S(1)}, u32[]{:S(2)}, u32[]{:S(2)}) collective-permute-start(bf16[512,256]{1,0:T(8,128)(2,1)S(1)} %collective-permute-done.6), channel_id=1, source_target_pairs={{0,1},{1,2},{2,3},{3,4},{4,5},{5,6},{6,7},{7,8},{8,9},{9,10},{10,1... | collective-permute-start | bytes 786440 | tf_op jit(solution)/shard_map/ppermute | solution.py:183
  108.1 0.2 convolution_add_fusion.9
  108.3 0.2 convolution_add_fusion.8
  108.6 7.1 %collective-permute-done.7 = bf16[512,256]{1,0:T(8,128)(2,1)S(1)} collective-permute-done((bf16[512,256]{1,0:T(8,128)(2,1)S(1)}, bf16[512,256]{1,0:T(8,128)(2,1)S(1)}, u32[]{:S(2)}, u32[]{:S(2)}) %collective-permute-start.7) | collective-permute-done | bytes 262176 | tf_op jit(solution)/shard_map/ppermute | solution.py:183
  115.6 1.9 %collective-permute-start.16 = (bf16[512,256]{1,0:T(8,128)(2,1)S(1)}, bf16[512,256]{1,0:T(8,128)(2,1)S(1)}, u32[]{:S(2)}, u32[]{:S(2)}) collective-permute-start(bf16[512,256]{1,0:T(8,128)(2,1)S(1)} %collective-permute-done.7), channel_id=1, source_target_pairs={{0,1},{1,2},{2,3},{3,4},{4,5},{5,6},{6,7},{7,8},{8,9},{9,10},{10,1... | collective-permute-start | bytes 786440 | tf_op jit(solution)/shard_map/ppermute | solution.py:183
  117.6 0.2 fusion
  117.8 7.3 %collective-permute-done.16 = bf16[512,256]{1,0:T(8,128)(2,1)S(1)} collective-permute-done((bf16[512,256]{1,0:T(8,128)(2,1)S(1)}, bf16[512,256]{1,0:T(8,128)(2,1)S(1)}, u32[]{:S(2)}, u32[]{:S(2)}) %collective-permute-start.16) | collective-permute-done | bytes 262176 | tf_op jit(solution)/shard_map/ppermute | solution.py:183
  125.1 0.9 fusion.1
  (18 shorter events, 0.4 us)
Async XLA Ops:
  0.0 58.3 %copy-start = (bf16[4096,256]{1,0:T(8,128)(2,1)S(1)}, bf16[4096,256]{1,0:T(8,128)(2,1)}, u32[]{:S(2)}) copy-start(bf16[4096,256]{1,0:T(8,128)(2,1)} %param.13) | copy-start | bytes 6291460
  0.0 19.7 %copy-start.1 = (bf16[512,256]{1,0:T(8,128)(2,1)S(1)}, bf16[512,256]{1,0:T(8,128)(2,1)}, u32[]{:S(2)}) copy-start(bf16[512,256]{1,0:T(8,128)(2,1)} %q_own_ref.1) | copy-start | bytes 786436
  0.0 7.3 %copy-start.6 = (f32[16,256]{1,0:T(8,128)S(1)}, f32[16,256]{1,0:T(8,128)}, u32[]{:S(2)}) copy-start(f32[16,256]{1,0:T(8,128)} %rates_ref.5) | copy-start | bytes 49156
  2.3 3.9 %collective-permute-start = (bf16[2,512,256]{2,1,0:T(8,128)(2,1)S(1)}, bf16[2,512,256]{2,1,0:T(8,128)(2,1)}, u32[]{:S(2)}, u32[]{:S(2)}) collective-permute-start(bf16[2,512,256]{2,1,0:T(8,128)(2,1)S(1)} %pad_maximum_fusion), channel_id=1, source_target_pairs={{0,16},{16,0},{1,17},{17,1},{2,18},{18,2},{3,19},{19,3},{4,20},{20... | collective-permute-start | bytes 1572872 | tf_op jit(solution)/shard_map/ppermute | solution.py:146
  9.8 17.2 %all-to-all-start = ((f32[16,16,256]{2,1,0:T(8,128)}), f32[16,16,256]{2,1,0:T(8,128)S(1)}, u32[]{:S(2)}, u32[]{:S(2)}) async-start(f32[16,16,256]{2,1,0:T(8,128)} %broadcast_in_dim.4), calls=%async_computation | async-start | bytes 524288 | tf_op jit(solution)/shard_map/all_to_all | solution.py:158
  19.7 0.7 copy-start.7
  20.4 0.7 copy-start.9
  24.9 1.0 copy-start.2
  25.9 1.0 copy-start.4
  27.0 1.2 copy-start.3
  28.2 1.2 copy-start.5
  29.5 0.7 copy-start.8
  30.2 0.7 copy-start.10
  33.1 13.9 %collective-permute-start.8 = (bf16[512,256]{1,0:T(8,128)(2,1)S(1)}, bf16[512,256]{1,0:T(8,128)(2,1)S(1)}, u32[]{:S(2)}, u32[]{:S(2)}) collective-permute-start(bf16[512,256]{1,0:T(8,128)(2,1)S(1)} %get-tuple-element.16), channel_id=1, source_target_pairs={{0,1},{1,2},{2,3},{3,4},{4,5},{5,6},{6,7},{7,8},{8,9},{9,10},{10,1... | collective-permute-start | bytes 786440 | tf_op jit(solution)/shard_map/ppermute | solution.py:183
  35.0 14.7 %collective-permute-start.1 = (bf16[512,256]{1,0:T(8,128)(2,1)S(1)}, bf16[512,256]{1,0:T(8,128)(2,1)S(1)}, u32[]{:S(2)}, u32[]{:S(2)}) collective-permute-start(bf16[512,256]{1,0:T(8,128)(2,1)S(1)} %get-tuple-element.15), channel_id=1, source_target_pairs={{0,1},{1,2},{2,3},{3,4},{4,5},{5,6},{6,7},{7,8},{8,9},{9,10},{10,1... | collective-permute-start | bytes 786440 | tf_op jit(solution)/shard_map/ppermute | solution.py:183
  47.0 9.5 %collective-permute-start.9 = (bf16[512,256]{1,0:T(8,128)(2,1)S(1)}, bf16[512,256]{1,0:T(8,128)(2,1)S(1)}, u32[]{:S(2)}, u32[]{:S(2)}) collective-permute-start(bf16[512,256]{1,0:T(8,128)(2,1)S(1)} %collective-permute-done.8), channel_id=1, source_target_pairs={{0,1},{1,2},{2,3},{3,4},{4,5},{5,6},{6,7},{7,8},{8,9},{9,10},{10,1... | collective-permute-start | bytes 786440 | tf_op jit(solution)/shard_map/ppermute | solution.py:183
  49.8 9.5 %collective-permute-start.2 = (bf16[512,256]{1,0:T(8,128)(2,1)S(1)}, bf16[512,256]{1,0:T(8,128)(2,1)S(1)}, u32[]{:S(2)}, u32[]{:S(2)}) collective-permute-start(bf16[512,256]{1,0:T(8,128)(2,1)S(1)} %collective-permute-done.1), channel_id=1, source_target_pairs={{0,1},{1,2},{2,3},{3,4},{4,5},{5,6},{6,7},{7,8},{8,9},{9,10},{10,1... | collective-permute-start | bytes 786440 | tf_op jit(solution)/shard_map/ppermute | solution.py:183
  56.4 9.5 %collective-permute-start.10 = (bf16[512,256]{1,0:T(8,128)(2,1)S(1)}, bf16[512,256]{1,0:T(8,128)(2,1)S(1)}, u32[]{:S(2)}, u32[]{:S(2)}) collective-permute-start(bf16[512,256]{1,0:T(8,128)(2,1)S(1)} %collective-permute-done.9), channel_id=1, source_target_pairs={{0,1},{1,2},{2,3},{3,4},{4,5},{5,6},{6,7},{7,8},{8,9},{9,10},{10,1... | collective-permute-start | bytes 786440 | tf_op jit(solution)/shard_map/ppermute | solution.py:183
  59.2 9.5 %collective-permute-start.3 = (bf16[512,256]{1,0:T(8,128)(2,1)S(1)}, bf16[512,256]{1,0:T(8,128)(2,1)S(1)}, u32[]{:S(2)}, u32[]{:S(2)}) collective-permute-start(bf16[512,256]{1,0:T(8,128)(2,1)S(1)} %collective-permute-done.2), channel_id=1, source_target_pairs={{0,1},{1,2},{2,3},{3,4},{4,5},{5,6},{6,7},{7,8},{8,9},{9,10},{10,1... | collective-permute-start | bytes 786440 | tf_op jit(solution)/shard_map/ppermute | solution.py:183
  65.9 9.5 %collective-permute-start.11 = (bf16[512,256]{1,0:T(8,128)(2,1)S(1)}, bf16[512,256]{1,0:T(8,128)(2,1)S(1)}, u32[]{:S(2)}, u32[]{:S(2)}) collective-permute-start(bf16[512,256]{1,0:T(8,128)(2,1)S(1)} %collective-permute-done.10), channel_id=1, source_target_pairs={{0,1},{1,2},{2,3},{3,4},{4,5},{5,6},{6,7},{7,8},{8,9},{9,10},{10,1... | collective-permute-start | bytes 786440 | tf_op jit(solution)/shard_map/ppermute | solution.py:183
  68.7 9.5 %collective-permute-start.4 = (bf16[512,256]{1,0:T(8,128)(2,1)S(1)}, bf16[512,256]{1,0:T(8,128)(2,1)S(1)}, u32[]{:S(2)}, u32[]{:S(2)}) collective-permute-start(bf16[512,256]{1,0:T(8,128)(2,1)S(1)} %collective-permute-done.3), channel_id=1, source_target_pairs={{0,1},{1,2},{2,3},{3,4},{4,5},{5,6},{6,7},{7,8},{8,9},{9,10},{10,1... | collective-permute-start | bytes 786440 | tf_op jit(solution)/shard_map/ppermute | solution.py:183
  75.4 9.5 %collective-permute-start.12 = (bf16[512,256]{1,0:T(8,128)(2,1)S(1)}, bf16[512,256]{1,0:T(8,128)(2,1)S(1)}, u32[]{:S(2)}, u32[]{:S(2)}) collective-permute-start(bf16[512,256]{1,0:T(8,128)(2,1)S(1)} %collective-permute-done.11), channel_id=1, source_target_pairs={{0,1},{1,2},{2,3},{3,4},{4,5},{5,6},{6,7},{7,8},{8,9},{9,10},{10,1... | collective-permute-start | bytes 786440 | tf_op jit(solution)/shard_map/ppermute | solution.py:183
  78.2 9.5 %collective-permute-start.5 = (bf16[512,256]{1,0:T(8,128)(2,1)S(1)}, bf16[512,256]{1,0:T(8,128)(2,1)S(1)}, u32[]{:S(2)}, u32[]{:S(2)}) collective-permute-start(bf16[512,256]{1,0:T(8,128)(2,1)S(1)} %collective-permute-done.4), channel_id=1, source_target_pairs={{0,1},{1,2},{2,3},{3,4},{4,5},{5,6},{6,7},{7,8},{8,9},{9,10},{10,1... | collective-permute-start | bytes 786440 | tf_op jit(solution)/shard_map/ppermute | solution.py:183
  84.8 9.5 %collective-permute-start.13 = (bf16[512,256]{1,0:T(8,128)(2,1)S(1)}, bf16[512,256]{1,0:T(8,128)(2,1)S(1)}, u32[]{:S(2)}, u32[]{:S(2)}) collective-permute-start(bf16[512,256]{1,0:T(8,128)(2,1)S(1)} %collective-permute-done.12), channel_id=1, source_target_pairs={{0,1},{1,2},{2,3},{3,4},{4,5},{5,6},{6,7},{7,8},{8,9},{9,10},{10,1... | collective-permute-start | bytes 786440 | tf_op jit(solution)/shard_map/ppermute | solution.py:183
  87.6 18.5 %collective-permute-start.6 = (bf16[512,256]{1,0:T(8,128)(2,1)S(1)}, bf16[512,256]{1,0:T(8,128)(2,1)S(1)}, u32[]{:S(2)}, u32[]{:S(2)}) collective-permute-start(bf16[512,256]{1,0:T(8,128)(2,1)S(1)} %collective-permute-done.5), channel_id=1, source_target_pairs={{0,1},{1,2},{2,3},{3,4},{4,5},{5,6},{6,7},{7,8},{8,9},{9,10},{10,1... | collective-permute-start | bytes 786440 | tf_op jit(solution)/shard_map/ppermute | solution.py:183
  94.3 9.5 %collective-permute-start.14 = (bf16[512,256]{1,0:T(8,128)(2,1)S(1)}, bf16[512,256]{1,0:T(8,128)(2,1)S(1)}, u32[]{:S(2)}, u32[]{:S(2)}) collective-permute-start(bf16[512,256]{1,0:T(8,128)(2,1)S(1)} %collective-permute-done.13), channel_id=1, source_target_pairs={{0,1},{1,2},{2,3},{3,4},{4,5},{5,6},{6,7},{7,8},{8,9},{9,10},{10,1... | collective-permute-start | bytes 786440 | tf_op jit(solution)/shard_map/ppermute | solution.py:183
  104.0 13.6 %collective-permute-start.15 = (f32[512,256]{1,0:T(8,128)S(1)}, f32[512,256]{1,0:T(8,128)S(1)}, u32[]{:S(2)}, u32[]{:S(2)}) collective-permute-start(f32[512,256]{1,0:T(8,128)S(1)} %convolution_add_fusion.1), channel_id=1, source_target_pairs={{0,16},{16,0},{1,17},{17,1},{2,18},{18,2},{3,19},{19,3},{4,20},{20... | collective-permute-start | bytes 1572872 | tf_op jit(solution)/shard_map/ppermute | solution.py:197
  106.2 9.5 %collective-permute-start.7 = (bf16[512,256]{1,0:T(8,128)(2,1)S(1)}, bf16[512,256]{1,0:T(8,128)(2,1)S(1)}, u32[]{:S(2)}, u32[]{:S(2)}) collective-permute-start(bf16[512,256]{1,0:T(8,128)(2,1)S(1)} %collective-permute-done.6), channel_id=1, source_target_pairs={{0,1},{1,2},{2,3},{3,4},{4,5},{5,6},{6,7},{7,8},{8,9},{9,10},{10,1... | collective-permute-start | bytes 786440 | tf_op jit(solution)/shard_map/ppermute | solution.py:183
  115.6 9.5 %collective-permute-start.16 = (bf16[512,256]{1,0:T(8,128)(2,1)S(1)}, bf16[512,256]{1,0:T(8,128)(2,1)S(1)}, u32[]{:S(2)}, u32[]{:S(2)}) collective-permute-start(bf16[512,256]{1,0:T(8,128)(2,1)S(1)} %collective-permute-done.7), channel_id=1, source_target_pairs={{0,1},{1,2},{2,3},{3,4},{4,5},{5,6},{6,7},{7,8},{8,9},{9,10},{10,1... | collective-permute-start | bytes 786440 | tf_op jit(solution)/shard_map/ppermute | solution.py:183
where the time goes:
time: 127 us; the launch traced here: 126 us
  waiting for transfers between devices  57.8 us (46%)
  starting transfers between devices  43.7 us (34%)
  local copies, waits for them, and re-layouts  8.96 us (7%)
  Pallas kernels  7.86 us (6%)
  matrix products  4.39 us (3%)
  other arithmetic  2.91 us (2%)
    ppermute x15, waiting for transfers between devices, body(): hop = lambda array: lax.ppermute(array, ('core', 'ch'), ring)  55.7 us
    ppermute x15, starting transfers between devices, body(): hop = lambda array: lax.ppermute(array, ('core', 'ch'), ring)  30.6 us
    all_to_all x1, starting transfers between devices, body(): lax.all_to_all(jnp.broadcast_to(total[None], (chips, modes, width)), ('y'...  9.22 us
    unnamed x22, local copies, waits for them, and re-layouts  7.17 us
    dot_general x16, matrix products, project(): return jnp.dot(array, weight, preferred_element_type=F32)  4.39 us
    pallas_call x1, Pallas kernels, body(): pl.pallas_call(local_kernel, out_shape=(shape((steps, BLOCKS, width)), sh...  3.86 us
  transfers between devices with their start and end apart: 18, of which 16 were waited for; matrix products, arithmetic and copies ran while one was open for 3% of the time, Pallas kernels for 3%

commit v1 on v0

v1 whole, which is shorter than its diff:
```python
import jax
import jax.numpy as jnp
from jax import lax
from jax.experimental import pallas as pl
from jax.experimental.pallas import tpu as pltpu
from jax.sharding import Mesh
from jax.sharding import PartitionSpec as P

BLOCKS = 8
LANES = 128
F32 = jnp.float32
BF16 = jnp.bfloat16


def spread(ref, mode, lanes):
    return jnp.broadcast_to(ref[mode : mode + 1, lanes], (BLOCKS, LANES))


def tree_sum(terms):
    terms = list(terms)
    while len(terms) > 1:
        terms = [a + b for a, b in zip(terms[::2], terms[1::2])]
    return terms[0]


def fetch(pairs, sems):
    copies = [pltpu.make_async_copy(source, target, sems.at[i]) for i, (source, target) in enumerate(pairs)]
    for copy in copies:
        copy.start()
    return copies


def fill(flat, rows, value):
    piece = 64

    @pl.loop(0, rows // piece)
    def _(i):
        at = pl.ds(pl.multiple_of(i * piece, piece), piece)
        now = value(at)
        for half in range(flat.shape[0]):
            flat[half, at, :] = now[:, half * LANES : (half + 1) * LANES]


def mixed_in(k_ref, v_ref):
    return lambda at: (k_ref[at, :].astype(F32) * v_ref[at, :].astype(F32)).astype(BF16).astype(F32)


def block_ends(flat, rates_ref, half):
    modes, steps = rates_ref.shape[0], flat.shape[1] // BLOCKS
    lanes = slice(half * LANES, (half + 1) * LANES)
    poles = [jnp.exp(-spread(rates_ref, m, lanes)) for m in range(modes)]

    def step(j, held):
        now = flat[half, pl.ds(j, BLOCKS, stride=steps), :]
        return tuple(p * h + now for p, h in zip(poles, held))

    return poles, lax.fori_loop(0, steps, step, (jnp.zeros((BLOCKS, LANES), F32),) * modes, unroll=8)


def states_kernel(k_hbm, v_hbm, rates_hbm, total_ref, flat, k_ref, v_ref, rates_ref, sems):
    modes, width = rates_ref.shape
    rows = k_ref.shape[0]
    steps = rows // BLOCKS
    for copy in fetch(((rates_hbm, rates_ref), (k_hbm, k_ref), (v_hbm, v_ref)), sems):
        copy.wait()
    fill(flat, rows, mixed_in(k_ref, v_ref))
    block = lax.broadcasted_iota(jnp.int32, (BLOCKS, LANES), 0).astype(F32)
    for half in range(width // LANES):
        lanes = slice(half * LANES, (half + 1) * LANES)
        _, held = block_ends(flat, rates_ref, half)
        for m in range(modes):
            fade = jnp.exp(-spread(rates_ref, m, lanes) * (steps * (BLOCKS - 1 - block)))
            total_ref[m : m + 1, lanes] = jnp.sum(fade * held[m], axis=0, keepdims=True)


def local_kernel(core_ref, k_hbm, v_hbm, q_hbm, rates_hbm, resid_hbm, skip_hbm, oth_hbm, out_hbm, flat, flat_q, k_ref, v_ref, q_ref, rates_ref, resid_ref, oth_ref, skip_ref, out_ref, sems):
    modes, width = rates_ref.shape
    rows = q_ref.shape[0]
    steps = rows // BLOCKS
    pairs = ((rates_hbm, rates_ref), (resid_hbm, resid_ref), (skip_hbm, skip_ref), (oth_hbm, oth_ref))
    for copy in fetch(pairs + ((k_hbm, k_ref), (v_hbm, v_ref), (q_hbm, q_ref)), sems):
        copy.wait()
    fill(flat, rows, mixed_in(k_ref, v_ref))
    fill(flat_q, rows, lambda at: q_ref[at, :].astype(F32))
    block = lax.broadcasted_iota(jnp.int32, (BLOCKS, LANES), 0)
    second = (core_ref[0] > 0).astype(F32)
    for half in range(width // LANES):
        lanes = slice(half * LANES, (half + 1) * LANES)
        poles, held = block_ends(flat, rates_ref, half)
        weights, first = [], []
        for m in range(modes):
            rate = spread(rates_ref, m, lanes)
            weights.append(spread(resid_ref, m, lanes))
            come = second * spread(oth_ref, m, lanes)
            scan = jnp.where(block >= 1, pltpu.roll(held[m], 1, 0), come)
            for shift in (1, 2, 4):
                moved = jnp.where(block >= shift, pltpu.roll(scan, shift, 0), 0.0)
                scan = scan + jnp.exp(-rate * float(steps * shift)) * moved
            first.append(scan)
        direct = spread(skip_ref, 0, lanes)

        def step(j, held):
            now = flat[half, pl.ds(j, BLOCKS, stride=steps), :]
            held = tuple(p * h + now for p, h in zip(poles, held))
            out_ref[j, 0:BLOCKS, lanes] = tree_sum(w * h for w, h in zip(weights, held)) + direct * now
            out_ref[j, BLOCKS : 2 * BLOCKS, lanes] = flat_q[half, pl.ds(j, BLOCKS, stride=steps), :]
            return held

        lax.fori_loop(0, steps, step, tuple(first), unroll=4)
    copy = pltpu.make_async_copy(out_ref, out_hbm, sems.at[7])
    copy.start()
    copy.wait()


def gate_kernel(core_ref, chip_ref, all_hbm, rates_hbm, resid_hbm, local_hbm, out_hbm, flat, all_ref, rates_ref, resid_ref, local_ref, out_ref, sems):
    chips, modes, width = all_ref.shape
    steps = local_ref.shape[0]
    rows = out_ref.shape[0]
    small = fetch(((rates_hbm, rates_ref), (resid_hbm, resid_ref), (all_hbm, all_ref), (local_hbm, local_ref)), sems)
    large = small.pop()
    for copy in small:
        copy.wait()
    chip, core = chip_ref[0], core_ref[0]
    block = lax.broadcasted_iota(jnp.int32, (BLOCKS, LANES), 0).astype(F32)
    rates = rates_ref[...]
    fade = jnp.exp(-rates * float(2 * rows))
    before = jnp.zeros((modes, width), F32)
    for c in range(chips - 1):
        before = jnp.where(c < chip, fade * before + all_ref[c], before)
    before = jnp.where(core == 0, before, jnp.exp(-rates * float(rows)) * before)
    before = before * resid_ref[...]
    sent = []
    for half in range(width // LANES):
        lanes = slice(half * LANES, (half + 1) * LANES)
        poles, first = [], []
        for m in range(modes):
            rate = spread(rates_ref, m, lanes)
            poles.append(jnp.exp(-rate))
            come = jnp.broadcast_to(before[m : m + 1, lanes], (BLOCKS, LANES))
            first.append(come * jnp.exp(-rate * (steps * block + 1.0)))
        if half == 0:
            large.wait()

        def step(j, held):
            conv = local_ref[j, 0:BLOCKS, lanes] + tree_sum(held)
            flat[half, pl.ds(j, BLOCKS, stride=steps), :] = local_ref[j, BLOCKS : 2 * BLOCKS, lanes] * conv
            return tuple(p * h for p, h in zip(poles, held))

        lax.fori_loop(0, steps, step, tuple(first), unroll=4)
        piece = 64

        @pl.loop(0, rows // piece)
        def _(i):
            at = pl.ds(pl.multiple_of(i * piece, piece), piece)
            out_ref[at, lanes] = flat[half, at, :].astype(BF16)

        sent.append(pltpu.make_async_copy(out_ref.at[:, lanes], out_hbm.at[:, lanes], sems.at[4 + half]))
        sent[-1].start()
    for copy in sent:
        copy.wait()


VMEM = pl.BlockSpec(memory_space=pltpu.VMEM)
ANY = pl.BlockSpec(memory_space=pl.ANY)
SMEM = pl.BlockSpec(memory_space=pltpu.SMEM)


def kernel_call(kernel, name, cost, **kwargs):
    return pl.pallas_call(
        kernel,
        name=name,
        cost_estimate=pl.CostEstimate(flops=cost, bytes_accessed=1 << 20, transcendentals=0),
        **kwargs,
    )


def body(q_branch, k_branch, v_branch, decay_rates, residues, skip_gain, out_weight):
    rows, width = k_branch.shape
    modes = decay_rates.shape[0]
    steps = rows // BLOCKS
    chips = lax.axis_size("y") * lax.axis_size("x")
    depth = lax.axis_size("ch")
    core, z = lax.axis_index("core"), lax.axis_index("ch")
    chip = lax.axis_index("y") * lax.axis_size("x") + lax.axis_index("x")
    core_at = core.reshape(1).astype(jnp.int32)
    chip_at = chip.reshape(1).astype(jnp.int32)
    shape = lambda s, d=F32: jax.ShapeDtypeStruct(s, d)
    flat_shape = (width // LANES, rows, LANES)
    work = modes * rows * width
    swap = lambda array: lax.ppermute(array, "core", [(0, 1), (1, 0)])

    flat_of = pltpu.VMEM(flat_shape, F32)
    half_of = pltpu.VMEM((rows, width), BF16)
    modal = pltpu.VMEM((modes, width), F32)
    sems = lambda count: pltpu.SemaphoreType.DMA((count,))

    by_step = (steps, 2 * BLOCKS, width)
    total = kernel_call(
        states_kernel,
        "states",
        2 * work,
        out_shape=shape((modes, width)),
        in_specs=[ANY] * 3,
        out_specs=VMEM,
        scratch_shapes=[flat_of, half_of, half_of, modal, sems(3)],
    )(k_branch, v_branch, decay_rates)
    total_oth = swap(total)
    first = core == 0
    every = jnp.exp(-decay_rates * float(rows)) * jnp.where(first, total, total_oth) + jnp.where(first, total_oth, total)
    every = jnp.broadcast_to(every[None], (chips, modes, width))
    every = lax.all_to_all(every, ("y", "x"), split_axis=0, concat_axis=0, tiled=True)
    local = kernel_call(
        local_kernel,
        "chip_convolution",
        6 * work,
        out_shape=shape(by_step),
        in_specs=[SMEM] + [ANY] * 6 + [ANY],
        out_specs=ANY,
        scratch_shapes=[flat_of, flat_of, half_of, half_of, half_of, modal, modal, modal]
        + [pltpu.VMEM((1, width), F32), pltpu.VMEM(by_step, F32), sems(8)],
    )(core_at, k_branch, v_branch, q_branch, decay_rates, residues, skip_gain[None, :], total_oth)
    own = kernel_call(
        gate_kernel,
        "carry_and_gate",
        2 * work,
        out_shape=shape((rows, width), BF16),
        in_specs=[SMEM, SMEM] + [ANY] * 4,
        out_specs=ANY,
        scratch_shapes=[flat_of, pltpu.VMEM((chips, modes, width), F32), modal, modal]
        + [pltpu.VMEM(by_step, F32), half_of, sems(4 + width // LANES)],
    )(core_at, chip_at, every, decay_rates, residues, local)

    ring = [(c * depth + i, c * depth + (i + 1 - 2 * c) % depth) for c in range(2) for i in range(depth)]
    cross = [((1 - c) * depth + i, c * depth + (i + 1 - 2 * c) % depth) for c in range(2) for i in range(depth)]
    hop = lambda array, pairs=ring: lax.ppermute(array, ("core", "ch"), pairs)

    def project(array, distance):
        source = lax.rem(z + (2 * core - 1) * distance + depth, depth)
        weight = lax.dynamic_slice(out_weight, (source * width, 0), (width, out_weight.shape[1]))
        return jnp.dot(array, weight, preferred_element_type=F32)

    sum_own = project(own, 0)
    own, oth = hop(own), hop(own, cross)
    sum_own, sum_oth = sum_own + project(own, 1), project(oth, 1)
    last_oth = oth
    for distance in range(2, depth // 2):
        last_own = own
        own = hop(own)
        oth, last_own = lax.optimization_barrier((oth, last_own))
        last_oth, oth = oth, hop(oth)
        own, last_oth = lax.optimization_barrier((own, last_oth))
        sum_own = sum_own + project(own, distance)
        sum_oth = sum_oth + project(oth, distance)
    last_own, own = own, hop(own, ring[depth:])
    oth, last_own = lax.optimization_barrier((oth, last_own))
    oth = hop(oth, ring[depth:])
    sum_own = sum_own + project(own, depth // 2)
    sum_oth = sum_oth + project(oth, depth // 2)
    sum_oth, sum_own = lax.optimization_barrier((sum_oth, sum_own))
    return (sum_own + swap(sum_oth)).astype(BF16)


def solution(mesh):
    chips = Mesh(mesh.devices.reshape(4, 4, 2, 16), ("y", "x", "core", "ch"))
    seq = ("y", "x", "core")
    placed = (P(seq, "ch"), P(seq, "ch"), P(seq, "ch"), P(None, "ch"), P(None, "ch"), P("ch"), P(None, "ch"))
    return jax.shard_map(body, mesh=chips, in_specs=placed, out_specs=P(seq, "ch"), check_vma=False)
```

time: 127 us -> 114 us (0.90)
  the two profiles are of different devices: /device:TPU:2 before, /device:TPU:1 now
where the time goes in v1:
time: 114 us; the launch traced here: 112 us
  starting transfers between devices  81.9 us (72%)
  waiting for transfers between devices  11.2 us (10%)
  Pallas kernels  10.9 us (10%)
  matrix products  5.02 us (4%)
  other arithmetic  1.5 us (1%)
  local copies, waits for them, and re-layouts  1.44 us (1%)
    ppermute x16, starting transfers between devices, body(): hop = lambda array, pairs=ring: lax.ppermute(array, ('core', 'ch'), pairs)  64.5 us
    ppermute x2, starting transfers between devices, body(): swap = lambda array: lax.ppermute(array, 'core', [(0, 1), (1, 0)])  13.9 us
    ppermute x16, waiting for transfers between devices, body(): hop = lambda array, pairs=ring: lax.ppermute(array, ('core', 'ch'), pairs)  5.41 us
    pallas_call x1, Pallas kernels, body(): kernel_call(local_kernel, 'chip_convolution', 6 * work, out_shape=shape(b...  5.12 us
    dot_general x17, matrix products, project(): return jnp.dot(array, weight, preferred_element_type=F32)  5.02 us
    all_to_all x1, starting transfers between devices, body(): lax.all_to_all(every, ('y', 'x'), split_axis=0, concat_axis=0, tiled=True)  3.53 us
    all_to_all x1, waiting for transfers between devices, body(): lax.all_to_all(every, ('y', 'x'), split_axis=0, concat_axis=0, tiled=True)  3.28 us
    pallas_call x1, Pallas kernels, body(): kernel_call(gate_kernel, 'carry_and_gate', 2 * work, out_shape=shape((row...  2.93 us
  transfers between devices with their start and end apart: 19, of which 6 were waited for; matrix products, arithmetic and copies ran while one was open for 4% of the time, Pallas kernels for 5%

profile of v1, /device:TPU:1, one launch (start us, length us, event | category | flops | bytes accessed | tf_op | source)
XLA Modules:
  0.0 112.4 jit_solution(6335217462223316090)
XLA Ops:
  0.0 2.8 %states.1 = f32[16,256]{1,0:T(8,128)} custom-call(bf16[512,256]{1,0:T(8,128)(2,1)} %k_hbm.3, bf16[512,256]{1,0:T(8,128)(2,1)} %v_hbm.3, f32[16,256]{1,0:T(8,128)} %rates_hbm.5), custom_call_target="tpu_custom_call" | custom-call | flops 4194304 | bytes 1048576 | tf_op jit(solution)/shard_map/states/pallas_call | solution.py:198
  2.8 8.8 %collective-permute-start = (f32[16,256]{1,0:T(8,128)}, f32[16,256]{1,0:T(8,128)S(1)}, u32[]{:S(2)}, u32[]{:S(2)}) collective-permute-start(f32[16,256]{1,0:T(8,128)} %states.1), channel_id=1, source_target_pairs={{0,16},{16,0},{1,17},{17,1},{2,18},{18,2},{3,19},{19,3},{4,20},{20... | collective-permute-start | bytes 49160 | tf_op jit(solution)/shard_map/ppermute | solution.py:190
  11.6 1.0 collective-permute-done.oth_hbm
  12.6 0.8 select_add_fusion
  13.4 0.7 broadcast_in_dim.4
  14.1 3.5 %all-to-all-start = ((f32[16,16,256]{2,1,0:T(8,128)}), f32[16,16,256]{2,1,0:T(8,128)S(1)}, u32[]{:S(2)}, u32[]{:S(2)}) async-start(f32[16,16,256]{2,1,0:T(8,128)} %broadcast_in_dim.4), calls=%async_computation | async-start | bytes 524288 | tf_op jit(solution)/shard_map/all_to_all | solution.py:211
  17.7 0.0 copy-done.2
  17.7 5.1 %chip_convolution.1.local_hbm = f32[64,16,256]{2,1,0:T(8,128)} custom-call(s32[1]{0:T(128)} %bitcast.core_ref, bf16[512,256]{1,0:T(8,128)(2,1)} %k_hbm.3, bf16[512,256]{1,0:T(8,128)(2,1)} %v_hbm.3, bf16[512,256]{1,0:T(8,128)(2,1)} %q_hbm.1, f32[16,256]{1,0:T(8,128)} %rates_hbm.5, f32[16,256]{1,0:T(8,128)} %resid_hbm.3, f32[1,256]{1,0:T(1,128)} %bitcast.20, ...), custom_call_target="tpu_custom_call" | custom-call | flops 12582912 | bytes 1048576 | tf_op jit(solution)/shard_map/chip_convolution/pallas_call | solution.py:212
  22.8 3.3 %all-to-all-done.all_hbm = f32[16,16,256]{2,1,0:T(8,128)S(1)} async-done(((f32[16,16,256]{2,1,0:T(8,128)}), f32[16,16,256]{2,1,0:T(8,128)S(1)}, u32[]{:S(2)}, u32[]{:S(2)}) %all-to-all-start) | async-done | bytes 262176 | tf_op jit(solution)/shard_map/all_to_all | solution.py:211
  26.1 0.7 copy-done.1
  26.8 2.9 %carry_and_gate.1 = bf16[512,256]{1,0:T(8,128)(2,1)} custom-call(s32[1]{0:T(128)} %bitcast.core_ref, s32[1]{0:T(128)} %bitcast.1.chip_ref, f32[16,16,256]{2,1,0:T(8,128)} %copy-done.1, f32[16,256]{1,0:T(8,128)} %rates_hbm.5, f32[16,256]{1,0:T(8,128)} %resid_hbm.3, f32[64,16,256]{2,1,0:T(8,128)} %chip_convolution.1.local_hbm), custom_call_target="tpu_custom_call" | custom-call | flops 4194304 | bytes 1048576 | tf_op jit(solution)/shard_map/carry_and_gate/pallas_call | solution.py:222
  29.7 8.7 %collective-permute-start.2 = (bf16[512,256]{1,0:T(8,128)(2,1)}, bf16[512,256]{1,0:T(8,128)(2,1)S(1)}, u32[]{:S(2)}, u32[]{:S(2)}) collective-permute-start(bf16[512,256]{1,0:T(8,128)(2,1)} %carry_and_gate.1), channel_id=1, source_target_pairs={{0,1},{1,2},{2,3},{3,4},{4,5},{5,6},{6,7},{7,8},{8,9},{9,10},{10,1... | collective-permute-start | bytes 786440 | tf_op jit(solution)/shard_map/ppermute | solution.py:235
  38.4 1.9 %collective-permute-start.1 = (bf16[512,256]{1,0:T(8,128)(2,1)}, bf16[512,256]{1,0:T(8,128)(2,1)S(1)}, u32[]{:S(2)}, u32[]{:S(2)}) collective-permute-start(bf16[512,256]{1,0:T(8,128)(2,1)} %carry_and_gate.1), channel_id=1, source_target_pairs={{16,1},{17,2},{18,3},{19,4},{20,5},{21,6},{22,7},{23,8},{24,9},{25... | collective-permute-start | bytes 786440 | tf_op jit(solution)/shard_map/ppermute | solution.py:235
  40.4 1.7 %collective-permute-done.2 = bf16[512,256]{1,0:T(8,128)(2,1)S(1)} collective-permute-done((bf16[512,256]{1,0:T(8,128)(2,1)}, bf16[512,256]{1,0:T(8,128)(2,1)S(1)}, u32[]{:S(2)}, u32[]{:S(2)}) %collective-permute-start.2) | collective-permute-done | bytes 262176 | tf_op jit(solution)/shard_map/ppermute | solution.py:235
  42.0 4.9 %collective-permute-start.4 = (bf16[512,256]{1,0:T(8,128)(2,1)S(1)}, bf16[512,256]{1,0:T(8,128)(2,1)S(1)}, u32[]{:S(2)}, u32[]{:S(2)}) collective-permute-start(bf16[512,256]{1,0:T(8,128)(2,1)S(1)} %collective-permute-done.2), channel_id=1, source_target_pairs={{0,1},{1,2},{2,3},{3,4},{4,5},{5,6},{6,7},{7,8},{8,9},{9,10},{10,1... | collective-permute-start | bytes 786440 | tf_op jit(solution)/shard_map/ppermute | solution.py:235
  47.0 0.0 collective-permute-done.1
  47.0 3.2 %collective-permute-start.3 = (bf16[512,256]{1,0:T(8,128)(2,1)S(1)}, bf16[512,256]{1,0:T(8,128)(2,1)S(1)}, u32[]{:S(2)}, u32[]{:S(2)}) collective-permute-start(bf16[512,256]{1,0:T(8,128)(2,1)S(1)} %collective-permute-done.1), channel_id=1, source_target_pairs={{0,1},{1,2},{2,3},{3,4},{4,5},{5,6},{6,7},{7,8},{8,9},{9,10},{10,1... | collective-permute-start | bytes 786440 | tf_op jit(solution)/shard_map/ppermute | solution.py:235
  50.3 0.0 copy-done
  50.3 0.2 fusion.40
  50.5 0.0 collective-permute-done.4
  50.5 4.8 %collective-permute-start.6 = (bf16[512,256]{1,0:T(8,128)(2,1)S(1)}, bf16[512,256]{1,0:T(8,128)(2,1)S(1)}, u32[]{:S(2)}, u32[]{:S(2)}) collective-permute-start(bf16[512,256]{1,0:T(8,128)(2,1)S(1)} %collective-permute-done.4), channel_id=1, source_target_pairs={{0,1},{1,2},{2,3},{3,4},{4,5},{5,6},{6,7},{7,8},{8,9},{9,10},{10,1... | collective-permute-start | bytes 786440 | tf_op jit(solution)/shard_map/ppermute | solution.py:235
  55.3 0.0 collective-permute-done.3
  55.3 3.2 %collective-permute-start.5 = (bf16[512,256]{1,0:T(8,128)(2,1)S(1)}, bf16[512,256]{1,0:T(8,128)(2,1)S(1)}, u32[]{:S(2)}, u32[]{:S(2)}) collective-permute-start(bf16[512,256]{1,0:T(8,128)(2,1)S(1)} %collective-permute-done.3), channel_id=1, source_target_pairs={{0,1},{1,2},{2,3},{3,4},{4,5},{5,6},{6,7},{7,8},{8,9},{9,10},{10,1... | collective-permute-start | bytes 786440 | tf_op jit(solution)/shard_map/ppermute | solution.py:235
  58.5 1.2 %convolution_add_fusion.1 = f32[512,256]{1,0:T(8,128)S(1)} fusion(f32[512,256]{1,0:T(8,128)S(1)} %fusion.40, bf16[512,256]{1,0:T(8,128)(2,1)} %carry_and_gate.1, bf16[4096,256]{1,0:T(8,128)(2,1)S(1)} %copy-done, s32[]{:T(128)S(6)} %select_n.58), kind=kOutput, calls=%fused_computation.7 | convolution fusion | flops 67239936 | bytes 1441796 | tf_op jit(solution)/shard_map/dot_general | solution.py:240
  59.7 0.2 fusion.38
  59.9 0.0 collective-permute-done.6
  59.9 3.6 %collective-permute-start.8 = (bf16[512,256]{1,0:T(8,128)(2,1)S(1)}, bf16[512,256]{1,0:T(8,128)(2,1)S(1)}, u32[]{:S(2)}, u32[]{:S(2)}) collective-permute-start(bf16[512,256]{1,0:T(8,128)(2,1)S(1)} %collective-permute-done.6), channel_id=1, source_target_pairs={{0,1},{1,2},{2,3},{3,4},{4,5},{5,6},{6,7},{7,8},{8,9},{9,10},{10,1... | collective-permute-start | bytes 786440 | tf_op jit(solution)/shard_map/ppermute | solution.py:235
  63.6 0.0 collective-permute-done.5
  63.6 3.2 %collective-permute-start.7 = (bf16[512,256]{1,0:T(8,128)(2,1)S(1)}, bf16[512,256]{1,0:T(8,128)(2,1)S(1)}, u32[]{:S(2)}, u32[]{:S(2)}) collective-permute-start(bf16[512,256]{1,0:T(8,128)(2,1)S(1)} %collective-permute-done.5), channel_id=1, source_target_pairs={{0,1},{1,2},{2,3},{3,4},{4,5},{5,6},{6,7},{7,8},{8,9},{9,10},{10,1... | collective-permute-start | bytes 786440 | tf_op jit(solution)/shard_map/ppermute | solution.py:235
  66.8 0.2 fusion.33
  67.1 0.2 fusion.35
  67.3 0.1 collective-permute-done.8
  67.4 4.6 %collective-permute-start.10 = (bf16[512,256]{1,0:T(8,128)(2,1)S(1)}, bf16[512,256]{1,0:T(8,128)(2,1)S(1)}, u32[]{:S(2)}, u32[]{:S(2)}) collective-permute-start(bf16[512,256]{1,0:T(8,128)(2,1)S(1)} %collective-permute-done.8), channel_id=1, source_target_pairs={{0,1},{1,2},{2,3},{3,4},{4,5},{5,6},{6,7},{7,8},{8,9},{9,10},{10,1... | collective-permute-start | bytes 786440 | tf_op jit(solution)/shard_map/ppermute | solution.py:235
  71.9 0.0 collective-permute-done.7
  71.9 3.2 %collective-permute-start.9 = (bf16[512,256]{1,0:T(8,128)(2,1)S(1)}, bf16[512,256]{1,0:T(8,128)(2,1)S(1)}, u32[]{:S(2)}, u32[]{:S(2)}) collective-permute-start(bf16[512,256]{1,0:T(8,128)(2,1)S(1)} %collective-permute-done.7), channel_id=1, source_target_pairs={{0,1},{1,2},{2,3},{3,4},{4,5},{5,6},{6,7},{7,8},{8,9},{9,10},{10,1... | collective-permute-start | bytes 786440 | tf_op jit(solution)/shard_map/ppermute | solution.py:235
  75.1 0.2 fusion.29
  75.4 0.2 fusion.31
  75.6 0.0 collective-permute-done.10
  75.6 4.6 %collective-permute-start.12 = (bf16[512,256]{1,0:T(8,128)(2,1)S(1)}, bf16[512,256]{1,0:T(8,128)(2,1)S(1)}, u32[]{:S(2)}, u32[]{:S(2)}) collective-permute-start(bf16[512,256]{1,0:T(8,128)(2,1)S(1)} %collective-permute-done.10), channel_id=1, source_target_pairs={{0,1},{1,2},{2,3},{3,4},{4,5},{5,6},{6,7},{7,8},{8,9},{9,10},{10,1... | collective-permute-start | bytes 786440 | tf_op jit(solution)/shard_map/ppermute | solution.py:235
  80.2 0.0 collective-permute-done.9
  80.2 3.2 %collective-permute-start.11 = (bf16[512,256]{1,0:T(8,128)(2,1)S(1)}, bf16[512,256]{1,0:T(8,128)(2,1)S(1)}, u32[]{:S(2)}, u32[]{:S(2)}) collective-permute-start(bf16[512,256]{1,0:T(8,128)(2,1)S(1)} %collective-permute-done.9), channel_id=1, source_target_pairs={{0,1},{1,2},{2,3},{3,4},{4,5},{5,6},{6,7},{7,8},{8,9},{9,10},{10,1... | collective-permute-start | bytes 786440 | tf_op jit(solution)/shard_map/ppermute | solution.py:235
  83.4 0.2 fusion.25
  83.7 0.2 fusion.27
  83.9 0.0 collective-permute-done.12
  83.9 4.6 %collective-permute-start.14 = (bf16[512,256]{1,0:T(8,128)(2,1)S(1)}, bf16[512,256]{1,0:T(8,128)(2,1)S(1)}, u32[]{:S(2)}, u32[]{:S(2)}) collective-permute-start(bf16[512,256]{1,0:T(8,128)(2,1)S(1)} %collective-permute-done.12), channel_id=1, source_target_pairs={{0,1},{1,2},{2,3},{3,4},{4,5},{5,6},{6,7},{7,8},{8,9},{9,10},{10,1... | collective-permute-start | bytes 786440 | tf_op jit(solution)/shard_map/ppermute | solution.py:235
  88.5 0.2 fusion.21
  88.8 0.0 collective-permute-done.11
  88.8 3.0 %collective-permute-start.13 = (bf16[512,256]{1,0:T(8,128)(2,1)S(1)}, bf16[512,256]{1,0:T(8,128)(2,1)S(1)}, u32[]{:S(2)}, u32[]{:S(2)}) collective-permute-start(bf16[512,256]{1,0:T(8,128)(2,1)S(1)} %collective-permute-done.11), channel_id=1, source_target_pairs={{0,1},{1,2},{2,3},{3,4},{4,5},{5,6},{6,7},{7,8},{8,9},{9,10},{10,1... | collective-permute-start | bytes 786440 | tf_op jit(solution)/shard_map/ppermute | solution.py:235
  91.8 0.2 fusion.23
  92.0 0.0 collective-permute-done.14
  92.0 4.8 %collective-permute-start.16 = (bf16[512,256]{1,0:T(8,128)(2,1)S(1)}, bf16[512,256]{1,0:T(8,128)(2,1)S(1)}, u32[]{:S(2)}, u32[]{:S(2)}) collective-permute-start(bf16[512,256]{1,0:T(8,128)(2,1)S(1)} %collective-permute-done.14), channel_id=1, source_target_pairs={{16,31},{17,16},{18,17},{19,18},{20,19},{21,20},{22,21},{23,22},{2... | collective-permute-start | bytes 786440 | tf_op jit(solution)/shard_map/ppermute | solution.py:235
  96.9 0.2 fusion.17
  97.1 0.0 collective-permute-done.13
  97.1 3.0 %collective-permute-start.15 = (bf16[512,256]{1,0:T(8,128)(2,1)S(1)}, bf16[512,256]{1,0:T(8,128)(2,1)S(1)}, u32[]{:S(2)}, u32[]{:S(2)}) collective-permute-start(bf16[512,256]{1,0:T(8,128)(2,1)S(1)} %collective-permute-done.13), channel_id=1, source_target_pairs={{16,31},{17,16},{18,17},{19,18},{20,19},{21,20},{22,21},{23,22},{2... | collective-permute-start | bytes 786440 | tf_op jit(solution)/shard_map/ppermute | solution.py:235
  100.1 0.2 fusion.19
  100.3 0.0 collective-permute-done.16
  100.3 0.2 fusion.13
  100.6 0.3 fusion.5
  100.9 3.6 %collective-permute-done.15 = bf16[512,256]{1,0:T(8,128)(2,1)S(1)} collective-permute-done((bf16[512,256]{1,0:T(8,128)(2,1)S(1)}, bf16[512,256]{1,0:T(8,128)(2,1)S(1)}, u32[]{:S(2)}, u32[]{:S(2)}) %collective-permute-start.15) | collective-permute-done | bytes 262176 | tf_op jit(solution)/shard_map/ppermute | solution.py:235
  104.5 0.2 fusion.15
  104.7 0.3 fusion.11
  105.1 5.1 %collective-permute-start.17 = (f32[512,256]{1,0:T(8,128)S(1)}, f32[512,256]{1,0:T(8,128)S(1)}, u32[]{:S(2)}, u32[]{:S(2)}) collective-permute-start(f32[512,256]{1,0:T(8,128)S(1)} %fusion.11), channel_id=1, source_target_pairs={{0,16},{16,0},{1,17},{17,1},{2,18},{18,2},{3,19},{19,3},{4,20},{20... | collective-permute-start | bytes 1572872 | tf_op jit(solution)/shard_map/ppermute | solution.py:190
  110.2 1.5 %collective-permute-done.17 = f32[512,256]{1,0:T(8,128)S(1)} collective-permute-done((f32[512,256]{1,0:T(8,128)S(1)}, f32[512,256]{1,0:T(8,128)S(1)}, u32[]{:S(2)}, u32[]{:S(2)}) %collective-permute-start.17) | collective-permute-done | bytes 524320 | tf_op jit(solution)/shard_map/ppermute | solution.py:190
  111.7 0.8 add_convert_fusion
  (3 shorter events, 0.0 us)
Async XLA Ops:
  0.0 50.3 %copy-start = (bf16[4096,256]{1,0:T(8,128)(2,1)S(1)}, bf16[4096,256]{1,0:T(8,128)(2,1)}, u32[]{:S(2)}) copy-start(bf16[4096,256]{1,0:T(8,128)(2,1)} %param.13) | copy-start | bytes 6291460
  2.8 9.8 %collective-permute-start = (f32[16,256]{1,0:T(8,128)}, f32[16,256]{1,0:T(8,128)S(1)}, u32[]{:S(2)}, u32[]{:S(2)}) collective-permute-start(f32[16,256]{1,0:T(8,128)} %states.1), channel_id=1, source_target_pairs={{0,16},{16,0},{1,17},{17,1},{2,18},{18,2},{3,19},{19,3},{4,20},{20... | collective-permute-start | bytes 49160 | tf_op jit(solution)/shard_map/ppermute | solution.py:190
  12.6 5.0 %copy-start.2 = (f32[16,256]{1,0:T(8,128)}, f32[16,256]{1,0:T(8,128)S(1)}, u32[]{:S(2)}) copy-start(f32[16,256]{1,0:T(8,128)S(1)} %collective-permute-done.oth_hbm) | copy-start | bytes 49156
  14.1 12.0 %all-to-all-start = ((f32[16,16,256]{2,1,0:T(8,128)}), f32[16,16,256]{2,1,0:T(8,128)S(1)}, u32[]{:S(2)}, u32[]{:S(2)}) async-start(f32[16,16,256]{2,1,0:T(8,128)} %broadcast_in_dim.4), calls=%async_computation | async-start | bytes 524288 | tf_op jit(solution)/shard_map/all_to_all | solution.py:211
  26.1 0.7 copy-start.1
  29.7 12.3 %collective-permute-start.2 = (bf16[512,256]{1,0:T(8,128)(2,1)}, bf16[512,256]{1,0:T(8,128)(2,1)S(1)}, u32[]{:S(2)}, u32[]{:S(2)}) collective-permute-start(bf16[512,256]{1,0:T(8,128)(2,1)} %carry_and_gate.1), channel_id=1, source_target_pairs={{0,1},{1,2},{2,3},{3,4},{4,5},{5,6},{6,7},{7,8},{8,9},{9,10},{10,1... | collective-permute-start | bytes 786440 | tf_op jit(solution)/shard_map/ppermute | solution.py:235
  38.4 8.5 %collective-permute-start.1 = (bf16[512,256]{1,0:T(8,128)(2,1)}, bf16[512,256]{1,0:T(8,128)(2,1)S(1)}, u32[]{:S(2)}, u32[]{:S(2)}) collective-permute-start(bf16[512,256]{1,0:T(8,128)(2,1)} %carry_and_gate.1), channel_id=1, source_target_pairs={{16,1},{17,2},{18,3},{19,4},{20,5},{21,6},{22,7},{23,8},{24,9},{25... | collective-permute-start | bytes 786440 | tf_op jit(solution)/shard_map/ppermute | solution.py:235
  42.0 8.5 %collective-permute-start.4 = (bf16[512,256]{1,0:T(8,128)(2,1)S(1)}, bf16[512,256]{1,0:T(8,128)(2,1)S(1)}, u32[]{:S(2)}, u32[]{:S(2)}) collective-permute-start(bf16[512,256]{1,0:T(8,128)(2,1)S(1)} %collective-permute-done.2), channel_id=1, source_target_pairs={{0,1},{1,2},{2,3},{3,4},{4,5},{5,6},{6,7},{7,8},{8,9},{9,10},{10,1... | collective-permute-start | bytes 786440 | tf_op jit(solution)/shard_map/ppermute | solution.py:235
  47.0 8.3 %collective-permute-start.3 = (bf16[512,256]{1,0:T(8,128)(2,1)S(1)}, bf16[512,256]{1,0:T(8,128)(2,1)S(1)}, u32[]{:S(2)}, u32[]{:S(2)}) collective-permute-start(bf16[512,256]{1,0:T(8,128)(2,1)S(1)} %collective-permute-done.1), channel_id=1, source_target_pairs={{0,1},{1,2},{2,3},{3,4},{4,5},{5,6},{6,7},{7,8},{8,9},{9,10},{10,1... | collective-permute-start | bytes 786440 | tf_op jit(solution)/shard_map/ppermute | solution.py:235
  50.5 9.4 %collective-permute-start.6 = (bf16[512,256]{1,0:T(8,128)(2,1)S(1)}, bf16[512,256]{1,0:T(8,128)(2,1)S(1)}, u32[]{:S(2)}, u32[]{:S(2)}) collective-permute-start(bf16[512,256]{1,0:T(8,128)(2,1)S(1)} %collective-permute-done.4), channel_id=1, source_target_pairs={{0,1},{1,2},{2,3},{3,4},{4,5},{5,6},{6,7},{7,8},{8,9},{9,10},{10,1... | collective-permute-start | bytes 786440 | tf_op jit(solution)/shard_map/ppermute | solution.py:235
  55.3 8.3 %collective-permute-start.5 = (bf16[512,256]{1,0:T(8,128)(2,1)S(1)}, bf16[512,256]{1,0:T(8,128)(2,1)S(1)}, u32[]{:S(2)}, u32[]{:S(2)}) collective-permute-start(bf16[512,256]{1,0:T(8,128)(2,1)S(1)} %collective-permute-done.3), channel_id=1, source_target_pairs={{0,1},{1,2},{2,3},{3,4},{4,5},{5,6},{6,7},{7,8},{8,9},{9,10},{10,1... | collective-permute-start | bytes 786440 | tf_op jit(solution)/shard_map/ppermute | solution.py:235
  59.9 7.4 %collective-permute-start.8 = (bf16[512,256]{1,0:T(8,128)(2,1)S(1)}, bf16[512,256]{1,0:T(8,128)(2,1)S(1)}, u32[]{:S(2)}, u32[]{:S(2)}) collective-permute-start(bf16[512,256]{1,0:T(8,128)(2,1)S(1)} %collective-permute-done.6), channel_id=1, source_target_pairs={{0,1},{1,2},{2,3},{3,4},{4,5},{5,6},{6,7},{7,8},{8,9},{9,10},{10,1... | collective-permute-start | bytes 786440 | tf_op jit(solution)/shard_map/ppermute | solution.py:235
  63.6 8.3 %collective-permute-start.7 = (bf16[512,256]{1,0:T(8,128)(2,1)S(1)}, bf16[512,256]{1,0:T(8,128)(2,1)S(1)}, u32[]{:S(2)}, u32[]{:S(2)}) collective-permute-start(bf16[512,256]{1,0:T(8,128)(2,1)S(1)} %collective-permute-done.5), channel_id=1, source_target_pairs={{0,1},{1,2},{2,3},{3,4},{4,5},{5,6},{6,7},{7,8},{8,9},{9,10},{10,1... | collective-permute-start | bytes 786440 | tf_op jit(solution)/shard_map/ppermute | solution.py:235
  67.4 8.2 %collective-permute-start.10 = (bf16[512,256]{1,0:T(8,128)(2,1)S(1)}, bf16[512,256]{1,0:T(8,128)(2,1)S(1)}, u32[]{:S(2)}, u32[]{:S(2)}) collective-permute-start(bf16[512,256]{1,0:T(8,128)(2,1)S(1)} %collective-permute-done.8), channel_id=1, source_target_pairs={{0,1},{1,2},{2,3},{3,4},{4,5},{5,6},{6,7},{7,8},{8,9},{9,10},{10,1... | collective-permute-start | bytes 786440 | tf_op jit(solution)/shard_map/ppermute | solution.py:235
  71.9 8.3 %collective-permute-start.9 = (bf16[512,256]{1,0:T(8,128)(2,1)S(1)}, bf16[512,256]{1,0:T(8,128)(2,1)S(1)}, u32[]{:S(2)}, u32[]{:S(2)}) collective-permute-start(bf16[512,256]{1,0:T(8,128)(2,1)S(1)} %collective-permute-done.7), channel_id=1, source_target_pairs={{0,1},{1,2},{2,3},{3,4},{4,5},{5,6},{6,7},{7,8},{8,9},{9,10},{10,1... | collective-permute-start | bytes 786440 | tf_op jit(solution)/shard_map/ppermute | solution.py:235
  75.6 8.3 %collective-permute-start.12 = (bf16[512,256]{1,0:T(8,128)(2,1)S(1)}, bf16[512,256]{1,0:T(8,128)(2,1)S(1)}, u32[]{:S(2)}, u32[]{:S(2)}) collective-permute-start(bf16[512,256]{1,0:T(8,128)(2,1)S(1)} %collective-permute-done.10), channel_id=1, source_target_pairs={{0,1},{1,2},{2,3},{3,4},{4,5},{5,6},{6,7},{7,8},{8,9},{9,10},{10,1... | collective-permute-start | bytes 786440 | tf_op jit(solution)/shard_map/ppermute | solution.py:235
  80.2 8.5 %collective-permute-start.11 = (bf16[512,256]{1,0:T(8,128)(2,1)S(1)}, bf16[512,256]{1,0:T(8,128)(2,1)S(1)}, u32[]{:S(2)}, u32[]{:S(2)}) collective-permute-start(bf16[512,256]{1,0:T(8,128)(2,1)S(1)} %collective-permute-done.9), channel_id=1, source_target_pairs={{0,1},{1,2},{2,3},{3,4},{4,5},{5,6},{6,7},{7,8},{8,9},{9,10},{10,1... | collective-permute-start | bytes 786440 | tf_op jit(solution)/shard_map/ppermute | solution.py:235
  83.9 8.1 %collective-permute-start.14 = (bf16[512,256]{1,0:T(8,128)(2,1)S(1)}, bf16[512,256]{1,0:T(8,128)(2,1)S(1)}, u32[]{:S(2)}, u32[]{:S(2)}) collective-permute-start(bf16[512,256]{1,0:T(8,128)(2,1)S(1)} %collective-permute-done.12), channel_id=1, source_target_pairs={{0,1},{1,2},{2,3},{3,4},{4,5},{5,6},{6,7},{7,8},{8,9},{9,10},{10,1... | collective-permute-start | bytes 786440 | tf_op jit(solution)/shard_map/ppermute | solution.py:235
  88.8 8.3 %collective-permute-start.13 = (bf16[512,256]{1,0:T(8,128)(2,1)S(1)}, bf16[512,256]{1,0:T(8,128)(2,1)S(1)}, u32[]{:S(2)}, u32[]{:S(2)}) collective-permute-start(bf16[512,256]{1,0:T(8,128)(2,1)S(1)} %collective-permute-done.11), channel_id=1, source_target_pairs={{0,1},{1,2},{2,3},{3,4},{4,5},{5,6},{6,7},{7,8},{8,9},{9,10},{10,1... | collective-permute-start | bytes 786440 | tf_op jit(solution)/shard_map/ppermute | solution.py:235
  92.0 8.3 %collective-permute-start.16 = (bf16[512,256]{1,0:T(8,128)(2,1)S(1)}, bf16[512,256]{1,0:T(8,128)(2,1)S(1)}, u32[]{:S(2)}, u32[]{:S(2)}) collective-permute-start(bf16[512,256]{1,0:T(8,128)(2,1)S(1)} %collective-permute-done.14), channel_id=1, source_target_pairs={{16,31},{17,16},{18,17},{19,18},{20,19},{21,20},{22,21},{23,22},{2... | collective-permute-start | bytes 786440 | tf_op jit(solution)/shard_map/ppermute | solution.py:235
  97.1 7.4 %collective-permute-start.15 = (bf16[512,256]{1,0:T(8,128)(2,1)S(1)}, bf16[512,256]{1,0:T(8,128)(2,1)S(1)}, u32[]{:S(2)}, u32[]{:S(2)}) collective-permute-start(bf16[512,256]{1,0:T(8,128)(2,1)S(1)} %collective-permute-done.13), channel_id=1, source_target_pairs={{16,31},{17,16},{18,17},{19,18},{20,19},{21,20},{22,21},{23,22},{2... | collective-permute-start | bytes 786440 | tf_op jit(solution)/shard_map/ppermute | solution.py:235
  105.1 6.6 %collective-permute-start.17 = (f32[512,256]{1,0:T(8,128)S(1)}, f32[512,256]{1,0:T(8,128)S(1)}, u32[]{:S(2)}, u32[]{:S(2)}) collective-permute-start(f32[512,256]{1,0:T(8,128)S(1)} %fusion.11), channel_id=1, source_target_pairs={{0,16},{16,0},{1,17},{17,1},{2,18},{18,2},{3,19},{19,3},{4,20},{20... | collective-permute-start | bytes 1572872 | tf_op jit(solution)/shard_map/ppermute | solution.py:190

commit v2 on v1

--- a/solution.py
+++ b/solution.py
@@ -232,6 +232,7 @@
 
     ring = [(c * depth + i, c * depth + (i + 1 - 2 * c) % depth) for c in range(2) for i in range(depth)]
     cross = [((1 - c) * depth + i, c * depth + (i + 1 - 2 * c) % depth) for c in range(2) for i in range(depth)]
+    across = [(c * depth + i, (1 - c) * depth + (i + 1 - 2 * c) % depth) for c in range(2) for i in range(depth)]
     hop = lambda array, pairs=ring: lax.ppermute(array, ("core", "ch"), pairs)
 
     def project(array, distance):
@@ -243,7 +244,7 @@
     own, oth = hop(own), hop(own, cross)
     sum_own, sum_oth = sum_own + project(own, 1), project(oth, 1)
     last_oth = oth
-    for distance in range(2, depth // 2):
+    for distance in range(2, depth // 2 - 1):
         last_own = own
         own = hop(own)
         oth, last_own = lax.optimization_barrier((oth, last_own))
@@ -251,13 +252,23 @@
         own, last_oth = lax.optimization_barrier((own, last_oth))
         sum_own = sum_own + project(own, distance)
         sum_oth = sum_oth + project(oth, distance)
+    far = depth // 2
+    early = sum_oth
+    last_own = own
+    own = hop(own)
+    oth, last_own = lax.optimization_barrier((oth, last_own))
+    oth, from_up = hop(oth, ring[depth:]), hop(oth, across[:depth])
+    early = lax.ppermute(early, "core", [(0, 1)])
+    sum_own = sum_own + project(own, far - 1)
+    sum_oth = sum_oth + project(oth, far - 1)
     last_own, own = own, hop(own, ring[depth:])
     oth, last_own = lax.optimization_barrier((oth, last_own))
     oth = hop(oth, ring[depth:])
-    sum_own = sum_own + project(own, depth // 2)
-    sum_oth = sum_oth + project(oth, depth // 2)
-    sum_oth, sum_own = lax.optimization_barrier((sum_oth, sum_own))
-    return (sum_own + swap(sum_oth)).astype(BF16)
+    sum_oth = sum_oth + project(oth, far)
+    late = lax.ppermute(sum_oth, "core", [(1, 0)])
+    sum_own = sum_own + project(from_up, 1 - far) + project(own, far)
+    sum_own, early, late = lax.optimization_barrier((sum_own, early, late))
+    return (sum_own + (early + late)).astype(BF16)
 
 
 def solution(mesh):

time: 114 us -> 111 us (0.974)
  starting transfers between devices: 81.9 us -> 79.3 us
    ppermute x2 -> x1, starting transfers between devices: 13.9 us -> 8.79 us  [body(): swap = lambda array: lax.ppermute(array, 'core', [(0, 1), (1, 0)])]
    ppermute x0 -> x2, starting transfers between devices: none -> 2.71 us  [the longest x1 1.42 us: body(): late = lax.ppermute(sum_oth, 'core', [(1, 0)])]
    ppermute x2 -> x1, waiting for transfers between devices: 2.53 us -> 1.02 us  [body(): swap = lambda array: lax.ppermute(array, 'core', [(0, 1), (1, 0)])]
    ppermute x16 -> x17, waiting for transfers between devices: 5.41 us -> 5.89 us  [body(): hop = lambda array, pairs=ring: lax.ppermute(array, ('core', 'ch'), pairs)]
    ppermute x16 -> x17, starting transfers between devices: 64.5 us -> 64.2 us  [body(): hop = lambda array, pairs=ring: lax.ppermute(array, ('core', 'ch'), pairs)]
    dot_general x17 -> x18, matrix products: 5.02 us -> 5.2 us  [project(): return jnp.dot(array, weight, preferred_element_type=F32)]
  transfers between devices with their start and end apart: 19 -> 21, of which waited for: 6 -> 7; matrix products, arithmetic and copies ran while one was open for 4% -> 5% of each run, Pallas kernels for 5% -> 5%
where the time goes in v2:
time: 111 us; the launch traced here: 110 us
  starting transfers between devices  79.3 us (71%)
  waiting for transfers between devices  11.1 us (10%)
  Pallas kernels  10.8 us (10%)
  matrix products  5.2 us (5%)
  other arithmetic  1.53 us (1%)
  local copies, waits for them, and re-layouts  1.44 us (1%)
    ppermute x17, starting transfers between devices, body(): hop = lambda array, pairs=ring: lax.ppermute(array, ('core', 'ch'), pairs)  64.2 us
    ppermute x1, starting transfers between devices, body(): swap = lambda array: lax.ppermute(array, 'core', [(0, 1), (1, 0)])  8.79 us
    ppermute x17, waiting for transfers between devices, body(): hop = lambda array, pairs=ring: lax.ppermute(array, ('core', 'ch'), pairs)  5.89 us
    dot_general x18, matrix products, project(): return jnp.dot(array, weight, preferred_element_type=F32)  5.2 us
    pallas_call x1, Pallas kernels, body(): kernel_call(local_kernel, 'chip_convolution', 6 * work, out_shape=shape(b...  5.11 us
    all_to_all x1, starting transfers between devices, body(): lax.all_to_all(every, ('y', 'x'), split_axis=0, concat_axis=0, tiled=True)  3.53 us
    all_to_all x1, waiting for transfers between devices, body(): lax.all_to_all(every, ('y', 'x'), split_axis=0, concat_axis=0, tiled=True)  3.29 us
    pallas_call x1, Pallas kernels, body(): kernel_call(gate_kernel, 'carry_and_gate', 2 * work, out_shape=shape((row...  2.93 us
  transfers between devices with their start and end apart: 21, of which 7 were waited for; matrix products, arithmetic and copies ran while one was open for 5% of the time, Pallas kernels for 5%

profile of v2, /device:TPU:1, one launch (start us, length us, event | category | flops | bytes accessed | tf_op | source)
XLA Modules:
  0.0 109.9 jit_solution(2464092868262682720)
XLA Ops:
  0.0 2.8 %states.1 = f32[16,256]{1,0:T(8,128)} custom-call(bf16[512,256]{1,0:T(8,128)(2,1)} %k_hbm.3, bf16[512,256]{1,0:T(8,128)(2,1)} %v_hbm.3, f32[16,256]{1,0:T(8,128)} %rates_hbm.5), custom_call_target="tpu_custom_call" | custom-call | flops 4194304 | bytes 1048576 | tf_op jit(solution)/shard_map/states/pallas_call | solution.py:198
  2.8 8.8 %collective-permute-start = (f32[16,256]{1,0:T(8,128)}, f32[16,256]{1,0:T(8,128)S(1)}, u32[]{:S(2)}, u32[]{:S(2)}) collective-permute-start(f32[16,256]{1,0:T(8,128)} %states.1), channel_id=1, source_target_pairs={{0,16},{16,0},{1,17},{17,1},{2,18},{18,2},{3,19},{19,3},{4,20},{20... | collective-permute-start | bytes 49160 | tf_op jit(solution)/shard_map/ppermute | solution.py:190
  11.6 1.0 collective-permute-done.oth_hbm
  12.6 0.8 select_add_fusion
  13.4 0.7 broadcast_in_dim.4
  14.1 3.5 %all-to-all-start = ((f32[16,16,256]{2,1,0:T(8,128)}), f32[16,16,256]{2,1,0:T(8,128)S(1)}, u32[]{:S(2)}, u32[]{:S(2)}) async-start(f32[16,16,256]{2,1,0:T(8,128)} %broadcast_in_dim.4), calls=%async_computation | async-start | bytes 524288 | tf_op jit(solution)/shard_map/all_to_all | solution.py:211
  17.7 5.1 %chip_convolution.1.local_hbm = f32[64,16,256]{2,1,0:T(8,128)} custom-call(s32[1]{0:T(128)} %bitcast.core_ref, bf16[512,256]{1,0:T(8,128)(2,1)} %k_hbm.3, bf16[512,256]{1,0:T(8,128)(2,1)} %v_hbm.3, bf16[512,256]{1,0:T(8,128)(2,1)} %q_hbm.1, f32[16,256]{1,0:T(8,128)} %rates_hbm.5, f32[16,256]{1,0:T(8,128)} %resid_hbm.3, f32[1,256]{1,0:T(1,128)} %bitcast.21, ...), custom_call_target="tpu_custom_call" | custom-call | flops 12582912 | bytes 1048576 | tf_op jit(solution)/shard_map/chip_convolution/pallas_call | solution.py:212
  22.8 3.3 %all-to-all-done.all_hbm = f32[16,16,256]{2,1,0:T(8,128)S(1)} async-done(((f32[16,16,256]{2,1,0:T(8,128)}), f32[16,16,256]{2,1,0:T(8,128)S(1)}, u32[]{:S(2)}, u32[]{:S(2)}) %all-to-all-start) | async-done | bytes 262176 | tf_op jit(solution)/shard_map/all_to_all | solution.py:211
  26.1 0.7 copy-done.1
  26.8 2.9 %carry_and_gate.1 = bf16[512,256]{1,0:T(8,128)(2,1)} custom-call(s32[1]{0:T(128)} %bitcast.core_ref, s32[1]{0:T(128)} %bitcast.1.chip_ref, f32[16,16,256]{2,1,0:T(8,128)} %copy-done.1, f32[16,256]{1,0:T(8,128)} %rates_hbm.5, f32[16,256]{1,0:T(8,128)} %resid_hbm.3, f32[64,16,256]{2,1,0:T(8,128)} %chip_convolution.1.local_hbm), custom_call_target="tpu_custom_call" | custom-call | flops 4194304 | bytes 1048576 | tf_op jit(solution)/shard_map/carry_and_gate/pallas_call | solution.py:222
  29.7 8.7 %collective-permute-start.1 = (bf16[512,256]{1,0:T(8,128)(2,1)}, bf16[512,256]{1,0:T(8,128)(2,1)S(1)}, u32[]{:S(2)}, u32[]{:S(2)}) collective-permute-start(bf16[512,256]{1,0:T(8,128)(2,1)} %carry_and_gate.1), channel_id=1, source_target_pairs={{0,1},{1,2},{2,3},{3,4},{4,5},{5,6},{6,7},{7,8},{8,9},{9,10},{10,1... | collective-permute-start | bytes 786440 | tf_op jit(solution)/shard_map/ppermute | solution.py:236
  38.4 1.9 %collective-permute-start.3 = (bf16[512,256]{1,0:T(8,128)(2,1)}, bf16[512,256]{1,0:T(8,128)(2,1)S(1)}, u32[]{:S(2)}, u32[]{:S(2)}) collective-permute-start(bf16[512,256]{1,0:T(8,128)(2,1)} %carry_and_gate.1), channel_id=1, source_target_pairs={{16,1},{17,2},{18,3},{19,4},{20,5},{21,6},{22,7},{23,8},{24,9},{25... | collective-permute-start | bytes 786440 | tf_op jit(solution)/shard_map/ppermute | solution.py:236
  40.4 1.7 %collective-permute-done.1 = bf16[512,256]{1,0:T(8,128)(2,1)S(1)} collective-permute-done((bf16[512,256]{1,0:T(8,128)(2,1)}, bf16[512,256]{1,0:T(8,128)(2,1)S(1)}, u32[]{:S(2)}, u32[]{:S(2)}) %collective-permute-start.1) | collective-permute-done | bytes 262176 | tf_op jit(solution)/shard_map/ppermute | solution.py:236
  42.0 4.9 %collective-permute-start.2 = (bf16[512,256]{1,0:T(8,128)(2,1)S(1)}, bf16[512,256]{1,0:T(8,128)(2,1)S(1)}, u32[]{:S(2)}, u32[]{:S(2)}) collective-permute-start(bf16[512,256]{1,0:T(8,128)(2,1)S(1)} %collective-permute-done.1), channel_id=1, source_target_pairs={{0,1},{1,2},{2,3},{3,4},{4,5},{5,6},{6,7},{7,8},{8,9},{9,10},{10,1... | collective-permute-start | bytes 786440 | tf_op jit(solution)/shard_map/ppermute | solution.py:236
  47.0 0.0 collective-permute-done.3
  47.0 3.2 %collective-permute-start.5 = (bf16[512,256]{1,0:T(8,128)(2,1)S(1)}, bf16[512,256]{1,0:T(8,128)(2,1)S(1)}, u32[]{:S(2)}, u32[]{:S(2)}) collective-permute-start(bf16[512,256]{1,0:T(8,128)(2,1)S(1)} %collective-permute-done.3), channel_id=1, source_target_pairs={{0,1},{1,2},{2,3},{3,4},{4,5},{5,6},{6,7},{7,8},{8,9},{9,10},{10,1... | collective-permute-start | bytes 786440 | tf_op jit(solution)/shard_map/ppermute | solution.py:236
  50.3 0.2 fusion.40
  50.5 0.0 collective-permute-done.2
  50.5 4.7 %collective-permute-start.4 = (bf16[512,256]{1,0:T(8,128)(2,1)S(1)}, bf16[512,256]{1,0:T(8,128)(2,1)S(1)}, u32[]{:S(2)}, u32[]{:S(2)}) collective-permute-start(bf16[512,256]{1,0:T(8,128)(2,1)S(1)} %collective-permute-done.2), channel_id=1, source_target_pairs={{0,1},{1,2},{2,3},{3,4},{4,5},{5,6},{6,7},{7,8},{8,9},{9,10},{10,1... | collective-permute-start | bytes 786440 | tf_op jit(solution)/shard_map/ppermute | solution.py:236
  55.3 0.0 collective-permute-done.5
  55.3 3.2 %collective-permute-start.7 = (bf16[512,256]{1,0:T(8,128)(2,1)S(1)}, bf16[512,256]{1,0:T(8,128)(2,1)S(1)}, u32[]{:S(2)}, u32[]{:S(2)}) collective-permute-start(bf16[512,256]{1,0:T(8,128)(2,1)S(1)} %collective-permute-done.5), channel_id=1, source_target_pairs={{0,1},{1,2},{2,3},{3,4},{4,5},{5,6},{6,7},{7,8},{8,9},{9,10},{10,1... | collective-permute-start | bytes 786440 | tf_op jit(solution)/shard_map/ppermute | solution.py:236
  58.5 1.2 %convolution_add_fusion.4 = f32[512,256]{1,0:T(8,128)S(1)} fusion(f32[512,256]{1,0:T(8,128)S(1)} %fusion.40, bf16[512,256]{1,0:T(8,128)(2,1)} %carry_and_gate.1, bf16[4096,256]{1,0:T(8,128)(2,1)S(1)} %copy-done, s32[]{:T(128)S(6)} %select_n.53), kind=kOutput, calls=%fused_computation.15 | convolution fusion | flops 67239936 | bytes 1441796 | tf_op jit(solution)/shard_map/dot_general | solution.py:241
  59.7 0.2 fusion.36
  59.9 0.0 collective-permute-done.4
  59.9 3.7 %collective-permute-start.6 = (bf16[512,256]{1,0:T(8,128)(2,1)S(1)}, bf16[512,256]{1,0:T(8,128)(2,1)S(1)}, u32[]{:S(2)}, u32[]{:S(2)}) collective-permute-start(bf16[512,256]{1,0:T(8,128)(2,1)S(1)} %collective-permute-done.4), channel_id=1, source_target_pairs={{0,1},{1,2},{2,3},{3,4},{4,5},{5,6},{6,7},{7,8},{8,9},{9,10},{10,1... | collective-permute-start | bytes 786440 | tf_op jit(solution)/shard_map/ppermute | solution.py:236
  63.6 0.0 collective-permute-done.7
  63.6 3.2 %collective-permute-start.9 = (bf16[512,256]{1,0:T(8,128)(2,1)S(1)}, bf16[512,256]{1,0:T(8,128)(2,1)S(1)}, u32[]{:S(2)}, u32[]{:S(2)}) collective-permute-start(bf16[512,256]{1,0:T(8,128)(2,1)S(1)} %collective-permute-done.7), channel_id=1, source_target_pairs={{0,1},{1,2},{2,3},{3,4},{4,5},{5,6},{6,7},{7,8},{8,9},{9,10},{10,1... | collective-permute-start | bytes 786440 | tf_op jit(solution)/shard_map/ppermute | solution.py:236
  66.8 0.2 fusion.34
  67.1 0.2 fusion.32
  67.3 0.1 collective-permute-done.6
  67.3 4.6 %collective-permute-start.8 = (bf16[512,256]{1,0:T(8,128)(2,1)S(1)}, bf16[512,256]{1,0:T(8,128)(2,1)S(1)}, u32[]{:S(2)}, u32[]{:S(2)}) collective-permute-start(bf16[512,256]{1,0:T(8,128)(2,1)S(1)} %collective-permute-done.6), channel_id=1, source_target_pairs={{0,1},{1,2},{2,3},{3,4},{4,5},{5,6},{6,7},{7,8},{8,9},{9,10},{10,1... | collective-permute-start | bytes 786440 | tf_op jit(solution)/shard_map/ppermute | solution.py:236
  71.9 0.0 collective-permute-done.9
  71.9 3.2 %collective-permute-start.11 = (bf16[512,256]{1,0:T(8,128)(2,1)S(1)}, bf16[512,256]{1,0:T(8,128)(2,1)S(1)}, u32[]{:S(2)}, u32[]{:S(2)}) collective-permute-start(bf16[512,256]{1,0:T(8,128)(2,1)S(1)} %collective-permute-done.9), channel_id=1, source_target_pairs={{0,1},{1,2},{2,3},{3,4},{4,5},{5,6},{6,7},{7,8},{8,9},{9,10},{10,1... | collective-permute-start | bytes 786440 | tf_op jit(solution)/shard_map/ppermute | solution.py:236
  75.1 0.2 fusion.30
  75.4 0.2 fusion.28
  75.6 0.0 collective-permute-done.8
  75.6 4.6 %collective-permute-start.10 = (bf16[512,256]{1,0:T(8,128)(2,1)S(1)}, bf16[512,256]{1,0:T(8,128)(2,1)S(1)}, u32[]{:S(2)}, u32[]{:S(2)}) collective-permute-start(bf16[512,256]{1,0:T(8,128)(2,1)S(1)} %collective-permute-done.8), channel_id=1, source_target_pairs={{0,1},{1,2},{2,3},{3,4},{4,5},{5,6},{6,7},{7,8},{8,9},{9,10},{10,1... | collective-permute-start | bytes 786440 | tf_op jit(solution)/shard_map/ppermute | solution.py:236
  80.2 3.2 %collective-permute-start.13 = (bf16[512,256]{1,0:T(8,128)(2,1)S(1)}, bf16[512,256]{1,0:T(8,128)(2,1)S(1)}, u32[]{:S(2)}, u32[]{:S(2)}) collective-permute-start(bf16[512,256]{1,0:T(8,128)(2,1)S(1)} %collective-permute-done.11), channel_id=1, source_target_pairs={{0,1},{1,2},{2,3},{3,4},{4,5},{5,6},{6,7},{7,8},{8,9},{9,10},{10,1... | collective-permute-start | bytes 786440 | tf_op jit(solution)/shard_map/ppermute | solution.py:236
  83.4 0.2 fusion.26
  83.7 0.2 fusion.24
  83.9 0.0 collective-permute-done.10
  83.9 4.6 %collective-permute-start.12 = (bf16[512,256]{1,0:T(8,128)(2,1)S(1)}, bf16[512,256]{1,0:T(8,128)(2,1)S(1)}, u32[]{:S(2)}, u32[]{:S(2)}) collective-permute-start(bf16[512,256]{1,0:T(8,128)(2,1)S(1)} %collective-permute-done.10), channel_id=1, source_target_pairs={{0,1},{1,2},{2,3},{3,4},{4,5},{5,6},{6,7},{7,8},{8,9},{9,10},{10,1... | collective-permute-start | bytes 786440 | tf_op jit(solution)/shard_map/ppermute | solution.py:236
  88.5 0.0 collective-permute-done.13
  88.6 3.2 %collective-permute-start.17 = (bf16[512,256]{1,0:T(8,128)(2,1)S(1)}, bf16[512,256]{1,0:T(8,128)(2,1)S(1)}, u32[]{:S(2)}, u32[]{:S(2)}) collective-permute-start(bf16[512,256]{1,0:T(8,128)(2,1)S(1)} %collective-permute-done.13), channel_id=1, source_target_pairs={{16,31},{17,16},{18,17},{19,18},{20,19},{21,20},{22,21},{23,22},{2... | collective-permute-start | bytes 786440 | tf_op jit(solution)/shard_map/ppermute | solution.py:236
  91.8 1.3 %collective-permute-start.14 = (bf16[512,256]{1,0:T(8,128)(2,1)S(1)}, bf16[512,256]{1,0:T(8,128)(2,1)S(1)}, u32[]{:S(2)}, u32[]{:S(2)}) collective-permute-start(bf16[512,256]{1,0:T(8,128)(2,1)S(1)} %collective-permute-done.13), channel_id=1, source_target_pairs={{0,17},{1,18},{2,19},{3,20},{4,21},{5,22},{6,23},{7,24},{8,25},{9,... | collective-permute-start | bytes 786440 | tf_op jit(solution)/shard_map/ppermute | solution.py:236
  93.1 0.2 fusion.20
  93.3 0.3 fusion.4
  93.6 0.2 fusion.22
  93.8 1.3 %collective-permute-start.16 = (f32[512,256]{1,0:T(8,128)S(1)}, f32[512,256]{1,0:T(8,128)S(1)}, u32[]{:S(2)}, u32[]{:S(2)}) collective-permute-start(f32[512,256]{1,0:T(8,128)S(1)} %fusion.4), channel_id=1, source_target_pairs={{0,16},{1,17},{2,18},{3,19},{4,20},{5,21},{6,22},{7,23},{8,24},{9,... | collective-permute-start | bytes 1572872 | tf_op jit(solution)/shard_map/ppermute | solution.py:261
  95.1 0.9 collective-permute-done.17
  96.0 0.0 collective-permute-done.12
  96.0 4.1 %collective-permute-start.18 = (bf16[512,256]{1,0:T(8,128)(2,1)S(1)}, bf16[512,256]{1,0:T(8,128)(2,1)S(1)}, u32[]{:S(2)}, u32[]{:S(2)}) collective-permute-start(bf16[512,256]{1,0:T(8,128)(2,1)S(1)} %collective-permute-done.17), channel_id=1, source_target_pairs={{16,31},{17,16},{18,17},{19,18},{20,19},{21,20},{22,21},{23,22},{2... | collective-permute-start | bytes 786440 | tf_op jit(solution)/shard_map/ppermute | solution.py:236
  100.1 1.9 %collective-permute-start.15 = (bf16[512,256]{1,0:T(8,128)(2,1)S(1)}, bf16[512,256]{1,0:T(8,128)(2,1)S(1)}, u32[]{:S(2)}, u32[]{:S(2)}) collective-permute-start(bf16[512,256]{1,0:T(8,128)(2,1)S(1)} %collective-permute-done.12), channel_id=1, source_target_pairs={{16,31},{17,16},{18,17},{19,18},{20,19},{21,20},{22,21},{23,22},{2... | collective-permute-start | bytes 786440 | tf_op jit(solution)/shard_map/ppermute | solution.py:236
  102.0 0.2 fusion.18
  102.2 3.3 %collective-permute-done.14 = bf16[512,256]{1,0:T(8,128)(2,1)S(1)} collective-permute-done((bf16[512,256]{1,0:T(8,128)(2,1)S(1)}, bf16[512,256]{1,0:T(8,128)(2,1)S(1)}, u32[]{:S(2)}, u32[]{:S(2)}) %collective-permute-start.14) | collective-permute-done | bytes 262176 | tf_op jit(solution)/shard_map/ppermute | solution.py:236
  105.5 0.2 fusion.11
  105.7 0.2 fusion.14
  106.0 0.2 fusion
  106.2 1.4 %collective-permute-start.19 = (f32[512,256]{1,0:T(8,128)S(1)}, f32[512,256]{1,0:T(8,128)S(1)}, u32[]{:S(2)}, u32[]{:S(2)}) collective-permute-start(f32[512,256]{1,0:T(8,128)S(1)} %fusion), channel_id=1, source_target_pairs={{16,0},{17,1},{18,2},{19,3},{20,4},{21,5},{22,6},{23,7},{24,8},{25... | collective-permute-start | bytes 1572872 | tf_op jit(solution)/shard_map/ppermute | solution.py:268
  107.7 0.3 fusion.10
  108.0 0.2 convolution_add_fusion.2
  108.2 0.0 collective-permute-done.16
  108.2 0.9 collective-permute-done.19
  109.1 0.8 add_convert_fusion
  (8 shorter events, 0.0 us)
Async XLA Ops:
  0.0 50.3 %copy-start = (bf16[4096,256]{1,0:T(8,128)(2,1)S(1)}, bf16[4096,256]{1,0:T(8,128)(2,1)}, u32[]{:S(2)}) copy-start(bf16[4096,256]{1,0:T(8,128)(2,1)} %param.13) | copy-start | bytes 6291460
  2.8 9.8 %collective-permute-start = (f32[16,256]{1,0:T(8,128)}, f32[16,256]{1,0:T(8,128)S(1)}, u32[]{:S(2)}, u32[]{:S(2)}) collective-permute-start(f32[16,256]{1,0:T(8,128)} %states.1), channel_id=1, source_target_pairs={{0,16},{16,0},{1,17},{17,1},{2,18},{18,2},{3,19},{19,3},{4,20},{20... | collective-permute-start | bytes 49160 | tf_op jit(solution)/shard_map/ppermute | solution.py:190
  12.6 5.0 %copy-start.2 = (f32[16,256]{1,0:T(8,128)}, f32[16,256]{1,0:T(8,128)S(1)}, u32[]{:S(2)}) copy-start(f32[16,256]{1,0:T(8,128)S(1)} %collective-permute-done.oth_hbm) | copy-start | bytes 49156
  14.1 12.0 %all-to-all-start = ((f32[16,16,256]{2,1,0:T(8,128)}), f32[16,16,256]{2,1,0:T(8,128)S(1)}, u32[]{:S(2)}, u32[]{:S(2)}) async-start(f32[16,16,256]{2,1,0:T(8,128)} %broadcast_in_dim.4), calls=%async_computation | async-start | bytes 524288 | tf_op jit(solution)/shard_map/all_to_all | solution.py:211
  26.1 0.7 copy-start.1
  29.7 12.3 %collective-permute-start.1 = (bf16[512,256]{1,0:T(8,128)(2,1)}, bf16[512,256]{1,0:T(8,128)(2,1)S(1)}, u32[]{:S(2)}, u32[]{:S(2)}) collective-permute-start(bf16[512,256]{1,0:T(8,128)(2,1)} %carry_and_gate.1), channel_id=1, source_target_pairs={{0,1},{1,2},{2,3},{3,4},{4,5},{5,6},{6,7},{7,8},{8,9},{9,10},{10,1... | collective-permute-start | bytes 786440 | tf_op jit(solution)/shard_map/ppermute | solution.py:236
  38.4 8.5 %collective-permute-start.3 = (bf16[512,256]{1,0:T(8,128)(2,1)}, bf16[512,256]{1,0:T(8,128)(2,1)S(1)}, u32[]{:S(2)}, u32[]{:S(2)}) collective-permute-start(bf16[512,256]{1,0:T(8,128)(2,1)} %carry_and_gate.1), channel_id=1, source_target_pairs={{16,1},{17,2},{18,3},{19,4},{20,5},{21,6},{22,7},{23,8},{24,9},{25... | collective-permute-start | bytes 786440 | tf_op jit(solution)/shard_map/ppermute | solution.py:236
  42.0 8.5 %collective-permute-start.2 = (bf16[512,256]{1,0:T(8,128)(2,1)S(1)}, bf16[512,256]{1,0:T(8,128)(2,1)S(1)}, u32[]{:S(2)}, u32[]{:S(2)}) collective-permute-start(bf16[512,256]{1,0:T(8,128)(2,1)S(1)} %collective-permute-done.1), channel_id=1, source_target_pairs={{0,1},{1,2},{2,3},{3,4},{4,5},{5,6},{6,7},{7,8},{8,9},{9,10},{10,1... | collective-permute-start | bytes 786440 | tf_op jit(solution)/shard_map/ppermute | solution.py:236
  47.0 8.3 %collective-permute-start.5 = (bf16[512,256]{1,0:T(8,128)(2,1)S(1)}, bf16[512,256]{1,0:T(8,128)(2,1)S(1)}, u32[]{:S(2)}, u32[]{:S(2)}) collective-permute-start(bf16[512,256]{1,0:T(8,128)(2,1)S(1)} %collective-permute-done.3), channel_id=1, source_target_pairs={{0,1},{1,2},{2,3},{3,4},{4,5},{5,6},{6,7},{7,8},{8,9},{9,10},{10,1... | collective-permute-start | bytes 786440 | tf_op jit(solution)/shard_map/ppermute | solution.py:236
  50.5 9.4 %collective-permute-start.4 = (bf16[512,256]{1,0:T(8,128)(2,1)S(1)}, bf16[512,256]{1,0:T(8,128)(2,1)S(1)}, u32[]{:S(2)}, u32[]{:S(2)}) collective-permute-start(bf16[512,256]{1,0:T(8,128)(2,1)S(1)} %collective-permute-done.2), channel_id=1, source_target_pairs={{0,1},{1,2},{2,3},{3,4},{4,5},{5,6},{6,7},{7,8},{8,9},{9,10},{10,1... | collective-permute-start | bytes 786440 | tf_op jit(solution)/shard_map/ppermute | solution.py:236
  55.3 8.3 %collective-permute-start.7 = (bf16[512,256]{1,0:T(8,128)(2,1)S(1)}, bf16[512,256]{1,0:T(8,128)(2,1)S(1)}, u32[]{:S(2)}, u32[]{:S(2)}) collective-permute-start(bf16[512,256]{1,0:T(8,128)(2,1)S(1)} %collective-permute-done.5), channel_id=1, source_target_pairs={{0,1},{1,2},{2,3},{3,4},{4,5},{5,6},{6,7},{7,8},{8,9},{9,10},{10,1... | collective-permute-start | bytes 786440 | tf_op jit(solution)/shard_map/ppermute | solution.py:236
  59.9 7.4 %collective-permute-start.6 = (bf16[512,256]{1,0:T(8,128)(2,1)S(1)}, bf16[512,256]{1,0:T(8,128)(2,1)S(1)}, u32[]{:S(2)}, u32[]{:S(2)}) collective-permute-start(bf16[512,256]{1,0:T(8,128)(2,1)S(1)} %collective-permute-done.4), channel_id=1, source_target_pairs={{0,1},{1,2},{2,3},{3,4},{4,5},{5,6},{6,7},{7,8},{8,9},{9,10},{10,1... | collective-permute-start | bytes 786440 | tf_op jit(solution)/shard_map/ppermute | solution.py:236
  63.6 8.3 %collective-permute-start.9 = (bf16[512,256]{1,0:T(8,128)(2,1)S(1)}, bf16[512,256]{1,0:T(8,128)(2,1)S(1)}, u32[]{:S(2)}, u32[]{:S(2)}) collective-permute-start(bf16[512,256]{1,0:T(8,128)(2,1)S(1)} %collective-permute-done.7), channel_id=1, source_target_pairs={{0,1},{1,2},{2,3},{3,4},{4,5},{5,6},{6,7},{7,8},{8,9},{9,10},{10,1... | collective-permute-start | bytes 786440 | tf_op jit(solution)/shard_map/ppermute | solution.py:236
  67.3 8.3 %collective-permute-start.8 = (bf16[512,256]{1,0:T(8,128)(2,1)S(1)}, bf16[512,256]{1,0:T(8,128)(2,1)S(1)}, u32[]{:S(2)}, u32[]{:S(2)}) collective-permute-start(bf16[512,256]{1,0:T(8,128)(2,1)S(1)} %collective-permute-done.6), channel_id=1, source_target_pairs={{0,1},{1,2},{2,3},{3,4},{4,5},{5,6},{6,7},{7,8},{8,9},{9,10},{10,1... | collective-permute-start | bytes 786440 | tf_op jit(solution)/shard_map/ppermute | solution.py:236
  71.9 8.3 %collective-permute-start.11 = (bf16[512,256]{1,0:T(8,128)(2,1)S(1)}, bf16[512,256]{1,0:T(8,128)(2,1)S(1)}, u32[]{:S(2)}, u32[]{:S(2)}) collective-permute-start(bf16[512,256]{1,0:T(8,128)(2,1)S(1)} %collective-permute-done.9), channel_id=1, source_target_pairs={{0,1},{1,2},{2,3},{3,4},{4,5},{5,6},{6,7},{7,8},{8,9},{9,10},{10,1... | collective-permute-start | bytes 786440 | tf_op jit(solution)/shard_map/ppermute | solution.py:236
  75.6 8.3 %collective-permute-start.10 = (bf16[512,256]{1,0:T(8,128)(2,1)S(1)}, bf16[512,256]{1,0:T(8,128)(2,1)S(1)}, u32[]{:S(2)}, u32[]{:S(2)}) collective-permute-start(bf16[512,256]{1,0:T(8,128)(2,1)S(1)} %collective-permute-done.8), channel_id=1, source_target_pairs={{0,1},{1,2},{2,3},{3,4},{4,5},{5,6},{6,7},{7,8},{8,9},{9,10},{10,1... | collective-permute-start | bytes 786440 | tf_op jit(solution)/shard_map/ppermute | solution.py:236
  80.2 8.3 %collective-permute-start.13 = (bf16[512,256]{1,0:T(8,128)(2,1)S(1)}, bf16[512,256]{1,0:T(8,128)(2,1)S(1)}, u32[]{:S(2)}, u32[]{:S(2)}) collective-permute-start(bf16[512,256]{1,0:T(8,128)(2,1)S(1)} %collective-permute-done.11), channel_id=1, source_target_pairs={{0,1},{1,2},{2,3},{3,4},{4,5},{5,6},{6,7},{7,8},{8,9},{9,10},{10,1... | collective-permute-start | bytes 786440 | tf_op jit(solution)/shard_map/ppermute | solution.py:236
  83.9 12.0 %collective-permute-start.12 = (bf16[512,256]{1,0:T(8,128)(2,1)S(1)}, bf16[512,256]{1,0:T(8,128)(2,1)S(1)}, u32[]{:S(2)}, u32[]{:S(2)}) collective-permute-start(bf16[512,256]{1,0:T(8,128)(2,1)S(1)} %collective-permute-done.10), channel_id=1, source_target_pairs={{0,1},{1,2},{2,3},{3,4},{4,5},{5,6},{6,7},{7,8},{8,9},{9,10},{10,1... | collective-permute-start | bytes 786440 | tf_op jit(solution)/shard_map/ppermute | solution.py:236
  88.6 7.4 %collective-permute-start.17 = (bf16[512,256]{1,0:T(8,128)(2,1)S(1)}, bf16[512,256]{1,0:T(8,128)(2,1)S(1)}, u32[]{:S(2)}, u32[]{:S(2)}) collective-permute-start(bf16[512,256]{1,0:T(8,128)(2,1)S(1)} %collective-permute-done.13), channel_id=1, source_target_pairs={{16,31},{17,16},{18,17},{19,18},{20,19},{21,20},{22,21},{23,22},{2... | collective-permute-start | bytes 786440 | tf_op jit(solution)/shard_map/ppermute | solution.py:236
  91.8 13.7 %collective-permute-start.14 = (bf16[512,256]{1,0:T(8,128)(2,1)S(1)}, bf16[512,256]{1,0:T(8,128)(2,1)S(1)}, u32[]{:S(2)}, u32[]{:S(2)}) collective-permute-start(bf16[512,256]{1,0:T(8,128)(2,1)S(1)} %collective-permute-done.13), channel_id=1, source_target_pairs={{0,17},{1,18},{2,19},{3,20},{4,21},{5,22},{6,23},{7,24},{8,25},{9,... | collective-permute-start | bytes 786440 | tf_op jit(solution)/shard_map/ppermute | solution.py:236
  93.8 14.4 %collective-permute-start.16 = (f32[512,256]{1,0:T(8,128)S(1)}, f32[512,256]{1,0:T(8,128)S(1)}, u32[]{:S(2)}, u32[]{:S(2)}) collective-permute-start(f32[512,256]{1,0:T(8,128)S(1)} %fusion.4), channel_id=1, source_target_pairs={{0,16},{1,17},{2,18},{3,19},{4,20},{5,21},{6,22},{7,23},{8,24},{9,... | collective-permute-start | bytes 1572872 | tf_op jit(solution)/shard_map/ppermute | solution.py:261
  96.0 9.8 %collective-permute-start.18 = (bf16[512,256]{1,0:T(8,128)(2,1)S(1)}, bf16[512,256]{1,0:T(8,128)(2,1)S(1)}, u32[]{:S(2)}, u32[]{:S(2)}) collective-permute-start(bf16[512,256]{1,0:T(8,128)(2,1)S(1)} %collective-permute-done.17), channel_id=1, source_target_pairs={{16,31},{17,16},{18,17},{19,18},{20,19},{21,20},{22,21},{23,22},{2... | collective-permute-start | bytes 786440 | tf_op jit(solution)/shard_map/ppermute | solution.py:236
  100.1 7.9 %collective-permute-start.15 = (bf16[512,256]{1,0:T(8,128)(2,1)S(1)}, bf16[512,256]{1,0:T(8,128)(2,1)S(1)}, u32[]{:S(2)}, u32[]{:S(2)}) collective-permute-start(bf16[512,256]{1,0:T(8,128)(2,1)S(1)} %collective-permute-done.12), channel_id=1, source_target_pairs={{16,31},{17,16},{18,17},{19,18},{20,19},{21,20},{22,21},{23,22},{2... | collective-permute-start | bytes 786440 | tf_op jit(solution)/shard_map/ppermute | solution.py:236
  106.2 2.9 %collective-permute-start.19 = (f32[512,256]{1,0:T(8,128)S(1)}, f32[512,256]{1,0:T(8,128)S(1)}, u32[]{:S(2)}, u32[]{:S(2)}) collective-permute-start(f32[512,256]{1,0:T(8,128)S(1)} %fusion), channel_id=1, source_target_pairs={{16,0},{17,1},{18,2},{19,3},{20,4},{21,5},{22,6},{23,7},{24,8},{25... | collective-permute-start | bytes 1572872 | tf_op jit(solution)/shard_map/ppermute | solution.py:268

commit v3 on v2

--- a/solution.py
+++ b/solution.py
@@ -57,7 +57,7 @@
     return poles, lax.fori_loop(0, steps, step, (jnp.zeros((BLOCKS, LANES), F32),) * modes, unroll=8)
 
 
-def states_kernel(k_hbm, v_hbm, rates_hbm, total_ref, flat, k_ref, v_ref, rates_ref, sems):
+def states_kernel(k_hbm, v_hbm, rates_hbm, every_hbm, total_ref, flat, k_ref, v_ref, rates_ref, sems, sent):
     modes, width = rates_ref.shape
     rows = k_ref.shape[0]
     steps = rows // BLOCKS
@@ -71,19 +71,23 @@
         for m in range(modes):
             fade = jnp.exp(-spread(rates_ref, m, lanes) * (steps * (BLOCKS - 1 - block)))
             total_ref[m : m + 1, lanes] = jnp.sum(fade * held[m], axis=0, keepdims=True)
-
-
-def local_kernel(core_ref, k_hbm, v_hbm, q_hbm, rates_hbm, resid_hbm, skip_hbm, oth_hbm, out_hbm, flat, flat_q, k_ref, v_ref, q_ref, rates_ref, resid_ref, oth_ref, skip_ref, out_ref, sems):
+    copies = [pltpu.make_async_copy(total_ref, every_hbm.at[i], sent.at[i]) for i in range(every_hbm.shape[0])]
+    for copy in copies:
+        copy.start()
+    for copy in copies:
+        copy.wait()
+
+
+def local_kernel(k_hbm, v_hbm, q_hbm, rates_hbm, resid_hbm, skip_hbm, out_hbm, flat, flat_q, k_ref, v_ref, q_ref, rates_ref, resid_ref, skip_ref, out_ref, sems):
     modes, width = rates_ref.shape
     rows = q_ref.shape[0]
     steps = rows // BLOCKS
-    pairs = ((rates_hbm, rates_ref), (resid_hbm, resid_ref), (skip_hbm, skip_ref), (oth_hbm, oth_ref))
+    pairs = ((rates_hbm, rates_ref), (resid_hbm, resid_ref), (skip_hbm, skip_ref))
     for copy in fetch(pairs + ((k_hbm, k_ref), (v_hbm, v_ref), (q_hbm, q_ref)), sems):
         copy.wait()
     fill(flat, rows, mixed_in(k_ref, v_ref))
     fill(flat_q, rows, lambda at: q_ref[at, :].astype(F32))
     block = lax.broadcasted_iota(jnp.int32, (BLOCKS, LANES), 0)
-    second = (core_ref[0] > 0).astype(F32)
     for half in range(width // LANES):
         lanes = slice(half * LANES, (half + 1) * LANES)
         poles, held = block_ends(flat, rates_ref, half)
@@ -91,8 +95,7 @@
         for m in range(modes):
             rate = spread(rates_ref, m, lanes)
             weights.append(spread(resid_ref, m, lanes))
-            come = second * spread(oth_ref, m, lanes)
-            scan = jnp.where(block >= 1, pltpu.roll(held[m], 1, 0), come)
+            scan = jnp.where(block >= 1, pltpu.roll(held[m], 1, 0), 0.0)
             for shift in (1, 2, 4):
                 moved = jnp.where(block >= shift, pltpu.roll(scan, shift, 0), 0.0)
                 scan = scan + jnp.exp(-rate * float(steps * shift)) * moved
@@ -112,22 +115,20 @@
     copy.wait()
 
 
-def gate_kernel(core_ref, chip_ref, all_hbm, rates_hbm, resid_hbm, local_hbm, out_hbm, flat, all_ref, rates_ref, resid_ref, local_ref, out_ref, sems):
-    chips, modes, width = all_ref.shape
+def gate_kernel(at_ref, all_hbm, rates_hbm, resid_hbm, local_hbm, out_hbm, flat, all_ref, rates_ref, resid_ref, local_ref, out_ref, sems):
+    devices, modes, width = all_ref.shape
     steps = local_ref.shape[0]
     rows = out_ref.shape[0]
     small = fetch(((rates_hbm, rates_ref), (resid_hbm, resid_ref), (all_hbm, all_ref), (local_hbm, local_ref)), sems)
     large = small.pop()
     for copy in small:
         copy.wait()
-    chip, core = chip_ref[0], core_ref[0]
     block = lax.broadcasted_iota(jnp.int32, (BLOCKS, LANES), 0).astype(F32)
     rates = rates_ref[...]
-    fade = jnp.exp(-rates * float(2 * rows))
+    fade = jnp.exp(-rates * float(rows))
     before = jnp.zeros((modes, width), F32)
-    for c in range(chips - 1):
-        before = jnp.where(c < chip, fade * before + all_ref[c], before)
-    before = jnp.where(core == 0, before, jnp.exp(-rates * float(rows)) * before)
+    for d in range(devices - 1):
+        before = jnp.where(d < at_ref[0], fade * before + all_ref[d], before)
     before = before * resid_ref[...]
     sent = []
     for half in range(width // LANES):
@@ -178,16 +179,14 @@
     rows, width = k_branch.shape
     modes = decay_rates.shape[0]
     steps = rows // BLOCKS
-    chips = lax.axis_size("y") * lax.axis_size("x")
+    seq = ("y", "x", "core")
+    devices = lax.axis_size(seq)
     depth = lax.axis_size("ch")
     core, z = lax.axis_index("core"), lax.axis_index("ch")
-    chip = lax.axis_index("y") * lax.axis_size("x") + lax.axis_index("x")
-    core_at = core.reshape(1).astype(jnp.int32)
-    chip_at = chip.reshape(1).astype(jnp.int32)
+    position = lax.axis_index(seq).reshape(1).astype(jnp.int32)
     shape = lambda s, d=F32: jax.ShapeDtypeStruct(s, d)
     flat_shape = (width // LANES, rows, LANES)
     work = modes * rows * width
-    swap = lambda array: lax.ppermute(array, "core", [(0, 1), (1, 0)])
 
     flat_of = pltpu.VMEM(flat_shape, F32)
     half_of = pltpu.VMEM((rows, width), BF16)
@@ -195,40 +194,36 @@
     sems = lambda count: pltpu.SemaphoreType.DMA((count,))
 
     by_step = (steps, 2 * BLOCKS, width)
-    total = kernel_call(
+    every = kernel_call(
         states_kernel,
         "states",
         2 * work,
-        out_shape=shape((modes, width)),
+        out_shape=shape((devices, modes, width)),
         in_specs=[ANY] * 3,
-        out_specs=VMEM,
-        scratch_shapes=[flat_of, half_of, half_of, modal, sems(3)],
+        out_specs=ANY,
+        scratch_shapes=[modal, flat_of, half_of, half_of, modal, sems(3), sems(devices)],
     )(k_branch, v_branch, decay_rates)
-    total_oth = swap(total)
-    first = core == 0
-    every = jnp.exp(-decay_rates * float(rows)) * jnp.where(first, total, total_oth) + jnp.where(first, total_oth, total)
-    every = jnp.broadcast_to(every[None], (chips, modes, width))
-    every = lax.all_to_all(every, ("y", "x"), split_axis=0, concat_axis=0, tiled=True)
+    every = lax.all_to_all(every, seq, split_axis=0, concat_axis=0, tiled=True)
     local = kernel_call(
         local_kernel,
-        "chip_convolution",
+        "local_convolution",
         6 * work,
         out_shape=shape(by_step),
-        in_specs=[SMEM] + [ANY] * 6 + [ANY],
+        in_specs=[ANY] * 6,
         out_specs=ANY,
-        scratch_shapes=[flat_of, flat_of, half_of, half_of, half_of, modal, modal, modal]
+        scratch_shapes=[flat_of, flat_of, half_of, half_of, half_of, modal, modal]
         + [pltpu.VMEM((1, width), F32), pltpu.VMEM(by_step, F32), sems(8)],
-    )(core_at, k_branch, v_branch, q_branch, decay_rates, residues, skip_gain[None, :], total_oth)
+    )(k_branch, v_branch, q_branch, decay_rates, residues, skip_gain[None, :])
     own = kernel_call(
         gate_kernel,
         "carry_and_gate",
         2 * work,
         out_shape=shape((rows, width), BF16),
-        in_specs=[SMEM, SMEM] + [ANY] * 4,
+        in_specs=[SMEM] + [ANY] * 4,
         out_specs=ANY,
-        scratch_shapes=[flat_of, pltpu.VMEM((chips, modes, width), F32), modal, modal]
+        scratch_shapes=[flat_of, pltpu.VMEM((devices, modes, width), F32), modal, modal]
         + [pltpu.VMEM(by_step, F32), half_of, sems(4 + width // LANES)],
-    )(core_at, chip_at, every, decay_rates, residues, local)
+    )(position, every, decay_rates, residues, local)
 
     ring = [(c * depth + i, c * depth + (i + 1 - 2 * c) % depth) for c in range(2) for i in range(depth)]
     cross = [((1 - c) * depth + i, c * depth + (i + 1 - 2 * c) % depth) for c in range(2) for i in range(depth)]

time: 111 us -> 109 us (0.982)
    ppermute x1 -> x0, starting transfers between devices: 8.79 us -> none  [body(): swap = lambda array: lax.ppermute(array, 'core', [(0, 1), (1, 0)])]
    all_to_all x1, starting transfers between devices: 3.53 us -> 10.4 us  [body(): every = lax.all_to_all(every, seq, split_axis=0, concat_axis=0, tiled=True)]
    all_to_all x1, waiting for transfers between devices: 3.29 us -> 6.55 us  [body(): every = lax.all_to_all(every, seq, split_axis=0, concat_axis=0, tiled=True)]
    ppermute x17, waiting for transfers between devices: 5.89 us -> 4.73 us  [body(): hop = lambda array, pairs=ring: lax.ppermute(array, ('core', 'ch'), pairs)]
  transfers between devices with their start and end apart: 21 -> 20, of which waited for: 7 -> 5; matrix products, arithmetic and copies ran while one was open for 5% -> 5% of each run, Pallas kernels for 5% -> 5%
where the time goes in v3:
time: 109 us; the launch traced here: 108 us
  starting transfers between devices  78.2 us (72%)
  Pallas kernels  11.4 us (10%)
  waiting for transfers between devices  11.3 us (10%)
  matrix products  5.2 us (5%)
    ppermute x17, starting transfers between devices, body(): hop = lambda array, pairs=ring: lax.ppermute(array, ('core', 'ch'), pairs)  65.1 us
    all_to_all x1, starting transfers between devices, body(): every = lax.all_to_all(every, seq, split_axis=0, concat_axis=0, tiled=True)  10.4 us
    all_to_all x1, waiting for transfers between devices, body(): every = lax.all_to_all(every, seq, split_axis=0, concat_axis=0, tiled=True)  6.55 us
    dot_general x18, matrix products, project(): return jnp.dot(array, weight, preferred_element_type=F32)  5.2 us
    pallas_call x1, Pallas kernels, body(): kernel_call(local_kernel, 'local_convolution', 6 * work, out_shape=shape(...  5.09 us
    ppermute x17, waiting for transfers between devices, body(): hop = lambda array, pairs=ring: lax.ppermute(array, ('core', 'ch'), pairs)  4.73 us
    pallas_call x1, Pallas kernels, body(): kernel_call(states_kernel, 'states', 2 * work, out_shape=shape((devices,...  3.29 us
    pallas_call x1, Pallas kernels, body(): kernel_call(gate_kernel, 'carry_and_gate', 2 * work, out_shape=shape((row...  3.01 us
  transfers between devices with their start and end apart: 20, of which 5 were waited for; matrix products, arithmetic and copies ran while one was open for 5% of the time, Pallas kernels for 5%

profile of v3, /device:TPU:1, one launch (start us, length us, event | category | flops | bytes accessed | tf_op | source)
XLA Modules:
  0.0 108.2 jit_solution(3371822693330692257)
XLA Ops:
  0.0 0.0 copy-start
  0.0 3.3 %states.1 = f32[32,16,256]{2,1,0:T(8,128)} custom-call(bf16[512,256]{1,0:T(8,128)(2,1)} %k_hbm.3, bf16[512,256]{1,0:T(8,128)(2,1)} %v_hbm.3, f32[16,256]{1,0:T(8,128)} %rates_hbm.5), custom_call_target="tpu_custom_call" | custom-call | flops 4194304 | bytes 1048576 | tf_op jit(solution)/shard_map/states/pallas_call | solution.py:197
  3.3 10.4 %all-to-all-start = ((f32[32,16,256]{2,1,0:T(8,128)}), f32[32,16,256]{2,1,0:T(8,128)S(1)}, u32[]{:S(2)}, u32[]{:S(2)}) async-start(f32[32,16,256]{2,1,0:T(8,128)} %states.1), calls=%async_computation | async-start | bytes 1048576 | tf_op jit(solution)/shard_map/all_to_all | solution.py:206
  13.7 5.1 %local_convolution.1.local_hbm = f32[64,16,256]{2,1,0:T(8,128)} custom-call(bf16[512,256]{1,0:T(8,128)(2,1)} %k_hbm.3, bf16[512,256]{1,0:T(8,128)(2,1)} %v_hbm.3, bf16[512,256]{1,0:T(8,128)(2,1)} %q_hbm.1, f32[16,256]{1,0:T(8,128)} %rates_hbm.5, f32[16,256]{1,0:T(8,128)} %resid_hbm.3, f32[1,256]{1,0:T(1,128)} %bitcast.20), custom_call_target="tpu_custom_call" | custom-call | flops 12582912 | bytes 1048576 | tf_op jit(solution)/shard_map/local_convolution/pallas_call | solution.py:207
  18.8 6.6 %all-to-all-done.all_hbm = f32[32,16,256]{2,1,0:T(8,128)S(1)} async-done(((f32[32,16,256]{2,1,0:T(8,128)}), f32[32,16,256]{2,1,0:T(8,128)S(1)}, u32[]{:S(2)}, u32[]{:S(2)}) %all-to-all-start) | async-done | bytes 524320 | tf_op jit(solution)/shard_map/all_to_all | solution.py:206
  25.4 0.8 copy-done.1
  26.2 3.0 %carry_and_gate.1 = bf16[512,256]{1,0:T(8,128)(2,1)} custom-call(s32[1]{0:T(128)} %bitcast.at_ref, f32[32,16,256]{2,1,0:T(8,128)} %copy-done.1, f32[16,256]{1,0:T(8,128)} %rates_hbm.5, f32[16,256]{1,0:T(8,128)} %resid_hbm.3, f32[64,16,256]{2,1,0:T(8,128)} %local_convolution.1.local_hbm), custom_call_target="tpu_custom_call" | custom-call | flops 4194304 | bytes 1048576 | tf_op jit(solution)/shard_map/carry_and_gate/pallas_call | solution.py:217
  29.2 9.2 %collective-permute-start = (bf16[512,256]{1,0:T(8,128)(2,1)}, bf16[512,256]{1,0:T(8,128)(2,1)S(1)}, u32[]{:S(2)}, u32[]{:S(2)}) collective-permute-start(bf16[512,256]{1,0:T(8,128)(2,1)} %carry_and_gate.1), channel_id=1, source_target_pairs={{0,1},{1,2},{2,3},{3,4},{4,5},{5,6},{6,7},{7,8},{8,9},{9,10},{10,1... | collective-permute-start | bytes 786440 | tf_op jit(solution)/shard_map/ppermute | solution.py:231
  38.4 1.9 %collective-permute-start.2 = (bf16[512,256]{1,0:T(8,128)(2,1)}, bf16[512,256]{1,0:T(8,128)(2,1)S(1)}, u32[]{:S(2)}, u32[]{:S(2)}) collective-permute-start(bf16[512,256]{1,0:T(8,128)(2,1)} %carry_and_gate.1), channel_id=1, source_target_pairs={{16,1},{17,2},{18,3},{19,4},{20,5},{21,6},{22,7},{23,8},{24,9},{25... | collective-permute-start | bytes 786440 | tf_op jit(solution)/shard_map/ppermute | solution.py:231
  40.3 1.7 %collective-permute-done = bf16[512,256]{1,0:T(8,128)(2,1)S(1)} collective-permute-done((bf16[512,256]{1,0:T(8,128)(2,1)}, bf16[512,256]{1,0:T(8,128)(2,1)S(1)}, u32[]{:S(2)}, u32[]{:S(2)}) %collective-permute-start) | collective-permute-done | bytes 262176 | tf_op jit(solution)/shard_map/ppermute | solution.py:231
  42.0 4.9 %collective-permute-start.1 = (bf16[512,256]{1,0:T(8,128)(2,1)S(1)}, bf16[512,256]{1,0:T(8,128)(2,1)S(1)}, u32[]{:S(2)}, u32[]{:S(2)}) collective-permute-start(bf16[512,256]{1,0:T(8,128)(2,1)S(1)} %collective-permute-done), channel_id=1, source_target_pairs={{0,1},{1,2},{2,3},{3,4},{4,5},{5,6},{6,7},{7,8},{8,9},{9,10},{10,1... | collective-permute-start | bytes 786440 | tf_op jit(solution)/shard_map/ppermute | solution.py:231
  46.9 0.0 collective-permute-done.2
  46.9 3.2 %collective-permute-start.4 = (bf16[512,256]{1,0:T(8,128)(2,1)S(1)}, bf16[512,256]{1,0:T(8,128)(2,1)S(1)}, u32[]{:S(2)}, u32[]{:S(2)}) collective-permute-start(bf16[512,256]{1,0:T(8,128)(2,1)S(1)} %collective-permute-done.2), channel_id=1, source_target_pairs={{0,1},{1,2},{2,3},{3,4},{4,5},{5,6},{6,7},{7,8},{8,9},{9,10},{10,1... | collective-permute-start | bytes 786440 | tf_op jit(solution)/shard_map/ppermute | solution.py:231
  50.2 1.2 %fusion.13 = f32[512,256]{1,0:T(8,128)S(1)} fusion(bf16[512,256]{1,0:T(8,128)(2,1)} %carry_and_gate.1, bf16[4096,256]{1,0:T(8,128)(2,1)S(1)} %copy-done, s32[]{:T(128)S(6)} %select_n.38), kind=kOutput, calls=%fused_computation.19 | convolution fusion | flops 67108864 | bytes 917508 | tf_op jit(solution)/shard_map/dot_general | solution.py:236
  51.4 0.0 collective-permute-done.1
  51.4 3.8 %collective-permute-start.3 = (bf16[512,256]{1,0:T(8,128)(2,1)S(1)}, bf16[512,256]{1,0:T(8,128)(2,1)S(1)}, u32[]{:S(2)}, u32[]{:S(2)}) collective-permute-start(bf16[512,256]{1,0:T(8,128)(2,1)S(1)} %collective-permute-done.1), channel_id=1, source_target_pairs={{0,1},{1,2},{2,3},{3,4},{4,5},{5,6},{6,7},{7,8},{8,9},{9,10},{10,1... | collective-permute-start | bytes 786440 | tf_op jit(solution)/shard_map/ppermute | solution.py:231
  55.2 0.0 collective-permute-done.4
  55.3 3.2 %collective-permute-start.6 = (bf16[512,256]{1,0:T(8,128)(2,1)S(1)}, bf16[512,256]{1,0:T(8,128)(2,1)S(1)}, u32[]{:S(2)}, u32[]{:S(2)}) collective-permute-start(bf16[512,256]{1,0:T(8,128)(2,1)S(1)} %collective-permute-done.4), channel_id=1, source_target_pairs={{0,1},{1,2},{2,3},{3,4},{4,5},{5,6},{6,7},{7,8},{8,9},{9,10},{10,1... | collective-permute-start | bytes 786440 | tf_op jit(solution)/shard_map/ppermute | solution.py:231
  58.5 0.2 convolution_add_fusion.4
  58.7 0.2 fusion.37
  58.9 0.0 collective-permute-done.3
  58.9 4.6 %collective-permute-start.5 = (bf16[512,256]{1,0:T(8,128)(2,1)S(1)}, bf16[512,256]{1,0:T(8,128)(2,1)S(1)}, u32[]{:S(2)}, u32[]{:S(2)}) collective-permute-start(bf16[512,256]{1,0:T(8,128)(2,1)S(1)} %collective-permute-done.3), channel_id=1, source_target_pairs={{0,1},{1,2},{2,3},{3,4},{4,5},{5,6},{6,7},{7,8},{8,9},{9,10},{10,1... | collective-permute-start | bytes 786440 | tf_op jit(solution)/shard_map/ppermute | solution.py:231
  63.6 0.0 collective-permute-done.6
  63.6 3.2 %collective-permute-start.8 = (bf16[512,256]{1,0:T(8,128)(2,1)S(1)}, bf16[512,256]{1,0:T(8,128)(2,1)S(1)}, u32[]{:S(2)}, u32[]{:S(2)}) collective-permute-start(bf16[512,256]{1,0:T(8,128)(2,1)S(1)} %collective-permute-done.6), channel_id=1, source_target_pairs={{0,1},{1,2},{2,3},{3,4},{4,5},{5,6},{6,7},{7,8},{8,9},{9,10},{10,1... | collective-permute-start | bytes 786440 | tf_op jit(solution)/shard_map/ppermute | solution.py:231
  66.8 0.2 fusion.35
  67.0 0.2 fusion.33
  67.2 0.0 collective-permute-done.5
  67.2 4.6 %collective-permute-start.7 = (bf16[512,256]{1,0:T(8,128)(2,1)S(1)}, bf16[512,256]{1,0:T(8,128)(2,1)S(1)}, u32[]{:S(2)}, u32[]{:S(2)}) collective-permute-start(bf16[512,256]{1,0:T(8,128)(2,1)S(1)} %collective-permute-done.5), channel_id=1, source_target_pairs={{0,1},{1,2},{2,3},{3,4},{4,5},{5,6},{6,7},{7,8},{8,9},{9,10},{10,1... | collective-permute-start | bytes 786440 | tf_op jit(solution)/shard_map/ppermute | solution.py:231
  71.9 0.0 collective-permute-done.8
  71.9 3.2 %collective-permute-start.10 = (bf16[512,256]{1,0:T(8,128)(2,1)S(1)}, bf16[512,256]{1,0:T(8,128)(2,1)S(1)}, u32[]{:S(2)}, u32[]{:S(2)}) collective-permute-start(bf16[512,256]{1,0:T(8,128)(2,1)S(1)} %collective-permute-done.8), channel_id=1, source_target_pairs={{0,1},{1,2},{2,3},{3,4},{4,5},{5,6},{6,7},{7,8},{8,9},{9,10},{10,1... | collective-permute-start | bytes 786440 | tf_op jit(solution)/shard_map/ppermute | solution.py:231
  75.1 0.2 fusion.31
  75.3 0.2 fusion.29
  75.6 0.0 collective-permute-done.7
  75.6 4.6 %collective-permute-start.9 = (bf16[512,256]{1,0:T(8,128)(2,1)S(1)}, bf16[512,256]{1,0:T(8,128)(2,1)S(1)}, u32[]{:S(2)}, u32[]{:S(2)}) collective-permute-start(bf16[512,256]{1,0:T(8,128)(2,1)S(1)} %collective-permute-done.7), channel_id=1, source_target_pairs={{0,1},{1,2},{2,3},{3,4},{4,5},{5,6},{6,7},{7,8},{8,9},{9,10},{10,1... | collective-permute-start | bytes 786440 | tf_op jit(solution)/shard_map/ppermute | solution.py:231
  80.2 0.0 collective-permute-done.10
  80.2 3.2 %collective-permute-start.12 = (bf16[512,256]{1,0:T(8,128)(2,1)S(1)}, bf16[512,256]{1,0:T(8,128)(2,1)S(1)}, u32[]{:S(2)}, u32[]{:S(2)}) collective-permute-start(bf16[512,256]{1,0:T(8,128)(2,1)S(1)} %collective-permute-done.10), channel_id=1, source_target_pairs={{0,1},{1,2},{2,3},{3,4},{4,5},{5,6},{6,7},{7,8},{8,9},{9,10},{10,1... | collective-permute-start | bytes 786440 | tf_op jit(solution)/shard_map/ppermute | solution.py:231
  83.4 0.2 fusion.27
  83.6 0.2 fusion.25
  83.9 0.0 collective-permute-done.9
  83.9 4.6 %collective-permute-start.11 = (bf16[512,256]{1,0:T(8,128)(2,1)S(1)}, bf16[512,256]{1,0:T(8,128)(2,1)S(1)}, u32[]{:S(2)}, u32[]{:S(2)}) collective-permute-start(bf16[512,256]{1,0:T(8,128)(2,1)S(1)} %collective-permute-done.9), channel_id=1, source_target_pairs={{0,1},{1,2},{2,3},{3,4},{4,5},{5,6},{6,7},{7,8},{8,9},{9,10},{10,1... | collective-permute-start | bytes 786440 | tf_op jit(solution)/shard_map/ppermute | solution.py:231
  88.5 0.0 collective-permute-done.12
  88.5 3.2 %collective-permute-start.16 = (bf16[512,256]{1,0:T(8,128)(2,1)S(1)}, bf16[512,256]{1,0:T(8,128)(2,1)S(1)}, u32[]{:S(2)}, u32[]{:S(2)}) collective-permute-start(bf16[512,256]{1,0:T(8,128)(2,1)S(1)} %collective-permute-done.12), channel_id=1, source_target_pairs={{16,31},{17,16},{18,17},{19,18},{20,19},{21,20},{22,21},{23,22},{2... | collective-permute-start | bytes 786440 | tf_op jit(solution)/shard_map/ppermute | solution.py:231
  91.7 1.3 %collective-permute-start.13 = (bf16[512,256]{1,0:T(8,128)(2,1)S(1)}, bf16[512,256]{1,0:T(8,128)(2,1)S(1)}, u32[]{:S(2)}, u32[]{:S(2)}) collective-permute-start(bf16[512,256]{1,0:T(8,128)(2,1)S(1)} %collective-permute-done.12), channel_id=1, source_target_pairs={{0,17},{1,18},{2,19},{3,20},{4,21},{5,22},{6,23},{7,24},{8,25},{9,... | collective-permute-start | bytes 786440 | tf_op jit(solution)/shard_map/ppermute | solution.py:231
  93.0 0.2 fusion.21
  93.3 0.3 fusion.4
  93.5 0.2 fusion.23
  93.8 1.3 %collective-permute-start.15 = (f32[512,256]{1,0:T(8,128)S(1)}, f32[512,256]{1,0:T(8,128)S(1)}, u32[]{:S(2)}, u32[]{:S(2)}) collective-permute-start(f32[512,256]{1,0:T(8,128)S(1)} %fusion.4), channel_id=1, source_target_pairs={{0,16},{1,17},{2,18},{3,19},{4,20},{5,21},{6,22},{7,23},{8,24},{9,... | collective-permute-start | bytes 1572872 | tf_op jit(solution)/shard_map/ppermute | solution.py:256
  95.1 0.6 collective-permute-done.16
  95.6 0.0 collective-permute-done.11
  95.6 4.4 %collective-permute-start.17 = (bf16[512,256]{1,0:T(8,128)(2,1)S(1)}, bf16[512,256]{1,0:T(8,128)(2,1)S(1)}, u32[]{:S(2)}, u32[]{:S(2)}) collective-permute-start(bf16[512,256]{1,0:T(8,128)(2,1)S(1)} %collective-permute-done.16), channel_id=1, source_target_pairs={{16,31},{17,16},{18,17},{19,18},{20,19},{21,20},{22,21},{23,22},{2... | collective-permute-start | bytes 786440 | tf_op jit(solution)/shard_map/ppermute | solution.py:231
  100.0 1.9 %collective-permute-start.14 = (bf16[512,256]{1,0:T(8,128)(2,1)S(1)}, bf16[512,256]{1,0:T(8,128)(2,1)S(1)}, u32[]{:S(2)}, u32[]{:S(2)}) collective-permute-start(bf16[512,256]{1,0:T(8,128)(2,1)S(1)} %collective-permute-done.11), channel_id=1, source_target_pairs={{16,31},{17,16},{18,17},{19,18},{20,19},{21,20},{22,21},{23,22},{2... | collective-permute-start | bytes 786440 | tf_op jit(solution)/shard_map/ppermute | solution.py:231
  102.0 0.2 fusion.19
  102.2 1.1 %collective-permute-done.13 = bf16[512,256]{1,0:T(8,128)(2,1)S(1)} collective-permute-done((bf16[512,256]{1,0:T(8,128)(2,1)S(1)}, bf16[512,256]{1,0:T(8,128)(2,1)S(1)}, u32[]{:S(2)}, u32[]{:S(2)}) %collective-permute-start.13) | collective-permute-done | bytes 262176 | tf_op jit(solution)/shard_map/ppermute | solution.py:231
  103.3 0.2 fusion.11
  103.5 0.0 collective-permute-done.17
  103.6 0.2 fusion.15
  103.8 0.3 fusion
  104.0 1.4 %collective-permute-start.18 = (f32[512,256]{1,0:T(8,128)S(1)}, f32[512,256]{1,0:T(8,128)S(1)}, u32[]{:S(2)}, u32[]{:S(2)}) collective-permute-start(f32[512,256]{1,0:T(8,128)S(1)} %fusion), channel_id=1, source_target_pairs={{16,0},{17,1},{18,2},{19,3},{20,4},{21,5},{22,6},{23,7},{24,8},{25... | collective-permute-start | bytes 1572872 | tf_op jit(solution)/shard_map/ppermute | solution.py:263
  105.5 0.3 fusion.10
  105.8 1.4 %collective-permute-done.14 = bf16[512,256]{1,0:T(8,128)(2,1)S(1)} collective-permute-done((bf16[512,256]{1,0:T(8,128)(2,1)S(1)}, bf16[512,256]{1,0:T(8,128)(2,1)S(1)}, u32[]{:S(2)}, u32[]{:S(2)}) %collective-permute-start.14) | collective-permute-done | bytes 262176 | tf_op jit(solution)/shard_map/ppermute | solution.py:231
  107.2 0.2 convolution_add_fusion.2
  107.4 0.0 collective-permute-done.15
  107.4 0.0 collective-permute-done.18
  107.4 0.8 add_convert_fusion
  (2 shorter events, 0.0 us)
Async XLA Ops:
  0.0 50.2 %copy-start = (bf16[4096,256]{1,0:T(8,128)(2,1)S(1)}, bf16[4096,256]{1,0:T(8,128)(2,1)}, u32[]{:S(2)}) copy-start(bf16[4096,256]{1,0:T(8,128)(2,1)} %param.13) | copy-start | bytes 6291460
  3.3 22.1 %all-to-all-start = ((f32[32,16,256]{2,1,0:T(8,128)}), f32[32,16,256]{2,1,0:T(8,128)S(1)}, u32[]{:S(2)}, u32[]{:S(2)}) async-start(f32[32,16,256]{2,1,0:T(8,128)} %states.1), calls=%async_computation | async-start | bytes 1048576 | tf_op jit(solution)/shard_map/all_to_all | solution.py:206
  25.4 0.8 copy-start.1
  29.2 12.8 %collective-permute-start = (bf16[512,256]{1,0:T(8,128)(2,1)}, bf16[512,256]{1,0:T(8,128)(2,1)S(1)}, u32[]{:S(2)}, u32[]{:S(2)}) collective-permute-start(bf16[512,256]{1,0:T(8,128)(2,1)} %carry_and_gate.1), channel_id=1, source_target_pairs={{0,1},{1,2},{2,3},{3,4},{4,5},{5,6},{6,7},{7,8},{8,9},{9,10},{10,1... | collective-permute-start | bytes 786440 | tf_op jit(solution)/shard_map/ppermute | solution.py:231
  38.4 8.5 %collective-permute-start.2 = (bf16[512,256]{1,0:T(8,128)(2,1)}, bf16[512,256]{1,0:T(8,128)(2,1)S(1)}, u32[]{:S(2)}, u32[]{:S(2)}) collective-permute-start(bf16[512,256]{1,0:T(8,128)(2,1)} %carry_and_gate.1), channel_id=1, source_target_pairs={{16,1},{17,2},{18,3},{19,4},{20,5},{21,6},{22,7},{23,8},{24,9},{25... | collective-permute-start | bytes 786440 | tf_op jit(solution)/shard_map/ppermute | solution.py:231
  42.0 9.4 %collective-permute-start.1 = (bf16[512,256]{1,0:T(8,128)(2,1)S(1)}, bf16[512,256]{1,0:T(8,128)(2,1)S(1)}, u32[]{:S(2)}, u32[]{:S(2)}) collective-permute-start(bf16[512,256]{1,0:T(8,128)(2,1)S(1)} %collective-permute-done), channel_id=1, source_target_pairs={{0,1},{1,2},{2,3},{3,4},{4,5},{5,6},{6,7},{7,8},{8,9},{9,10},{10,1... | collective-permute-start | bytes 786440 | tf_op jit(solution)/shard_map/ppermute | solution.py:231
  46.9 8.3 %collective-permute-start.4 = (bf16[512,256]{1,0:T(8,128)(2,1)S(1)}, bf16[512,256]{1,0:T(8,128)(2,1)S(1)}, u32[]{:S(2)}, u32[]{:S(2)}) collective-permute-start(bf16[512,256]{1,0:T(8,128)(2,1)S(1)} %collective-permute-done.2), channel_id=1, source_target_pairs={{0,1},{1,2},{2,3},{3,4},{4,5},{5,6},{6,7},{7,8},{8,9},{9,10},{10,1... | collective-permute-start | bytes 786440 | tf_op jit(solution)/shard_map/ppermute | solution.py:231
  51.4 7.5 %collective-permute-start.3 = (bf16[512,256]{1,0:T(8,128)(2,1)S(1)}, bf16[512,256]{1,0:T(8,128)(2,1)S(1)}, u32[]{:S(2)}, u32[]{:S(2)}) collective-permute-start(bf16[512,256]{1,0:T(8,128)(2,1)S(1)} %collective-permute-done.1), channel_id=1, source_target_pairs={{0,1},{1,2},{2,3},{3,4},{4,5},{5,6},{6,7},{7,8},{8,9},{9,10},{10,1... | collective-permute-start | bytes 786440 | tf_op jit(solution)/shard_map/ppermute | solution.py:231
  55.3 8.3 %collective-permute-start.6 = (bf16[512,256]{1,0:T(8,128)(2,1)S(1)}, bf16[512,256]{1,0:T(8,128)(2,1)S(1)}, u32[]{:S(2)}, u32[]{:S(2)}) collective-permute-start(bf16[512,256]{1,0:T(8,128)(2,1)S(1)} %collective-permute-done.4), channel_id=1, source_target_pairs={{0,1},{1,2},{2,3},{3,4},{4,5},{5,6},{6,7},{7,8},{8,9},{9,10},{10,1... | collective-permute-start | bytes 786440 | tf_op jit(solution)/shard_map/ppermute | solution.py:231
  58.9 8.3 %collective-permute-start.5 = (bf16[512,256]{1,0:T(8,128)(2,1)S(1)}, bf16[512,256]{1,0:T(8,128)(2,1)S(1)}, u32[]{:S(2)}, u32[]{:S(2)}) collective-permute-start(bf16[512,256]{1,0:T(8,128)(2,1)S(1)} %collective-permute-done.3), channel_id=1, source_target_pairs={{0,1},{1,2},{2,3},{3,4},{4,5},{5,6},{6,7},{7,8},{8,9},{9,10},{10,1... | collective-permute-start | bytes 786440 | tf_op jit(solution)/shard_map/ppermute | solution.py:231
  63.6 8.3 %collective-permute-start.8 = (bf16[512,256]{1,0:T(8,128)(2,1)S(1)}, bf16[512,256]{1,0:T(8,128)(2,1)S(1)}, u32[]{:S(2)}, u32[]{:S(2)}) collective-permute-start(bf16[512,256]{1,0:T(8,128)(2,1)S(1)} %collective-permute-done.6), channel_id=1, source_target_pairs={{0,1},{1,2},{2,3},{3,4},{4,5},{5,6},{6,7},{7,8},{8,9},{9,10},{10,1... | collective-permute-start | bytes 786440 | tf_op jit(solution)/shard_map/ppermute | solution.py:231
  67.2 8.3 %collective-permute-start.7 = (bf16[512,256]{1,0:T(8,128)(2,1)S(1)}, bf16[512,256]{1,0:T(8,128)(2,1)S(1)}, u32[]{:S(2)}, u32[]{:S(2)}) collective-permute-start(bf16[512,256]{1,0:T(8,128)(2,1)S(1)} %collective-permute-done.5), channel_id=1, source_target_pairs={{0,1},{1,2},{2,3},{3,4},{4,5},{5,6},{6,7},{7,8},{8,9},{9,10},{10,1... | collective-permute-start | bytes 786440 | tf_op jit(solution)/shard_map/ppermute | solution.py:231
  71.9 8.3 %collective-permute-start.10 = (bf16[512,256]{1,0:T(8,128)(2,1)S(1)}, bf16[512,256]{1,0:T(8,128)(2,1)S(1)}, u32[]{:S(2)}, u32[]{:S(2)}) collective-permute-start(bf16[512,256]{1,0:T(8,128)(2,1)S(1)} %collective-permute-done.8), channel_id=1, source_target_pairs={{0,1},{1,2},{2,3},{3,4},{4,5},{5,6},{6,7},{7,8},{8,9},{9,10},{10,1... | collective-permute-start | bytes 786440 | tf_op jit(solution)/shard_map/ppermute | solution.py:231
  75.6 8.3 %collective-permute-start.9 = (bf16[512,256]{1,0:T(8,128)(2,1)S(1)}, bf16[512,256]{1,0:T(8,128)(2,1)S(1)}, u32[]{:S(2)}, u32[]{:S(2)}) collective-permute-start(bf16[512,256]{1,0:T(8,128)(2,1)S(1)} %collective-permute-done.7), channel_id=1, source_target_pairs={{0,1},{1,2},{2,3},{3,4},{4,5},{5,6},{6,7},{7,8},{8,9},{9,10},{10,1... | collective-permute-start | bytes 786440 | tf_op jit(solution)/shard_map/ppermute | solution.py:231
  80.2 8.3 %collective-permute-start.12 = (bf16[512,256]{1,0:T(8,128)(2,1)S(1)}, bf16[512,256]{1,0:T(8,128)(2,1)S(1)}, u32[]{:S(2)}, u32[]{:S(2)}) collective-permute-start(bf16[512,256]{1,0:T(8,128)(2,1)S(1)} %collective-permute-done.10), channel_id=1, source_target_pairs={{0,1},{1,2},{2,3},{3,4},{4,5},{5,6},{6,7},{7,8},{8,9},{9,10},{10,1... | collective-permute-start | bytes 786440 | tf_op jit(solution)/shard_map/ppermute | solution.py:231
  83.9 11.8 %collective-permute-start.11 = (bf16[512,256]{1,0:T(8,128)(2,1)S(1)}, bf16[512,256]{1,0:T(8,128)(2,1)S(1)}, u32[]{:S(2)}, u32[]{:S(2)}) collective-permute-start(bf16[512,256]{1,0:T(8,128)(2,1)S(1)} %collective-permute-done.9), channel_id=1, source_target_pairs={{0,1},{1,2},{2,3},{3,4},{4,5},{5,6},{6,7},{7,8},{8,9},{9,10},{10,1... | collective-permute-start | bytes 786440 | tf_op jit(solution)/shard_map/ppermute | solution.py:231
  88.5 7.1 %collective-permute-start.16 = (bf16[512,256]{1,0:T(8,128)(2,1)S(1)}, bf16[512,256]{1,0:T(8,128)(2,1)S(1)}, u32[]{:S(2)}, u32[]{:S(2)}) collective-permute-start(bf16[512,256]{1,0:T(8,128)(2,1)S(1)} %collective-permute-done.12), channel_id=1, source_target_pairs={{16,31},{17,16},{18,17},{19,18},{20,19},{21,20},{22,21},{23,22},{2... | collective-permute-start | bytes 786440 | tf_op jit(solution)/shard_map/ppermute | solution.py:231
  91.7 11.6 %collective-permute-start.13 = (bf16[512,256]{1,0:T(8,128)(2,1)S(1)}, bf16[512,256]{1,0:T(8,128)(2,1)S(1)}, u32[]{:S(2)}, u32[]{:S(2)}) collective-permute-start(bf16[512,256]{1,0:T(8,128)(2,1)S(1)} %collective-permute-done.12), channel_id=1, source_target_pairs={{0,17},{1,18},{2,19},{3,20},{4,21},{5,22},{6,23},{7,24},{8,25},{9,... | collective-permute-start | bytes 786440 | tf_op jit(solution)/shard_map/ppermute | solution.py:231
  93.8 13.6 %collective-permute-start.15 = (f32[512,256]{1,0:T(8,128)S(1)}, f32[512,256]{1,0:T(8,128)S(1)}, u32[]{:S(2)}, u32[]{:S(2)}) collective-permute-start(f32[512,256]{1,0:T(8,128)S(1)} %fusion.4), channel_id=1, source_target_pairs={{0,16},{1,17},{2,18},{3,19},{4,20},{5,21},{6,22},{7,23},{8,24},{9,... | collective-permute-start | bytes 1572872 | tf_op jit(solution)/shard_map/ppermute | solution.py:256
  95.6 7.9 %collective-permute-start.17 = (bf16[512,256]{1,0:T(8,128)(2,1)S(1)}, bf16[512,256]{1,0:T(8,128)(2,1)S(1)}, u32[]{:S(2)}, u32[]{:S(2)}) collective-permute-start(bf16[512,256]{1,0:T(8,128)(2,1)S(1)} %collective-permute-done.16), channel_id=1, source_target_pairs={{16,31},{17,16},{18,17},{19,18},{20,19},{21,20},{22,21},{23,22},{2... | collective-permute-start | bytes 786440 | tf_op jit(solution)/shard_map/ppermute | solution.py:231
  100.0 7.1 %collective-permute-start.14 = (bf16[512,256]{1,0:T(8,128)(2,1)S(1)}, bf16[512,256]{1,0:T(8,128)(2,1)S(1)}, u32[]{:S(2)}, u32[]{:S(2)}) collective-permute-start(bf16[512,256]{1,0:T(8,128)(2,1)S(1)} %collective-permute-done.11), channel_id=1, source_target_pairs={{16,31},{17,16},{18,17},{19,18},{20,19},{21,20},{22,21},{23,22},{2... | collective-permute-start | bytes 786440 | tf_op jit(solution)/shard_map/ppermute | solution.py:231
  104.0 3.4 %collective-permute-start.18 = (f32[512,256]{1,0:T(8,128)S(1)}, f32[512,256]{1,0:T(8,128)S(1)}, u32[]{:S(2)}, u32[]{:S(2)}) collective-permute-start(f32[512,256]{1,0:T(8,128)S(1)} %fusion), channel_id=1, source_target_pairs={{16,0},{17,1},{18,2},{19,3},{20,4},{21,5},{22,6},{23,7},{24,8},{25... | collective-permute-start | bytes 1572872 | tf_op jit(solution)/shard_map/ppermute | solution.py:263

commit v4 on v3

--- a/solution.py
+++ b/solution.py
@@ -78,7 +78,7 @@
         copy.wait()
 
 
-def local_kernel(k_hbm, v_hbm, q_hbm, rates_hbm, resid_hbm, skip_hbm, out_hbm, flat, flat_q, k_ref, v_ref, q_ref, rates_ref, resid_ref, skip_ref, out_ref, sems):
+def local_kernel(k_hbm, v_hbm, q_hbm, rates_hbm, resid_hbm, skip_hbm, out_ref, flat, flat_q, k_ref, v_ref, q_ref, rates_ref, resid_ref, skip_ref, sems):
     modes, width = rates_ref.shape
     rows = q_ref.shape[0]
     steps = rows // BLOCKS
@@ -110,19 +110,12 @@
             return held
 
         lax.fori_loop(0, steps, step, tuple(first), unroll=4)
-    copy = pltpu.make_async_copy(out_ref, out_hbm, sems.at[7])
-    copy.start()
-    copy.wait()
-
-
-def gate_kernel(at_ref, all_hbm, rates_hbm, resid_hbm, local_hbm, out_hbm, flat, all_ref, rates_ref, resid_ref, local_ref, out_ref, sems):
+
+
+def gate_kernel(at_ref, all_ref, rates_ref, resid_ref, local_ref, out_ref, flat):
     devices, modes, width = all_ref.shape
     steps = local_ref.shape[0]
     rows = out_ref.shape[0]
-    small = fetch(((rates_hbm, rates_ref), (resid_hbm, resid_ref), (all_hbm, all_ref), (local_hbm, local_ref)), sems)
-    large = small.pop()
-    for copy in small:
-        copy.wait()
     block = lax.broadcasted_iota(jnp.int32, (BLOCKS, LANES), 0).astype(F32)
     rates = rates_ref[...]
     fade = jnp.exp(-rates * float(rows))
@@ -130,7 +123,6 @@
     for d in range(devices - 1):
         before = jnp.where(d < at_ref[0], fade * before + all_ref[d], before)
     before = before * resid_ref[...]
-    sent = []
     for half in range(width // LANES):
         lanes = slice(half * LANES, (half + 1) * LANES)
         poles, first = [], []
@@ -139,8 +131,6 @@
             poles.append(jnp.exp(-rate))
             come = jnp.broadcast_to(before[m : m + 1, lanes], (BLOCKS, LANES))
             first.append(come * jnp.exp(-rate * (steps * block + 1.0)))
-        if half == 0:
-            large.wait()
 
         def step(j, held):
             conv = local_ref[j, 0:BLOCKS, lanes] + tree_sum(held)
@@ -155,21 +145,17 @@
             at = pl.ds(pl.multiple_of(i * piece, piece), piece)
             out_ref[at, lanes] = flat[half, at, :].astype(BF16)
 
-        sent.append(pltpu.make_async_copy(out_ref.at[:, lanes], out_hbm.at[:, lanes], sems.at[4 + half]))
-        sent[-1].start()
-    for copy in sent:
-        copy.wait()
-
 
 VMEM = pl.BlockSpec(memory_space=pltpu.VMEM)
 ANY = pl.BlockSpec(memory_space=pl.ANY)
 SMEM = pl.BlockSpec(memory_space=pltpu.SMEM)
 
 
-def kernel_call(kernel, name, cost, **kwargs):
+def kernel_call(kernel, name, cost, limit=None, **kwargs):
     return pl.pallas_call(
         kernel,
         name=name,
+        compiler_params=pltpu.CompilerParams(vmem_limit_bytes=limit),
         cost_estimate=pl.CostEstimate(flops=cost, bytes_accessed=1 << 20, transcendentals=0),
         **kwargs,
     )
@@ -208,21 +194,22 @@
         local_kernel,
         "local_convolution",
         6 * work,
+        limit=8 << 20,
         out_shape=shape(by_step),
         in_specs=[ANY] * 6,
-        out_specs=ANY,
+        out_specs=VMEM,
         scratch_shapes=[flat_of, flat_of, half_of, half_of, half_of, modal, modal]
-        + [pltpu.VMEM((1, width), F32), pltpu.VMEM(by_step, F32), sems(8)],
+        + [pltpu.VMEM((1, width), F32), sems(7)],
     )(k_branch, v_branch, q_branch, decay_rates, residues, skip_gain[None, :])
     own = kernel_call(
         gate_kernel,
         "carry_and_gate",
         2 * work,
+        limit=8 << 20,
         out_shape=shape((rows, width), BF16),
-        in_specs=[SMEM] + [ANY] * 4,
-        out_specs=ANY,
-        scratch_shapes=[flat_of, pltpu.VMEM((devices, modes, width), F32), modal, modal]
-        + [pltpu.VMEM(by_step, F32), half_of, sems(4 + width // LANES)],
+        in_specs=[SMEM] + [VMEM] * 4,
+        out_specs=VMEM,
+        scratch_shapes=[flat_of],
     )(position, every, decay_rates, residues, local)
 
     ring = [(c * depth + i, c * depth + (i + 1 - 2 * c) % depth) for c in range(2) for i in range(depth)]

time: 109 us -> 107 us (0.982)
  Pallas kernels: 11.4 us -> 8.35 us
  local copies, waits for them, and re-layouts: 0.8 us -> 1.91 us
  starting transfers between devices: 78.2 us -> 79.3 us
    pallas_call x2, Pallas kernels: 8.1 us -> 5.05 us  [the longest x1 3.03 us: body(): kernel_call(local_kernel, 'local_convolution', 6 * work, limit=8 << 20, o...]
    unnamed x4 -> x14, local copies, waits for them, and re-layouts: 0.8 us -> 1.91 us
  transfers between devices with their start and end apart: 20 -> 20, of which waited for: 5 -> 5; matrix products, arithmetic and copies ran while one was open for 5% -> 4% of each run, Pallas kernels for 5% -> 3%
where the time goes in v4:
time: 107 us; the launch traced here: 106 us
  starting transfers between devices  79.3 us (74%)
  waiting for transfers between devices  11.1 us (10%)
  Pallas kernels  8.35 us (8%)
  matrix products  4.27 us (4%)
  local copies, waits for them, and re-layouts  1.91 us (2%)
    ppermute x17, starting transfers between devices, body(): hop = lambda array, pairs=ring: lax.ppermute(array, ('core', 'ch'), pairs)  65.5 us
    all_to_all x1, starting transfers between devices, body(): every = lax.all_to_all(every, seq, split_axis=0, concat_axis=0, tiled=True)  11.1 us
    all_to_all x1, waiting for transfers between devices, body(): every = lax.all_to_all(every, seq, split_axis=0, concat_axis=0, tiled=True)  6.72 us
    ppermute x17, waiting for transfers between devices, body(): hop = lambda array, pairs=ring: lax.ppermute(array, ('core', 'ch'), pairs)  4.42 us
    dot_general x18, matrix products, project(): return jnp.dot(array, weight, preferred_element_type=F32)  4.27 us
    pallas_call x1, Pallas kernels, body(): kernel_call(states_kernel, 'states', 2 * work, out_shape=shape((devices,...  3.3 us
    pallas_call x1, Pallas kernels, body(): kernel_call(local_kernel, 'local_convolution', 6 * work, limit=8 << 20, o...  3.03 us
  transfers between devices with their start and end apart: 20, of which 5 were waited for; matrix products, arithmetic and copies ran while one was open for 4% of the time, Pallas kernels for 3%

profile of v4, /device:TPU:1, one launch (start us, length us, event | category | flops | bytes accessed | tf_op | source)
XLA Modules:
  0.0 106.3 jit_solution(17689000506393103260)
XLA Ops:
  0.0 3.3 %states.1 = f32[32,16,256]{2,1,0:T(8,128)} custom-call(bf16[512,256]{1,0:T(8,128)(2,1)} %k_hbm.3, bf16[512,256]{1,0:T(8,128)(2,1)} %v_hbm.3, f32[16,256]{1,0:T(8,128)} %rates_ref.1), custom_call_target="tpu_custom_call" | custom-call | flops 4194304 | bytes 1048576 | tf_op jit(solution)/shard_map/states/pallas_call | solution.py:183
  3.3 11.1 %all-to-all-start = ((f32[32,16,256]{2,1,0:T(8,128)}), f32[32,16,256]{2,1,0:T(8,128)}, u32[]{:S(2)}, u32[]{:S(2)}) async-start(f32[32,16,256]{2,1,0:T(8,128)} %states.1), calls=%async_computation | async-start | bytes 1048576 | tf_op jit(solution)/shard_map/all_to_all | solution.py:192
  14.5 0.0 copy-start.2
  14.5 0.9 copy-done.2
  15.4 0.9 copy-done.3
  16.4 3.0 %local_convolution.1.local_ref = f32[64,16,256]{2,1,0:T(8,128)S(1)} custom-call(bf16[512,256]{1,0:T(8,128)(2,1)S(1)} %copy-done.1, bf16[512,256]{1,0:T(8,128)(2,1)S(1)} %copy-done.2, bf16[512,256]{1,0:T(8,128)(2,1)S(1)} %copy-done.3, f32[16,256]{1,0:T(8,128)S(1)} %copy-done.4, f32[16,256]{1,0:T(8,128)S(1)} %copy-done.5, f32[1,256]{1,0:T(1,128)S(1)} %bitcast.20), custom_call_target="tpu_custom_call" | custom-call | flops 12582912 | bytes 1048576 | tf_op jit(solution)/shard_map/local_convolution/pallas_call | solution.py:193
  19.4 6.7 %all-to-all-done.all_ref = f32[32,16,256]{2,1,0:T(8,128)} async-done(((f32[32,16,256]{2,1,0:T(8,128)}), f32[32,16,256]{2,1,0:T(8,128)}, u32[]{:S(2)}, u32[]{:S(2)}) %all-to-all-start) | async-done | bytes 524320 | tf_op jit(solution)/shard_map/all_to_all | solution.py:192
  26.1 2.0 %carry_and_gate.1 = bf16[512,256]{1,0:T(8,128)(2,1)S(1)} custom-call(s32[1]{0:T(128)} %bitcast.at_ref, f32[32,16,256]{2,1,0:T(8,128)} %all-to-all-done.all_ref, f32[16,256]{1,0:T(8,128)S(1)} %copy-done.4, f32[16,256]{1,0:T(8,128)S(1)} %copy-done.5, f32[64,16,256]{2,1,0:T(8,128)S(1)} %local_convolution.1.local_ref), custom_call_target="tpu_custom_call" | custom-call | flops 4194304 | bytes 1048576 | tf_op jit(solution)/shard_map/carry_and_gate/pallas_call | solution.py:204
  28.2 8.6 %collective-permute-start = (bf16[512,256]{1,0:T(8,128)(2,1)S(1)}, bf16[512,256]{1,0:T(8,128)(2,1)S(1)}, u32[]{:S(2)}, u32[]{:S(2)}) collective-permute-start(bf16[512,256]{1,0:T(8,128)(2,1)S(1)} %carry_and_gate.1), channel_id=1, source_target_pairs={{0,1},{1,2},{2,3},{3,4},{4,5},{5,6},{6,7},{7,8},{8,9},{9,10},{10,1... | collective-permute-start | bytes 786440 | tf_op jit(solution)/shard_map/ppermute | solution.py:218
  36.8 1.9 %collective-permute-start.2 = (bf16[512,256]{1,0:T(8,128)(2,1)S(1)}, bf16[512,256]{1,0:T(8,128)(2,1)S(1)}, u32[]{:S(2)}, u32[]{:S(2)}) collective-permute-start(bf16[512,256]{1,0:T(8,128)(2,1)S(1)} %carry_and_gate.1), channel_id=1, source_target_pairs={{16,1},{17,2},{18,3},{19,4},{20,5},{21,6},{22,7},{23,8},{24,9},{25... | collective-permute-start | bytes 786440 | tf_op jit(solution)/shard_map/ppermute | solution.py:218
  38.7 1.4 %collective-permute-done = bf16[512,256]{1,0:T(8,128)(2,1)S(1)} collective-permute-done((bf16[512,256]{1,0:T(8,128)(2,1)S(1)}, bf16[512,256]{1,0:T(8,128)(2,1)S(1)}, u32[]{:S(2)}, u32[]{:S(2)}) %collective-permute-start) | collective-permute-done | bytes 262176 | tf_op jit(solution)/shard_map/ppermute | solution.py:218
  40.1 5.0 %collective-permute-start.1 = (bf16[512,256]{1,0:T(8,128)(2,1)S(1)}, bf16[512,256]{1,0:T(8,128)(2,1)S(1)}, u32[]{:S(2)}, u32[]{:S(2)}) collective-permute-start(bf16[512,256]{1,0:T(8,128)(2,1)S(1)} %collective-permute-done), channel_id=1, source_target_pairs={{0,1},{1,2},{2,3},{3,4},{4,5},{5,6},{6,7},{7,8},{8,9},{9,10},{10,1... | collective-permute-start | bytes 786440 | tf_op jit(solution)/shard_map/ppermute | solution.py:218
  45.1 0.0 collective-permute-done.2
  45.1 3.2 %collective-permute-start.4 = (bf16[512,256]{1,0:T(8,128)(2,1)S(1)}, bf16[512,256]{1,0:T(8,128)(2,1)S(1)}, u32[]{:S(2)}, u32[]{:S(2)}) collective-permute-start(bf16[512,256]{1,0:T(8,128)(2,1)S(1)} %collective-permute-done.2), channel_id=1, source_target_pairs={{0,1},{1,2},{2,3},{3,4},{4,5},{5,6},{6,7},{7,8},{8,9},{9,10},{10,1... | collective-permute-start | bytes 786440 | tf_op jit(solution)/shard_map/ppermute | solution.py:218
  48.4 0.2 fusion.13
  48.6 0.0 collective-permute-done.1
  48.6 4.8 %collective-permute-start.3 = (bf16[512,256]{1,0:T(8,128)(2,1)S(1)}, bf16[512,256]{1,0:T(8,128)(2,1)S(1)}, u32[]{:S(2)}, u32[]{:S(2)}) collective-permute-start(bf16[512,256]{1,0:T(8,128)(2,1)S(1)} %collective-permute-done.1), channel_id=1, source_target_pairs={{0,1},{1,2},{2,3},{3,4},{4,5},{5,6},{6,7},{7,8},{8,9},{9,10},{10,1... | collective-permute-start | bytes 786440 | tf_op jit(solution)/shard_map/ppermute | solution.py:218
  53.4 0.0 collective-permute-done.4
  53.4 3.2 %collective-permute-start.6 = (bf16[512,256]{1,0:T(8,128)(2,1)S(1)}, bf16[512,256]{1,0:T(8,128)(2,1)S(1)}, u32[]{:S(2)}, u32[]{:S(2)}) collective-permute-start(bf16[512,256]{1,0:T(8,128)(2,1)S(1)} %collective-permute-done.4), channel_id=1, source_target_pairs={{0,1},{1,2},{2,3},{3,4},{4,5},{5,6},{6,7},{7,8},{8,9},{9,10},{10,1... | collective-permute-start | bytes 786440 | tf_op jit(solution)/shard_map/ppermute | solution.py:218
  56.6 0.2 convolution_add_fusion.4
  56.9 0.2 fusion.37
  57.1 0.0 collective-permute-done.3
  57.1 4.6 %collective-permute-start.5 = (bf16[512,256]{1,0:T(8,128)(2,1)S(1)}, bf16[512,256]{1,0:T(8,128)(2,1)S(1)}, u32[]{:S(2)}, u32[]{:S(2)}) collective-permute-start(bf16[512,256]{1,0:T(8,128)(2,1)S(1)} %collective-permute-done.3), channel_id=1, source_target_pairs={{0,1},{1,2},{2,3},{3,4},{4,5},{5,6},{6,7},{7,8},{8,9},{9,10},{10,1... | collective-permute-start | bytes 786440 | tf_op jit(solution)/shard_map/ppermute | solution.py:218
  61.7 0.0 collective-permute-done.6
  61.7 3.2 %collective-permute-start.8 = (bf16[512,256]{1,0:T(8,128)(2,1)S(1)}, bf16[512,256]{1,0:T(8,128)(2,1)S(1)}, u32[]{:S(2)}, u32[]{:S(2)}) collective-permute-start(bf16[512,256]{1,0:T(8,128)(2,1)S(1)} %collective-permute-done.6), channel_id=1, source_target_pairs={{0,1},{1,2},{2,3},{3,4},{4,5},{5,6},{6,7},{7,8},{8,9},{9,10},{10,1... | collective-permute-start | bytes 786440 | tf_op jit(solution)/shard_map/ppermute | solution.py:218
  64.9 0.2 fusion.35
  65.2 0.2 fusion.33
  65.4 0.0 collective-permute-done.5
  65.4 4.6 %collective-permute-start.7 = (bf16[512,256]{1,0:T(8,128)(2,1)S(1)}, bf16[512,256]{1,0:T(8,128)(2,1)S(1)}, u32[]{:S(2)}, u32[]{:S(2)}) collective-permute-start(bf16[512,256]{1,0:T(8,128)(2,1)S(1)} %collective-permute-done.5), channel_id=1, source_target_pairs={{0,1},{1,2},{2,3},{3,4},{4,5},{5,6},{6,7},{7,8},{8,9},{9,10},{10,1... | collective-permute-start | bytes 786440 | tf_op jit(solution)/shard_map/ppermute | solution.py:218
  70.0 0.0 collective-permute-done.8
  70.0 3.2 %collective-permute-start.10 = (bf16[512,256]{1,0:T(8,128)(2,1)S(1)}, bf16[512,256]{1,0:T(8,128)(2,1)S(1)}, u32[]{:S(2)}, u32[]{:S(2)}) collective-permute-start(bf16[512,256]{1,0:T(8,128)(2,1)S(1)} %collective-permute-done.8), channel_id=1, source_target_pairs={{0,1},{1,2},{2,3},{3,4},{4,5},{5,6},{6,7},{7,8},{8,9},{9,10},{10,1... | collective-permute-start | bytes 786440 | tf_op jit(solution)/shard_map/ppermute | solution.py:218
  73.2 0.2 fusion.31
  73.5 0.2 fusion.29
  73.7 0.0 collective-permute-done.7
  73.7 4.6 %collective-permute-start.9 = (bf16[512,256]{1,0:T(8,128)(2,1)S(1)}, bf16[512,256]{1,0:T(8,128)(2,1)S(1)}, u32[]{:S(2)}, u32[]{:S(2)}) collective-permute-start(bf16[512,256]{1,0:T(8,128)(2,1)S(1)} %collective-permute-done.7), channel_id=1, source_target_pairs={{0,1},{1,2},{2,3},{3,4},{4,5},{5,6},{6,7},{7,8},{8,9},{9,10},{10,1... | collective-permute-start | bytes 786440 | tf_op jit(solution)/shard_map/ppermute | solution.py:218
  78.3 0.0 collective-permute-done.10
  78.3 3.2 %collective-permute-start.12 = (bf16[512,256]{1,0:T(8,128)(2,1)S(1)}, bf16[512,256]{1,0:T(8,128)(2,1)S(1)}, u32[]{:S(2)}, u32[]{:S(2)}) collective-permute-start(bf16[512,256]{1,0:T(8,128)(2,1)S(1)} %collective-permute-done.10), channel_id=1, source_target_pairs={{0,1},{1,2},{2,3},{3,4},{4,5},{5,6},{6,7},{7,8},{8,9},{9,10},{10,1... | collective-permute-start | bytes 786440 | tf_op jit(solution)/shard_map/ppermute | solution.py:218
  81.6 0.2 fusion.27
  81.8 0.2 fusion.25
  82.0 0.0 collective-permute-done.9
  82.0 4.6 %collective-permute-start.11 = (bf16[512,256]{1,0:T(8,128)(2,1)S(1)}, bf16[512,256]{1,0:T(8,128)(2,1)S(1)}, u32[]{:S(2)}, u32[]{:S(2)}) collective-permute-start(bf16[512,256]{1,0:T(8,128)(2,1)S(1)} %collective-permute-done.9), channel_id=1, source_target_pairs={{0,1},{1,2},{2,3},{3,4},{4,5},{5,6},{6,7},{7,8},{8,9},{9,10},{10,1... | collective-permute-start | bytes 786440 | tf_op jit(solution)/shard_map/ppermute | solution.py:218
  86.7 0.0 collective-permute-done.12
  86.7 3.2 %collective-permute-start.16 = (bf16[512,256]{1,0:T(8,128)(2,1)S(1)}, bf16[512,256]{1,0:T(8,128)(2,1)S(1)}, u32[]{:S(2)}, u32[]{:S(2)}) collective-permute-start(bf16[512,256]{1,0:T(8,128)(2,1)S(1)} %collective-permute-done.12), channel_id=1, source_target_pairs={{16,31},{17,16},{18,17},{19,18},{20,19},{21,20},{22,21},{23,22},{2... | collective-permute-start | bytes 786440 | tf_op jit(solution)/shard_map/ppermute | solution.py:218
  89.9 1.3 %collective-permute-start.13 = (bf16[512,256]{1,0:T(8,128)(2,1)S(1)}, bf16[512,256]{1,0:T(8,128)(2,1)S(1)}, u32[]{:S(2)}, u32[]{:S(2)}) collective-permute-start(bf16[512,256]{1,0:T(8,128)(2,1)S(1)} %collective-permute-done.12), channel_id=1, source_target_pairs={{0,17},{1,18},{2,19},{3,20},{4,21},{5,22},{6,23},{7,24},{8,25},{9,... | collective-permute-start | bytes 786440 | tf_op jit(solution)/shard_map/ppermute | solution.py:218
  91.2 0.2 fusion.21
  91.4 0.3 fusion.4
  91.7 0.2 fusion.23
  91.9 1.3 %collective-permute-start.15 = (f32[512,256]{1,0:T(8,128)S(1)}, f32[512,256]{1,0:T(8,128)S(1)}, u32[]{:S(2)}, u32[]{:S(2)}) collective-permute-start(f32[512,256]{1,0:T(8,128)S(1)} %fusion.4), channel_id=1, source_target_pairs={{0,16},{1,17},{2,18},{3,19},{4,20},{5,21},{6,22},{7,23},{8,24},{9,... | collective-permute-start | bytes 1572872 | tf_op jit(solution)/shard_map/ppermute | solution.py:243
  93.2 0.6 collective-permute-done.16
  93.8 0.0 collective-permute-done.11
  93.8 4.4 %collective-permute-start.17 = (bf16[512,256]{1,0:T(8,128)(2,1)S(1)}, bf16[512,256]{1,0:T(8,128)(2,1)S(1)}, u32[]{:S(2)}, u32[]{:S(2)}) collective-permute-start(bf16[512,256]{1,0:T(8,128)(2,1)S(1)} %collective-permute-done.16), channel_id=1, source_target_pairs={{16,31},{17,16},{18,17},{19,18},{20,19},{21,20},{22,21},{23,22},{2... | collective-permute-start | bytes 786440 | tf_op jit(solution)/shard_map/ppermute | solution.py:218
  98.2 1.9 %collective-permute-start.14 = (bf16[512,256]{1,0:T(8,128)(2,1)S(1)}, bf16[512,256]{1,0:T(8,128)(2,1)S(1)}, u32[]{:S(2)}, u32[]{:S(2)}) collective-permute-start(bf16[512,256]{1,0:T(8,128)(2,1)S(1)} %collective-permute-done.11), channel_id=1, source_target_pairs={{16,31},{17,16},{18,17},{19,18},{20,19},{21,20},{22,21},{23,22},{2... | collective-permute-start | bytes 786440 | tf_op jit(solution)/shard_map/ppermute | solution.py:218
  100.1 0.2 fusion.19
  100.4 1.1 %collective-permute-done.13 = bf16[512,256]{1,0:T(8,128)(2,1)S(1)} collective-permute-done((bf16[512,256]{1,0:T(8,128)(2,1)S(1)}, bf16[512,256]{1,0:T(8,128)(2,1)S(1)}, u32[]{:S(2)}, u32[]{:S(2)}) %collective-permute-start.13) | collective-permute-done | bytes 262176 | tf_op jit(solution)/shard_map/ppermute | solution.py:218
  101.5 0.2 fusion.11
  101.7 0.2 fusion.15
  101.9 0.3 fusion
  102.2 1.4 %collective-permute-start.18 = (f32[512,256]{1,0:T(8,128)S(1)}, f32[512,256]{1,0:T(8,128)S(1)}, u32[]{:S(2)}, u32[]{:S(2)}) collective-permute-start(f32[512,256]{1,0:T(8,128)S(1)} %fusion), channel_id=1, source_target_pairs={{16,0},{17,1},{18,2},{19,3},{20,4},{21,5},{22,6},{23,7},{24,8},{25... | collective-permute-start | bytes 1572872 | tf_op jit(solution)/shard_map/ppermute | solution.py:250
  103.6 0.3 fusion.10
  104.0 1.4 %collective-permute-done.14 = bf16[512,256]{1,0:T(8,128)(2,1)S(1)} collective-permute-done((bf16[512,256]{1,0:T(8,128)(2,1)S(1)}, bf16[512,256]{1,0:T(8,128)(2,1)S(1)}, u32[]{:S(2)}, u32[]{:S(2)}) %collective-permute-start.14) | collective-permute-done | bytes 262176 | tf_op jit(solution)/shard_map/ppermute | solution.py:218
  105.3 0.2 convolution_add_fusion.2
  105.5 0.0 collective-permute-done.15
  105.6 0.0 collective-permute-done.18
  105.6 0.8 add_convert_fusion
  (12 shorter events, 0.0 us)
Async XLA Ops:
  0.0 48.4 %copy-start = (bf16[4096,256]{1,0:T(8,128)(2,1)S(1)}, bf16[4096,256]{1,0:T(8,128)(2,1)}, u32[]{:S(2)}) copy-start(bf16[4096,256]{1,0:T(8,128)(2,1)} %param.13) | copy-start | bytes 6291460
  0.0 14.4 %copy-start.4 = (f32[16,256]{1,0:T(8,128)S(1)}, f32[16,256]{1,0:T(8,128)}, u32[]{:S(2)}) copy-start(f32[16,256]{1,0:T(8,128)} %rates_ref.1) | copy-start | bytes 49156
  0.0 14.4 %copy-start.1 = (bf16[512,256]{1,0:T(8,128)(2,1)S(1)}, bf16[512,256]{1,0:T(8,128)(2,1)}, u32[]{:S(2)}) copy-start(bf16[512,256]{1,0:T(8,128)(2,1)} %k_hbm.3) | copy-start | bytes 786436
  0.0 14.4 %copy-start.6 = (f32[256]{0:T(256)S(1)}, f32[256]{0:T(256)}, u32[]{:S(2)}) copy-start(f32[256]{0:T(256)} %param.12) | copy-start | bytes 3076
  0.0 14.4 %copy-start.5 = (f32[16,256]{1,0:T(8,128)S(1)}, f32[16,256]{1,0:T(8,128)}, u32[]{:S(2)}) copy-start(f32[16,256]{1,0:T(8,128)} %resid_ref.1) | copy-start | bytes 49156
  3.3 22.8 %all-to-all-start = ((f32[32,16,256]{2,1,0:T(8,128)}), f32[32,16,256]{2,1,0:T(8,128)}, u32[]{:S(2)}, u32[]{:S(2)}) async-start(f32[32,16,256]{2,1,0:T(8,128)} %states.1), calls=%async_computation | async-start | bytes 1048576 | tf_op jit(solution)/shard_map/all_to_all | solution.py:192
  14.5 1.0 copy-start.2
  15.4 0.9 copy-start.3
  28.2 11.9 %collective-permute-start = (bf16[512,256]{1,0:T(8,128)(2,1)S(1)}, bf16[512,256]{1,0:T(8,128)(2,1)S(1)}, u32[]{:S(2)}, u32[]{:S(2)}) collective-permute-start(bf16[512,256]{1,0:T(8,128)(2,1)S(1)} %carry_and_gate.1), channel_id=1, source_target_pairs={{0,1},{1,2},{2,3},{3,4},{4,5},{5,6},{6,7},{7,8},{8,9},{9,10},{10,1... | collective-permute-start | bytes 786440 | tf_op jit(solution)/shard_map/ppermute | solution.py:218
  36.8 8.3 %collective-permute-start.2 = (bf16[512,256]{1,0:T(8,128)(2,1)S(1)}, bf16[512,256]{1,0:T(8,128)(2,1)S(1)}, u32[]{:S(2)}, u32[]{:S(2)}) collective-permute-start(bf16[512,256]{1,0:T(8,128)(2,1)S(1)} %carry_and_gate.1), channel_id=1, source_target_pairs={{16,1},{17,2},{18,3},{19,4},{20,5},{21,6},{22,7},{23,8},{24,9},{25... | collective-permute-start | bytes 786440 | tf_op jit(solution)/shard_map/ppermute | solution.py:218
  40.1 8.6 %collective-permute-start.1 = (bf16[512,256]{1,0:T(8,128)(2,1)S(1)}, bf16[512,256]{1,0:T(8,128)(2,1)S(1)}, u32[]{:S(2)}, u32[]{:S(2)}) collective-permute-start(bf16[512,256]{1,0:T(8,128)(2,1)S(1)} %collective-permute-done), channel_id=1, source_target_pairs={{0,1},{1,2},{2,3},{3,4},{4,5},{5,6},{6,7},{7,8},{8,9},{9,10},{10,1... | collective-permute-start | bytes 786440 | tf_op jit(solution)/shard_map/ppermute | solution.py:218
  45.1 8.3 %collective-permute-start.4 = (bf16[512,256]{1,0:T(8,128)(2,1)S(1)}, bf16[512,256]{1,0:T(8,128)(2,1)S(1)}, u32[]{:S(2)}, u32[]{:S(2)}) collective-permute-start(bf16[512,256]{1,0:T(8,128)(2,1)S(1)} %collective-permute-done.2), channel_id=1, source_target_pairs={{0,1},{1,2},{2,3},{3,4},{4,5},{5,6},{6,7},{7,8},{8,9},{9,10},{10,1... | collective-permute-start | bytes 786440 | tf_op jit(solution)/shard_map/ppermute | solution.py:218
  48.6 8.5 %collective-permute-start.3 = (bf16[512,256]{1,0:T(8,128)(2,1)S(1)}, bf16[512,256]{1,0:T(8,128)(2,1)S(1)}, u32[]{:S(2)}, u32[]{:S(2)}) collective-permute-start(bf16[512,256]{1,0:T(8,128)(2,1)S(1)} %collective-permute-done.1), channel_id=1, source_target_pairs={{0,1},{1,2},{2,3},{3,4},{4,5},{5,6},{6,7},{7,8},{8,9},{9,10},{10,1... | collective-permute-start | bytes 786440 | tf_op jit(solution)/shard_map/ppermute | solution.py:218
  53.4 8.3 %collective-permute-start.6 = (bf16[512,256]{1,0:T(8,128)(2,1)S(1)}, bf16[512,256]{1,0:T(8,128)(2,1)S(1)}, u32[]{:S(2)}, u32[]{:S(2)}) collective-permute-start(bf16[512,256]{1,0:T(8,128)(2,1)S(1)} %collective-permute-done.4), channel_id=1, source_target_pairs={{0,1},{1,2},{2,3},{3,4},{4,5},{5,6},{6,7},{7,8},{8,9},{9,10},{10,1... | collective-permute-start | bytes 786440 | tf_op jit(solution)/shard_map/ppermute | solution.py:218
  57.1 8.3 %collective-permute-start.5 = (bf16[512,256]{1,0:T(8,128)(2,1)S(1)}, bf16[512,256]{1,0:T(8,128)(2,1)S(1)}, u32[]{:S(2)}, u32[]{:S(2)}) collective-permute-start(bf16[512,256]{1,0:T(8,128)(2,1)S(1)} %collective-permute-done.3), channel_id=1, source_target_pairs={{0,1},{1,2},{2,3},{3,4},{4,5},{5,6},{6,7},{7,8},{8,9},{9,10},{10,1... | collective-permute-start | bytes 786440 | tf_op jit(solution)/shard_map/ppermute | solution.py:218
  61.7 8.3 %collective-permute-start.8 = (bf16[512,256]{1,0:T(8,128)(2,1)S(1)}, bf16[512,256]{1,0:T(8,128)(2,1)S(1)}, u32[]{:S(2)}, u32[]{:S(2)}) collective-permute-start(bf16[512,256]{1,0:T(8,128)(2,1)S(1)} %collective-permute-done.6), channel_id=1, source_target_pairs={{0,1},{1,2},{2,3},{3,4},{4,5},{5,6},{6,7},{7,8},{8,9},{9,10},{10,1... | collective-permute-start | bytes 786440 | tf_op jit(solution)/shard_map/ppermute | solution.py:218
  65.4 8.3 %collective-permute-start.7 = (bf16[512,256]{1,0:T(8,128)(2,1)S(1)}, bf16[512,256]{1,0:T(8,128)(2,1)S(1)}, u32[]{:S(2)}, u32[]{:S(2)}) collective-permute-start(bf16[512,256]{1,0:T(8,128)(2,1)S(1)} %collective-permute-done.5), channel_id=1, source_target_pairs={{0,1},{1,2},{2,3},{3,4},{4,5},{5,6},{6,7},{7,8},{8,9},{9,10},{10,1... | collective-permute-start | bytes 786440 | tf_op jit(solution)/shard_map/ppermute | solution.py:218
  70.0 8.3 %collective-permute-start.10 = (bf16[512,256]{1,0:T(8,128)(2,1)S(1)}, bf16[512,256]{1,0:T(8,128)(2,1)S(1)}, u32[]{:S(2)}, u32[]{:S(2)}) collective-permute-start(bf16[512,256]{1,0:T(8,128)(2,1)S(1)} %collective-permute-done.8), channel_id=1, source_target_pairs={{0,1},{1,2},{2,3},{3,4},{4,5},{5,6},{6,7},{7,8},{8,9},{9,10},{10,1... | collective-permute-start | bytes 786440 | tf_op jit(solution)/shard_map/ppermute | solution.py:218
  73.7 8.3 %collective-permute-start.9 = (bf16[512,256]{1,0:T(8,128)(2,1)S(1)}, bf16[512,256]{1,0:T(8,128)(2,1)S(1)}, u32[]{:S(2)}, u32[]{:S(2)}) collective-permute-start(bf16[512,256]{1,0:T(8,128)(2,1)S(1)} %collective-permute-done.7), channel_id=1, source_target_pairs={{0,1},{1,2},{2,3},{3,4},{4,5},{5,6},{6,7},{7,8},{8,9},{9,10},{10,1... | collective-permute-start | bytes 786440 | tf_op jit(solution)/shard_map/ppermute | solution.py:218
  78.3 8.3 %collective-permute-start.12 = (bf16[512,256]{1,0:T(8,128)(2,1)S(1)}, bf16[512,256]{1,0:T(8,128)(2,1)S(1)}, u32[]{:S(2)}, u32[]{:S(2)}) collective-permute-start(bf16[512,256]{1,0:T(8,128)(2,1)S(1)} %collective-permute-done.10), channel_id=1, source_target_pairs={{0,1},{1,2},{2,3},{3,4},{4,5},{5,6},{6,7},{7,8},{8,9},{9,10},{10,1... | collective-permute-start | bytes 786440 | tf_op jit(solution)/shard_map/ppermute | solution.py:218
  82.0 11.8 %collective-permute-start.11 = (bf16[512,256]{1,0:T(8,128)(2,1)S(1)}, bf16[512,256]{1,0:T(8,128)(2,1)S(1)}, u32[]{:S(2)}, u32[]{:S(2)}) collective-permute-start(bf16[512,256]{1,0:T(8,128)(2,1)S(1)} %collective-permute-done.9), channel_id=1, source_target_pairs={{0,1},{1,2},{2,3},{3,4},{4,5},{5,6},{6,7},{7,8},{8,9},{9,10},{10,1... | collective-permute-start | bytes 786440 | tf_op jit(solution)/shard_map/ppermute | solution.py:218
  86.7 7.1 %collective-permute-start.16 = (bf16[512,256]{1,0:T(8,128)(2,1)S(1)}, bf16[512,256]{1,0:T(8,128)(2,1)S(1)}, u32[]{:S(2)}, u32[]{:S(2)}) collective-permute-start(bf16[512,256]{1,0:T(8,128)(2,1)S(1)} %collective-permute-done.12), channel_id=1, source_target_pairs={{16,31},{17,16},{18,17},{19,18},{20,19},{21,20},{22,21},{23,22},{2... | collective-permute-start | bytes 786440 | tf_op jit(solution)/shard_map/ppermute | solution.py:218
  89.9 11.6 %collective-permute-start.13 = (bf16[512,256]{1,0:T(8,128)(2,1)S(1)}, bf16[512,256]{1,0:T(8,128)(2,1)S(1)}, u32[]{:S(2)}, u32[]{:S(2)}) collective-permute-start(bf16[512,256]{1,0:T(8,128)(2,1)S(1)} %collective-permute-done.12), channel_id=1, source_target_pairs={{0,17},{1,18},{2,19},{3,20},{4,21},{5,22},{6,23},{7,24},{8,25},{9,... | collective-permute-start | bytes 786440 | tf_op jit(solution)/shard_map/ppermute | solution.py:218
  91.9 13.6 %collective-permute-start.15 = (f32[512,256]{1,0:T(8,128)S(1)}, f32[512,256]{1,0:T(8,128)S(1)}, u32[]{:S(2)}, u32[]{:S(2)}) collective-permute-start(f32[512,256]{1,0:T(8,128)S(1)} %fusion.4), channel_id=1, source_target_pairs={{0,16},{1,17},{2,18},{3,19},{4,20},{5,21},{6,22},{7,23},{8,24},{9,... | collective-permute-start | bytes 1572872 | tf_op jit(solution)/shard_map/ppermute | solution.py:243
  93.8 7.9 %collective-permute-start.17 = (bf16[512,256]{1,0:T(8,128)(2,1)S(1)}, bf16[512,256]{1,0:T(8,128)(2,1)S(1)}, u32[]{:S(2)}, u32[]{:S(2)}) collective-permute-start(bf16[512,256]{1,0:T(8,128)(2,1)S(1)} %collective-permute-done.16), channel_id=1, source_target_pairs={{16,31},{17,16},{18,17},{19,18},{20,19},{21,20},{22,21},{23,22},{2... | collective-permute-start | bytes 786440 | tf_op jit(solution)/shard_map/ppermute | solution.py:218
  98.2 7.1 %collective-permute-start.14 = (bf16[512,256]{1,0:T(8,128)(2,1)S(1)}, bf16[512,256]{1,0:T(8,128)(2,1)S(1)}, u32[]{:S(2)}, u32[]{:S(2)}) collective-permute-start(bf16[512,256]{1,0:T(8,128)(2,1)S(1)} %collective-permute-done.11), channel_id=1, source_target_pairs={{16,31},{17,16},{18,17},{19,18},{20,19},{21,20},{22,21},{23,22},{2... | collective-permute-start | bytes 786440 | tf_op jit(solution)/shard_map/ppermute | solution.py:218
  102.2 3.4 %collective-permute-start.18 = (f32[512,256]{1,0:T(8,128)S(1)}, f32[512,256]{1,0:T(8,128)S(1)}, u32[]{:S(2)}, u32[]{:S(2)}) collective-permute-start(f32[512,256]{1,0:T(8,128)S(1)} %fusion), channel_id=1, source_target_pairs={{16,0},{17,1},{18,2},{19,3},{20,4},{21,5},{22,6},{23,7},{24,8},{25... | collective-permute-start | bytes 1572872 | tf_op jit(solution)/shard_map/ppermute | solution.py:250

commit v5 on v4

--- a/solution.py
+++ b/solution.py
@@ -112,33 +112,34 @@
         lax.fori_loop(0, steps, step, tuple(first), unroll=4)
 
 
-def gate_kernel(at_ref, all_ref, rates_ref, resid_ref, local_ref, out_ref, flat):
+def gate_kernel(at_ref, all_hbm, rates_ref, resid_ref, local_ref, out_ref, flat, all_ref, poles_ref, grown_ref, sems):
     devices, modes, width = all_ref.shape
     steps = local_ref.shape[0]
     rows = out_ref.shape[0]
+    (copy,) = fetch(((all_hbm, all_ref),), sems)
     block = lax.broadcasted_iota(jnp.int32, (BLOCKS, LANES), 0).astype(F32)
-    rates = rates_ref[...]
-    fade = jnp.exp(-rates * float(rows))
+    halves = [slice(half * LANES, (half + 1) * LANES) for half in range(width // LANES)]
+    for lanes in halves:
+        for m in range(modes):
+            rate = spread(rates_ref, m, lanes)
+            poles_ref[m, :, lanes] = jnp.exp(-rate)
+            grown_ref[m, :, lanes] = spread(resid_ref, m, lanes) * jnp.exp(-rate * (steps * block + 1.0))
+    fade = jnp.exp(-rates_ref[...] * float(rows))
+    copy.wait()
     before = jnp.zeros((modes, width), F32)
     for d in range(devices - 1):
         before = jnp.where(d < at_ref[0], fade * before + all_ref[d], before)
-    before = before * resid_ref[...]
-    for half in range(width // LANES):
-        lanes = slice(half * LANES, (half + 1) * LANES)
-        poles, first = [], []
-        for m in range(modes):
-            rate = spread(rates_ref, m, lanes)
-            poles.append(jnp.exp(-rate))
-            come = jnp.broadcast_to(before[m : m + 1, lanes], (BLOCKS, LANES))
-            first.append(come * jnp.exp(-rate * (steps * block + 1.0)))
+    for half, lanes in enumerate(halves):
+        poles = [poles_ref[m, :, lanes] for m in range(modes)]
+        first = [grown_ref[m, :, lanes] * jnp.broadcast_to(before[m : m + 1, lanes], (BLOCKS, LANES)) for m in range(modes)]
 
         def step(j, held):
             conv = local_ref[j, 0:BLOCKS, lanes] + tree_sum(held)
             flat[half, pl.ds(j, BLOCKS, stride=steps), :] = local_ref[j, BLOCKS : 2 * BLOCKS, lanes] * conv
             return tuple(p * h for p, h in zip(poles, held))
 
-        lax.fori_loop(0, steps, step, tuple(first), unroll=4)
-        piece = 64
+        lax.fori_loop(0, steps, step, tuple(first), unroll=8)
+        piece = 128
 
         @pl.loop(0, rows // piece)
         def _(i):
@@ -207,9 +208,11 @@
         2 * work,
         limit=8 << 20,
         out_shape=shape((rows, width), BF16),
-        in_specs=[SMEM] + [VMEM] * 4,
+        in_specs=[SMEM, ANY] + [VMEM] * 3,
         out_specs=VMEM,
-        scratch_shapes=[flat_of],
+        scratch_shapes=[flat_of, pltpu.VMEM((devices, modes, width), F32)]
+        + [pltpu.VMEM((modes, BLOCKS, width), F32)] * 2
+        + [sems(1)],
     )(position, every, decay_rates, residues, local)
 
     ring = [(c * depth + i, c * depth + (i + 1 - 2 * c) % depth) for c in range(2) for i in range(depth)]
@@ -222,6 +225,7 @@
         weight = lax.dynamic_slice(out_weight, (source * width, 0), (width, out_weight.shape[1]))
         return jnp.dot(array, weight, preferred_element_type=F32)
 
+    out_weight, own = lax.optimization_barrier((out_weight, own))
     sum_own = project(own, 0)
     own, oth = hop(own), hop(own, cross)
     sum_own, sum_oth = sum_own + project(own, 1), project(oth, 1)

time: 107 us -> 107 us (level)
  no operation moved by 1% of the time
where the time goes in v5:
time: 107 us; the launch traced here: 106 us
  starting transfers between devices  79.3 us (74%)
  waiting for transfers between devices  11.1 us (10%)
  Pallas kernels  8.23 us (8%)
  matrix products  4.27 us (4%)
  local copies, waits for them, and re-layouts  1.91 us (2%)
    ppermute x17, starting transfers between devices, body(): hop = lambda array, pairs=ring: lax.ppermute(array, ('core', 'ch'), pairs)  65.5 us
    all_to_all x1, starting transfers between devices, body(): every = lax.all_to_all(every, seq, split_axis=0, concat_axis=0, tiled=True)  11.1 us
    all_to_all x1, waiting for transfers between devices, body(): every = lax.all_to_all(every, seq, split_axis=0, concat_axis=0, tiled=True)  6.72 us
    ppermute x17, waiting for transfers between devices, body(): hop = lambda array, pairs=ring: lax.ppermute(array, ('core', 'ch'), pairs)  4.4 us
    dot_general x18, matrix products, project(): return jnp.dot(array, weight, preferred_element_type=F32)  4.27 us
    pallas_call x1, Pallas kernels, body(): kernel_call(states_kernel, 'states', 2 * work, out_shape=shape((devices,...  3.3 us
    pallas_call x1, Pallas kernels, body(): kernel_call(local_kernel, 'local_convolution', 6 * work, limit=8 << 20, o...  3.03 us
  transfers between devices with their start and end apart: 20, of which 5 were waited for; matrix products, arithmetic and copies ran while one was open for 4% of the time, Pallas kernels for 3%

profile of v5, /device:TPU:1, one launch (start us, length us, event | category | flops | bytes accessed | tf_op | source)
XLA Modules:
  0.0 106.2 jit_solution(3434811355736003947)
XLA Ops:
  0.0 3.3 %states.1 = f32[32,16,256]{2,1,0:T(8,128)} custom-call(bf16[512,256]{1,0:T(8,128)(2,1)} %k_hbm.3, bf16[512,256]{1,0:T(8,128)(2,1)} %v_hbm.3, f32[16,256]{1,0:T(8,128)} %rates_ref.1), custom_call_target="tpu_custom_call" | custom-call | flops 4194304 | bytes 1048576 | tf_op jit(solution)/shard_map/states/pallas_call | solution.py:184
  3.3 11.1 %all-to-all-start = ((f32[32,16,256]{2,1,0:T(8,128)}), f32[32,16,256]{2,1,0:T(8,128)}, u32[]{:S(2)}, u32[]{:S(2)}) async-start(f32[32,16,256]{2,1,0:T(8,128)} %states.1), calls=%async_computation | async-start | bytes 1048576 | tf_op jit(solution)/shard_map/all_to_all | solution.py:193
  14.5 0.0 copy-start.2
  14.5 0.9 copy-done.2
  15.4 0.9 copy-done.3
  16.4 3.0 %local_convolution.1.local_ref = f32[64,16,256]{2,1,0:T(8,128)S(1)} custom-call(bf16[512,256]{1,0:T(8,128)(2,1)S(1)} %copy-done.1, bf16[512,256]{1,0:T(8,128)(2,1)S(1)} %copy-done.2, bf16[512,256]{1,0:T(8,128)(2,1)S(1)} %copy-done.3, f32[16,256]{1,0:T(8,128)S(1)} %copy-done.4, f32[16,256]{1,0:T(8,128)S(1)} %copy-done.5, f32[1,256]{1,0:T(1,128)S(1)} %bitcast.20), custom_call_target="tpu_custom_call" | custom-call | flops 12582912 | bytes 1048576 | tf_op jit(solution)/shard_map/local_convolution/pallas_call | solution.py:194
  19.4 6.7 %all-to-all-done.all_hbm = f32[32,16,256]{2,1,0:T(8,128)} async-done(((f32[32,16,256]{2,1,0:T(8,128)}), f32[32,16,256]{2,1,0:T(8,128)}, u32[]{:S(2)}, u32[]{:S(2)}) %all-to-all-start) | async-done | bytes 524320 | tf_op jit(solution)/shard_map/all_to_all | solution.py:193
  26.1 1.9 %carry_and_gate.1 = bf16[512,256]{1,0:T(8,128)(2,1)S(1)} custom-call(s32[1]{0:T(128)} %bitcast.at_ref, f32[32,16,256]{2,1,0:T(8,128)} %all-to-all-done.all_hbm, f32[16,256]{1,0:T(8,128)S(1)} %copy-done.4, f32[16,256]{1,0:T(8,128)S(1)} %copy-done.5, f32[64,16,256]{2,1,0:T(8,128)S(1)} %local_convolution.1.local_ref), custom_call_target="tpu_custom_call" | custom-call | flops 4194304 | bytes 1048576 | tf_op jit(solution)/shard_map/carry_and_gate/pallas_call | solution.py:205
  28.0 8.6 %collective-permute-start = (bf16[512,256]{1,0:T(8,128)(2,1)S(1)}, bf16[512,256]{1,0:T(8,128)(2,1)S(1)}, u32[]{:S(2)}, u32[]{:S(2)}) collective-permute-start(bf16[512,256]{1,0:T(8,128)(2,1)S(1)} %carry_and_gate.1), channel_id=1, source_target_pairs={{0,1},{1,2},{2,3},{3,4},{4,5},{5,6},{6,7},{7,8},{8,9},{9,10},{10,1... | collective-permute-start | bytes 786440 | tf_op jit(solution)/shard_map/ppermute | solution.py:221
  36.6 1.9 %collective-permute-start.2 = (bf16[512,256]{1,0:T(8,128)(2,1)S(1)}, bf16[512,256]{1,0:T(8,128)(2,1)S(1)}, u32[]{:S(2)}, u32[]{:S(2)}) collective-permute-start(bf16[512,256]{1,0:T(8,128)(2,1)S(1)} %carry_and_gate.1), channel_id=1, source_target_pairs={{16,1},{17,2},{18,3},{19,4},{20,5},{21,6},{22,7},{23,8},{24,9},{25... | collective-permute-start | bytes 786440 | tf_op jit(solution)/shard_map/ppermute | solution.py:221
  38.6 1.4 %collective-permute-done = bf16[512,256]{1,0:T(8,128)(2,1)S(1)} collective-permute-done((bf16[512,256]{1,0:T(8,128)(2,1)S(1)}, bf16[512,256]{1,0:T(8,128)(2,1)S(1)}, u32[]{:S(2)}, u32[]{:S(2)}) %collective-permute-start) | collective-permute-done | bytes 262176 | tf_op jit(solution)/shard_map/ppermute | solution.py:221
  39.9 5.0 %collective-permute-start.1 = (bf16[512,256]{1,0:T(8,128)(2,1)S(1)}, bf16[512,256]{1,0:T(8,128)(2,1)S(1)}, u32[]{:S(2)}, u32[]{:S(2)}) collective-permute-start(bf16[512,256]{1,0:T(8,128)(2,1)S(1)} %collective-permute-done), channel_id=1, source_target_pairs={{0,1},{1,2},{2,3},{3,4},{4,5},{5,6},{6,7},{7,8},{8,9},{9,10},{10,1... | collective-permute-start | bytes 786440 | tf_op jit(solution)/shard_map/ppermute | solution.py:221
  45.0 0.0 collective-permute-done.2
  45.0 3.2 %collective-permute-start.4 = (bf16[512,256]{1,0:T(8,128)(2,1)S(1)}, bf16[512,256]{1,0:T(8,128)(2,1)S(1)}, u32[]{:S(2)}, u32[]{:S(2)}) collective-permute-start(bf16[512,256]{1,0:T(8,128)(2,1)S(1)} %collective-permute-done.2), channel_id=1, source_target_pairs={{0,1},{1,2},{2,3},{3,4},{4,5},{5,6},{6,7},{7,8},{8,9},{9,10},{10,1... | collective-permute-start | bytes 786440 | tf_op jit(solution)/shard_map/ppermute | solution.py:221
  48.3 0.2 fusion.13
  48.5 0.0 collective-permute-done.1
  48.5 4.8 %collective-permute-start.3 = (bf16[512,256]{1,0:T(8,128)(2,1)S(1)}, bf16[512,256]{1,0:T(8,128)(2,1)S(1)}, u32[]{:S(2)}, u32[]{:S(2)}) collective-permute-start(bf16[512,256]{1,0:T(8,128)(2,1)S(1)} %collective-permute-done.1), channel_id=1, source_target_pairs={{0,1},{1,2},{2,3},{3,4},{4,5},{5,6},{6,7},{7,8},{8,9},{9,10},{10,1... | collective-permute-start | bytes 786440 | tf_op jit(solution)/shard_map/ppermute | solution.py:221
  53.3 0.0 collective-permute-done.4
  53.3 3.2 %collective-permute-start.6 = (bf16[512,256]{1,0:T(8,128)(2,1)S(1)}, bf16[512,256]{1,0:T(8,128)(2,1)S(1)}, u32[]{:S(2)}, u32[]{:S(2)}) collective-permute-start(bf16[512,256]{1,0:T(8,128)(2,1)S(1)} %collective-permute-done.4), channel_id=1, source_target_pairs={{0,1},{1,2},{2,3},{3,4},{4,5},{5,6},{6,7},{7,8},{8,9},{9,10},{10,1... | collective-permute-start | bytes 786440 | tf_op jit(solution)/shard_map/ppermute | solution.py:221
  56.5 0.2 convolution_add_fusion.4
  56.7 0.2 fusion.37
  57.0 0.0 collective-permute-done.3
  57.0 4.6 %collective-permute-start.5 = (bf16[512,256]{1,0:T(8,128)(2,1)S(1)}, bf16[512,256]{1,0:T(8,128)(2,1)S(1)}, u32[]{:S(2)}, u32[]{:S(2)}) collective-permute-start(bf16[512,256]{1,0:T(8,128)(2,1)S(1)} %collective-permute-done.3), channel_id=1, source_target_pairs={{0,1},{1,2},{2,3},{3,4},{4,5},{5,6},{6,7},{7,8},{8,9},{9,10},{10,1... | collective-permute-start | bytes 786440 | tf_op jit(solution)/shard_map/ppermute | solution.py:221
  61.6 0.0 collective-permute-done.6
  61.6 3.2 %collective-permute-start.8 = (bf16[512,256]{1,0:T(8,128)(2,1)S(1)}, bf16[512,256]{1,0:T(8,128)(2,1)S(1)}, u32[]{:S(2)}, u32[]{:S(2)}) collective-permute-start(bf16[512,256]{1,0:T(8,128)(2,1)S(1)} %collective-permute-done.6), channel_id=1, source_target_pairs={{0,1},{1,2},{2,3},{3,4},{4,5},{5,6},{6,7},{7,8},{8,9},{9,10},{10,1... | collective-permute-start | bytes 786440 | tf_op jit(solution)/shard_map/ppermute | solution.py:221
  64.8 0.2 fusion.35
  65.0 0.2 fusion.33
  65.3 0.0 collective-permute-done.5
  65.3 4.6 %collective-permute-start.7 = (bf16[512,256]{1,0:T(8,128)(2,1)S(1)}, bf16[512,256]{1,0:T(8,128)(2,1)S(1)}, u32[]{:S(2)}, u32[]{:S(2)}) collective-permute-start(bf16[512,256]{1,0:T(8,128)(2,1)S(1)} %collective-permute-done.5), channel_id=1, source_target_pairs={{0,1},{1,2},{2,3},{3,4},{4,5},{5,6},{6,7},{7,8},{8,9},{9,10},{10,1... | collective-permute-start | bytes 786440 | tf_op jit(solution)/shard_map/ppermute | solution.py:221
  69.9 0.0 collective-permute-done.8
  69.9 3.2 %collective-permute-start.10 = (bf16[512,256]{1,0:T(8,128)(2,1)S(1)}, bf16[512,256]{1,0:T(8,128)(2,1)S(1)}, u32[]{:S(2)}, u32[]{:S(2)}) collective-permute-start(bf16[512,256]{1,0:T(8,128)(2,1)S(1)} %collective-permute-done.8), channel_id=1, source_target_pairs={{0,1},{1,2},{2,3},{3,4},{4,5},{5,6},{6,7},{7,8},{8,9},{9,10},{10,1... | collective-permute-start | bytes 786440 | tf_op jit(solution)/shard_map/ppermute | solution.py:221
  73.1 0.2 fusion.31
  73.4 0.2 fusion.29
  73.6 0.0 collective-permute-done.7
  73.6 4.6 %collective-permute-start.9 = (bf16[512,256]{1,0:T(8,128)(2,1)S(1)}, bf16[512,256]{1,0:T(8,128)(2,1)S(1)}, u32[]{:S(2)}, u32[]{:S(2)}) collective-permute-start(bf16[512,256]{1,0:T(8,128)(2,1)S(1)} %collective-permute-done.7), channel_id=1, source_target_pairs={{0,1},{1,2},{2,3},{3,4},{4,5},{5,6},{6,7},{7,8},{8,9},{9,10},{10,1... | collective-permute-start | bytes 786440 | tf_op jit(solution)/shard_map/ppermute | solution.py:221
  78.2 0.0 collective-permute-done.10
  78.2 3.2 %collective-permute-start.12 = (bf16[512,256]{1,0:T(8,128)(2,1)S(1)}, bf16[512,256]{1,0:T(8,128)(2,1)S(1)}, u32[]{:S(2)}, u32[]{:S(2)}) collective-permute-start(bf16[512,256]{1,0:T(8,128)(2,1)S(1)} %collective-permute-done.10), channel_id=1, source_target_pairs={{0,1},{1,2},{2,3},{3,4},{4,5},{5,6},{6,7},{7,8},{8,9},{9,10},{10,1... | collective-permute-start | bytes 786440 | tf_op jit(solution)/shard_map/ppermute | solution.py:221
  81.4 0.2 fusion.27
  81.7 0.2 fusion.25
  81.9 0.0 collective-permute-done.9
  81.9 4.6 %collective-permute-start.11 = (bf16[512,256]{1,0:T(8,128)(2,1)S(1)}, bf16[512,256]{1,0:T(8,128)(2,1)S(1)}, u32[]{:S(2)}, u32[]{:S(2)}) collective-permute-start(bf16[512,256]{1,0:T(8,128)(2,1)S(1)} %collective-permute-done.9), channel_id=1, source_target_pairs={{0,1},{1,2},{2,3},{3,4},{4,5},{5,6},{6,7},{7,8},{8,9},{9,10},{10,1... | collective-permute-start | bytes 786440 | tf_op jit(solution)/shard_map/ppermute | solution.py:221
  86.5 0.0 collective-permute-done.12
  86.5 3.2 %collective-permute-start.16 = (bf16[512,256]{1,0:T(8,128)(2,1)S(1)}, bf16[512,256]{1,0:T(8,128)(2,1)S(1)}, u32[]{:S(2)}, u32[]{:S(2)}) collective-permute-start(bf16[512,256]{1,0:T(8,128)(2,1)S(1)} %collective-permute-done.12), channel_id=1, source_target_pairs={{16,31},{17,16},{18,17},{19,18},{20,19},{21,20},{22,21},{23,22},{2... | collective-permute-start | bytes 786440 | tf_op jit(solution)/shard_map/ppermute | solution.py:221
  89.8 1.3 %collective-permute-start.13 = (bf16[512,256]{1,0:T(8,128)(2,1)S(1)}, bf16[512,256]{1,0:T(8,128)(2,1)S(1)}, u32[]{:S(2)}, u32[]{:S(2)}) collective-permute-start(bf16[512,256]{1,0:T(8,128)(2,1)S(1)} %collective-permute-done.12), channel_id=1, source_target_pairs={{0,17},{1,18},{2,19},{3,20},{4,21},{5,22},{6,23},{7,24},{8,25},{9,... | collective-permute-start | bytes 786440 | tf_op jit(solution)/shard_map/ppermute | solution.py:221
  91.1 0.2 fusion.21
  91.3 0.3 fusion.4
  91.6 0.2 fusion.23
  91.8 1.3 %collective-permute-start.15 = (f32[512,256]{1,0:T(8,128)S(1)}, f32[512,256]{1,0:T(8,128)S(1)}, u32[]{:S(2)}, u32[]{:S(2)}) collective-permute-start(f32[512,256]{1,0:T(8,128)S(1)} %fusion.4), channel_id=1, source_target_pairs={{0,16},{1,17},{2,18},{3,19},{4,20},{5,21},{6,22},{7,23},{8,24},{9,... | collective-permute-start | bytes 1572872 | tf_op jit(solution)/shard_map/ppermute | solution.py:247
  93.1 0.6 collective-permute-done.16
  93.7 0.0 collective-permute-done.11
  93.7 4.4 %collective-permute-start.17 = (bf16[512,256]{1,0:T(8,128)(2,1)S(1)}, bf16[512,256]{1,0:T(8,128)(2,1)S(1)}, u32[]{:S(2)}, u32[]{:S(2)}) collective-permute-start(bf16[512,256]{1,0:T(8,128)(2,1)S(1)} %collective-permute-done.16), channel_id=1, source_target_pairs={{16,31},{17,16},{18,17},{19,18},{20,19},{21,20},{22,21},{23,22},{2... | collective-permute-start | bytes 786440 | tf_op jit(solution)/shard_map/ppermute | solution.py:221
  98.1 1.9 %collective-permute-start.14 = (bf16[512,256]{1,0:T(8,128)(2,1)S(1)}, bf16[512,256]{1,0:T(8,128)(2,1)S(1)}, u32[]{:S(2)}, u32[]{:S(2)}) collective-permute-start(bf16[512,256]{1,0:T(8,128)(2,1)S(1)} %collective-permute-done.11), channel_id=1, source_target_pairs={{16,31},{17,16},{18,17},{19,18},{20,19},{21,20},{22,21},{23,22},{2... | collective-permute-start | bytes 786440 | tf_op jit(solution)/shard_map/ppermute | solution.py:221
  100.0 0.2 fusion.19
  100.2 1.1 %collective-permute-done.13 = bf16[512,256]{1,0:T(8,128)(2,1)S(1)} collective-permute-done((bf16[512,256]{1,0:T(8,128)(2,1)S(1)}, bf16[512,256]{1,0:T(8,128)(2,1)S(1)}, u32[]{:S(2)}, u32[]{:S(2)}) %collective-permute-start.13) | collective-permute-done | bytes 262176 | tf_op jit(solution)/shard_map/ppermute | solution.py:221
  101.3 0.2 fusion.11
  101.6 0.2 fusion.15
  101.8 0.3 fusion
  102.1 1.4 %collective-permute-start.18 = (f32[512,256]{1,0:T(8,128)S(1)}, f32[512,256]{1,0:T(8,128)S(1)}, u32[]{:S(2)}, u32[]{:S(2)}) collective-permute-start(f32[512,256]{1,0:T(8,128)S(1)} %fusion), channel_id=1, source_target_pairs={{16,0},{17,1},{18,2},{19,3},{20,4},{21,5},{22,6},{23,7},{24,8},{25... | collective-permute-start | bytes 1572872 | tf_op jit(solution)/shard_map/ppermute | solution.py:254
  103.5 0.3 fusion.10
  103.9 1.3 %collective-permute-done.14 = bf16[512,256]{1,0:T(8,128)(2,1)S(1)} collective-permute-done((bf16[512,256]{1,0:T(8,128)(2,1)S(1)}, bf16[512,256]{1,0:T(8,128)(2,1)S(1)}, u32[]{:S(2)}, u32[]{:S(2)}) %collective-permute-start.14) | collective-permute-done | bytes 262176 | tf_op jit(solution)/shard_map/ppermute | solution.py:221
  105.2 0.2 convolution_add_fusion.2
  105.4 0.0 collective-permute-done.15
  105.4 0.0 collective-permute-done.18
  105.5 0.8 add_convert_fusion
  (12 shorter events, 0.0 us)
Async XLA Ops:
  0.0 48.3 %copy-start = (bf16[4096,256]{1,0:T(8,128)(2,1)S(1)}, bf16[4096,256]{1,0:T(8,128)(2,1)}, u32[]{:S(2)}) copy-start(bf16[4096,256]{1,0:T(8,128)(2,1)} %param.13) | copy-start | bytes 6291460
  0.0 14.4 %copy-start.4 = (f32[16,256]{1,0:T(8,128)S(1)}, f32[16,256]{1,0:T(8,128)}, u32[]{:S(2)}) copy-start(f32[16,256]{1,0:T(8,128)} %rates_ref.1) | copy-start | bytes 49156
  0.0 14.4 %copy-start.1 = (bf16[512,256]{1,0:T(8,128)(2,1)S(1)}, bf16[512,256]{1,0:T(8,128)(2,1)}, u32[]{:S(2)}) copy-start(bf16[512,256]{1,0:T(8,128)(2,1)} %k_hbm.3) | copy-start | bytes 786436
  0.0 14.4 %copy-start.6 = (f32[256]{0:T(256)S(1)}, f32[256]{0:T(256)}, u32[]{:S(2)}) copy-start(f32[256]{0:T(256)} %param.12) | copy-start | bytes 3076
  0.0 14.4 %copy-start.5 = (f32[16,256]{1,0:T(8,128)S(1)}, f32[16,256]{1,0:T(8,128)}, u32[]{:S(2)}) copy-start(f32[16,256]{1,0:T(8,128)} %resid_ref.1) | copy-start | bytes 49156
  3.3 22.8 %all-to-all-start = ((f32[32,16,256]{2,1,0:T(8,128)}), f32[32,16,256]{2,1,0:T(8,128)}, u32[]{:S(2)}, u32[]{:S(2)}) async-start(f32[32,16,256]{2,1,0:T(8,128)} %states.1), calls=%async_computation | async-start | bytes 1048576 | tf_op jit(solution)/shard_map/all_to_all | solution.py:193
  14.5 1.0 copy-start.2
  15.4 0.9 copy-start.3
  28.0 11.9 %collective-permute-start = (bf16[512,256]{1,0:T(8,128)(2,1)S(1)}, bf16[512,256]{1,0:T(8,128)(2,1)S(1)}, u32[]{:S(2)}, u32[]{:S(2)}) collective-permute-start(bf16[512,256]{1,0:T(8,128)(2,1)S(1)} %carry_and_gate.1), channel_id=1, source_target_pairs={{0,1},{1,2},{2,3},{3,4},{4,5},{5,6},{6,7},{7,8},{8,9},{9,10},{10,1... | collective-permute-start | bytes 786440 | tf_op jit(solution)/shard_map/ppermute | solution.py:221
  36.6 8.3 %collective-permute-start.2 = (bf16[512,256]{1,0:T(8,128)(2,1)S(1)}, bf16[512,256]{1,0:T(8,128)(2,1)S(1)}, u32[]{:S(2)}, u32[]{:S(2)}) collective-permute-start(bf16[512,256]{1,0:T(8,128)(2,1)S(1)} %carry_and_gate.1), channel_id=1, source_target_pairs={{16,1},{17,2},{18,3},{19,4},{20,5},{21,6},{22,7},{23,8},{24,9},{25... | collective-permute-start | bytes 786440 | tf_op jit(solution)/shard_map/ppermute | solution.py:221
  39.9 8.6 %collective-permute-start.1 = (bf16[512,256]{1,0:T(8,128)(2,1)S(1)}, bf16[512,256]{1,0:T(8,128)(2,1)S(1)}, u32[]{:S(2)}, u32[]{:S(2)}) collective-permute-start(bf16[512,256]{1,0:T(8,128)(2,1)S(1)} %collective-permute-done), channel_id=1, source_target_pairs={{0,1},{1,2},{2,3},{3,4},{4,5},{5,6},{6,7},{7,8},{8,9},{9,10},{10,1... | collective-permute-start | bytes 786440 | tf_op jit(solution)/shard_map/ppermute | solution.py:221
  45.0 8.3 %collective-permute-start.4 = (bf16[512,256]{1,0:T(8,128)(2,1)S(1)}, bf16[512,256]{1,0:T(8,128)(2,1)S(1)}, u32[]{:S(2)}, u32[]{:S(2)}) collective-permute-start(bf16[512,256]{1,0:T(8,128)(2,1)S(1)} %collective-permute-done.2), channel_id=1, source_target_pairs={{0,1},{1,2},{2,3},{3,4},{4,5},{5,6},{6,7},{7,8},{8,9},{9,10},{10,1... | collective-permute-start | bytes 786440 | tf_op jit(solution)/shard_map/ppermute | solution.py:221
  48.5 8.5 %collective-permute-start.3 = (bf16[512,256]{1,0:T(8,128)(2,1)S(1)}, bf16[512,256]{1,0:T(8,128)(2,1)S(1)}, u32[]{:S(2)}, u32[]{:S(2)}) collective-permute-start(bf16[512,256]{1,0:T(8,128)(2,1)S(1)} %collective-permute-done.1), channel_id=1, source_target_pairs={{0,1},{1,2},{2,3},{3,4},{4,5},{5,6},{6,7},{7,8},{8,9},{9,10},{10,1... | collective-permute-start | bytes 786440 | tf_op jit(solution)/shard_map/ppermute | solution.py:221
  53.3 8.3 %collective-permute-start.6 = (bf16[512,256]{1,0:T(8,128)(2,1)S(1)}, bf16[512,256]{1,0:T(8,128)(2,1)S(1)}, u32[]{:S(2)}, u32[]{:S(2)}) collective-permute-start(bf16[512,256]{1,0:T(8,128)(2,1)S(1)} %collective-permute-done.4), channel_id=1, source_target_pairs={{0,1},{1,2},{2,3},{3,4},{4,5},{5,6},{6,7},{7,8},{8,9},{9,10},{10,1... | collective-permute-start | bytes 786440 | tf_op jit(solution)/shard_map/ppermute | solution.py:221
  57.0 8.3 %collective-permute-start.5 = (bf16[512,256]{1,0:T(8,128)(2,1)S(1)}, bf16[512,256]{1,0:T(8,128)(2,1)S(1)}, u32[]{:S(2)}, u32[]{:S(2)}) collective-permute-start(bf16[512,256]{1,0:T(8,128)(2,1)S(1)} %collective-permute-done.3), channel_id=1, source_target_pairs={{0,1},{1,2},{2,3},{3,4},{4,5},{5,6},{6,7},{7,8},{8,9},{9,10},{10,1... | collective-permute-start | bytes 786440 | tf_op jit(solution)/shard_map/ppermute | solution.py:221
  61.6 8.3 %collective-permute-start.8 = (bf16[512,256]{1,0:T(8,128)(2,1)S(1)}, bf16[512,256]{1,0:T(8,128)(2,1)S(1)}, u32[]{:S(2)}, u32[]{:S(2)}) collective-permute-start(bf16[512,256]{1,0:T(8,128)(2,1)S(1)} %collective-permute-done.6), channel_id=1, source_target_pairs={{0,1},{1,2},{2,3},{3,4},{4,5},{5,6},{6,7},{7,8},{8,9},{9,10},{10,1... | collective-permute-start | bytes 786440 | tf_op jit(solution)/shard_map/ppermute | solution.py:221
  65.3 8.3 %collective-permute-start.7 = (bf16[512,256]{1,0:T(8,128)(2,1)S(1)}, bf16[512,256]{1,0:T(8,128)(2,1)S(1)}, u32[]{:S(2)}, u32[]{:S(2)}) collective-permute-start(bf16[512,256]{1,0:T(8,128)(2,1)S(1)} %collective-permute-done.5), channel_id=1, source_target_pairs={{0,1},{1,2},{2,3},{3,4},{4,5},{5,6},{6,7},{7,8},{8,9},{9,10},{10,1... | collective-permute-start | bytes 786440 | tf_op jit(solution)/shard_map/ppermute | solution.py:221
  69.9 8.3 %collective-permute-start.10 = (bf16[512,256]{1,0:T(8,128)(2,1)S(1)}, bf16[512,256]{1,0:T(8,128)(2,1)S(1)}, u32[]{:S(2)}, u32[]{:S(2)}) collective-permute-start(bf16[512,256]{1,0:T(8,128)(2,1)S(1)} %collective-permute-done.8), channel_id=1, source_target_pairs={{0,1},{1,2},{2,3},{3,4},{4,5},{5,6},{6,7},{7,8},{8,9},{9,10},{10,1... | collective-permute-start | bytes 786440 | tf_op jit(solution)/shard_map/ppermute | solution.py:221
  73.6 8.3 %collective-permute-start.9 = (bf16[512,256]{1,0:T(8,128)(2,1)S(1)}, bf16[512,256]{1,0:T(8,128)(2,1)S(1)}, u32[]{:S(2)}, u32[]{:S(2)}) collective-permute-start(bf16[512,256]{1,0:T(8,128)(2,1)S(1)} %collective-permute-done.7), channel_id=1, source_target_pairs={{0,1},{1,2},{2,3},{3,4},{4,5},{5,6},{6,7},{7,8},{8,9},{9,10},{10,1... | collective-permute-start | bytes 786440 | tf_op jit(solution)/shard_map/ppermute | solution.py:221
  78.2 8.3 %collective-permute-start.12 = (bf16[512,256]{1,0:T(8,128)(2,1)S(1)}, bf16[512,256]{1,0:T(8,128)(2,1)S(1)}, u32[]{:S(2)}, u32[]{:S(2)}) collective-permute-start(bf16[512,256]{1,0:T(8,128)(2,1)S(1)} %collective-permute-done.10), channel_id=1, source_target_pairs={{0,1},{1,2},{2,3},{3,4},{4,5},{5,6},{6,7},{7,8},{8,9},{9,10},{10,1... | collective-permute-start | bytes 786440 | tf_op jit(solution)/shard_map/ppermute | solution.py:221
  81.9 11.7 %collective-permute-start.11 = (bf16[512,256]{1,0:T(8,128)(2,1)S(1)}, bf16[512,256]{1,0:T(8,128)(2,1)S(1)}, u32[]{:S(2)}, u32[]{:S(2)}) collective-permute-start(bf16[512,256]{1,0:T(8,128)(2,1)S(1)} %collective-permute-done.9), channel_id=1, source_target_pairs={{0,1},{1,2},{2,3},{3,4},{4,5},{5,6},{6,7},{7,8},{8,9},{9,10},{10,1... | collective-permute-start | bytes 786440 | tf_op jit(solution)/shard_map/ppermute | solution.py:221
  86.5 7.1 %collective-permute-start.16 = (bf16[512,256]{1,0:T(8,128)(2,1)S(1)}, bf16[512,256]{1,0:T(8,128)(2,1)S(1)}, u32[]{:S(2)}, u32[]{:S(2)}) collective-permute-start(bf16[512,256]{1,0:T(8,128)(2,1)S(1)} %collective-permute-done.12), channel_id=1, source_target_pairs={{16,31},{17,16},{18,17},{19,18},{20,19},{21,20},{22,21},{23,22},{2... | collective-permute-start | bytes 786440 | tf_op jit(solution)/shard_map/ppermute | solution.py:221
  89.8 11.6 %collective-permute-start.13 = (bf16[512,256]{1,0:T(8,128)(2,1)S(1)}, bf16[512,256]{1,0:T(8,128)(2,1)S(1)}, u32[]{:S(2)}, u32[]{:S(2)}) collective-permute-start(bf16[512,256]{1,0:T(8,128)(2,1)S(1)} %collective-permute-done.12), channel_id=1, source_target_pairs={{0,17},{1,18},{2,19},{3,20},{4,21},{5,22},{6,23},{7,24},{8,25},{9,... | collective-permute-start | bytes 786440 | tf_op jit(solution)/shard_map/ppermute | solution.py:221
  91.8 13.6 %collective-permute-start.15 = (f32[512,256]{1,0:T(8,128)S(1)}, f32[512,256]{1,0:T(8,128)S(1)}, u32[]{:S(2)}, u32[]{:S(2)}) collective-permute-start(f32[512,256]{1,0:T(8,128)S(1)} %fusion.4), channel_id=1, source_target_pairs={{0,16},{1,17},{2,18},{3,19},{4,20},{5,21},{6,22},{7,23},{8,24},{9,... | collective-permute-start | bytes 1572872 | tf_op jit(solution)/shard_map/ppermute | solution.py:247
  93.7 7.9 %collective-permute-start.17 = (bf16[512,256]{1,0:T(8,128)(2,1)S(1)}, bf16[512,256]{1,0:T(8,128)(2,1)S(1)}, u32[]{:S(2)}, u32[]{:S(2)}) collective-permute-start(bf16[512,256]{1,0:T(8,128)(2,1)S(1)} %collective-permute-done.16), channel_id=1, source_target_pairs={{16,31},{17,16},{18,17},{19,18},{20,19},{21,20},{22,21},{23,22},{2... | collective-permute-start | bytes 786440 | tf_op jit(solution)/shard_map/ppermute | solution.py:221
  98.1 7.1 %collective-permute-start.14 = (bf16[512,256]{1,0:T(8,128)(2,1)S(1)}, bf16[512,256]{1,0:T(8,128)(2,1)S(1)}, u32[]{:S(2)}, u32[]{:S(2)}) collective-permute-start(bf16[512,256]{1,0:T(8,128)(2,1)S(1)} %collective-permute-done.11), channel_id=1, source_target_pairs={{16,31},{17,16},{18,17},{19,18},{20,19},{21,20},{22,21},{23,22},{2... | collective-permute-start | bytes 786440 | tf_op jit(solution)/shard_map/ppermute | solution.py:221
  102.1 3.4 %collective-permute-start.18 = (f32[512,256]{1,0:T(8,128)S(1)}, f32[512,256]{1,0:T(8,128)S(1)}, u32[]{:S(2)}, u32[]{:S(2)}) collective-permute-start(f32[512,256]{1,0:T(8,128)S(1)} %fusion), channel_id=1, source_target_pairs={{16,0},{17,1},{18,2},{19,3},{20,4},{21,5},{22,6},{23,7},{24,8},{25... | collective-permute-start | bytes 1572872 | tf_op jit(solution)/shard_map/ppermute | solution.py:254

commit v6 on v5

--- a/solution.py
+++ b/solution.py
@@ -57,20 +57,32 @@
     return poles, lax.fori_loop(0, steps, step, (jnp.zeros((BLOCKS, LANES), F32),) * modes, unroll=8)
 
 
-def states_kernel(k_hbm, v_hbm, rates_hbm, every_hbm, total_ref, flat, k_ref, v_ref, rates_ref, sems, sent):
+def states_kernel(k_hbm, v_hbm, rates_hbm, every_hbm, total_ref, flat, k_ref, v_ref, rates_ref, poles_ref, fades_ref, sems, sent):
     modes, width = rates_ref.shape
     rows = k_ref.shape[0]
     steps = rows // BLOCKS
-    for copy in fetch(((rates_hbm, rates_ref), (k_hbm, k_ref), (v_hbm, v_ref)), sems):
+    rates_copy, *copies = fetch(((rates_hbm, rates_ref), (k_hbm, k_ref), (v_hbm, v_ref)), sems)
+    rates_copy.wait()
+    block = lax.broadcasted_iota(jnp.int32, (BLOCKS, LANES), 0).astype(F32)
+    halves = [slice(half * LANES, (half + 1) * LANES) for half in range(width // LANES)]
+    for lanes in halves:
+        for m in range(modes):
+            rate = spread(rates_ref, m, lanes)
+            poles_ref[m, :, lanes] = jnp.exp(-rate)
+            fades_ref[m, :, lanes] = jnp.exp(-rate * (steps * (BLOCKS - 1 - block)))
+    for copy in copies:
         copy.wait()
     fill(flat, rows, mixed_in(k_ref, v_ref))
-    block = lax.broadcasted_iota(jnp.int32, (BLOCKS, LANES), 0).astype(F32)
-    for half in range(width // LANES):
-        lanes = slice(half * LANES, (half + 1) * LANES)
-        _, held = block_ends(flat, rates_ref, half)
-        for m in range(modes):
-            fade = jnp.exp(-spread(rates_ref, m, lanes) * (steps * (BLOCKS - 1 - block)))
-            total_ref[m : m + 1, lanes] = jnp.sum(fade * held[m], axis=0, keepdims=True)
+    for half, lanes in enumerate(halves):
+        poles = [poles_ref[m, :, lanes] for m in range(modes)]
+
+        def step(j, held):
+            now = flat[half, pl.ds(j, BLOCKS, stride=steps), :]
+            return tuple(p * h + now for p, h in zip(poles, held))
+
+        held = lax.fori_loop(0, steps, step, (jnp.zeros((BLOCKS, LANES), F32),) * modes, unroll=8)
+        for m in range(modes):
+            total_ref[m : m + 1, lanes] = jnp.sum(fades_ref[m, :, lanes] * held[m], axis=0, keepdims=True)
     copies = [pltpu.make_async_copy(total_ref, every_hbm.at[i], sent.at[i]) for i in range(every_hbm.shape[0])]
     for copy in copies:
         copy.start()
@@ -178,6 +190,7 @@
     flat_of = pltpu.VMEM(flat_shape, F32)
     half_of = pltpu.VMEM((rows, width), BF16)
     modal = pltpu.VMEM((modes, width), F32)
+    by_block = pltpu.VMEM((modes, BLOCKS, width), F32)
     sems = lambda count: pltpu.SemaphoreType.DMA((count,))
 
     by_step = (steps, 2 * BLOCKS, width)
@@ -188,7 +201,7 @@
         out_shape=shape((devices, modes, width)),
         in_specs=[ANY] * 3,
         out_specs=ANY,
-        scratch_shapes=[modal, flat_of, half_of, half_of, modal, sems(3), sems(devices)],
+        scratch_shapes=[modal, flat_of, half_of, half_of, modal, by_block, by_block, sems(3), sems(devices)],
     )(k_branch, v_branch, decay_rates)
     every = lax.all_to_all(every, seq, split_axis=0, concat_axis=0, tiled=True)
     local = kernel_call(

time: 107 us -> 107 us (level)
  no operation moved by 1% of the time
where the time goes in v6:
time: 107 us; the launch traced here: 106 us
  starting transfers between devices  79.3 us (74%)
  waiting for transfers between devices  11.1 us (10%)
  Pallas kernels  8.19 us (8%)
  matrix products  4.27 us (4%)
  local copies, waits for them, and re-layouts  1.91 us (2%)
    ppermute x17, starting transfers between devices, body(): hop = lambda array, pairs=ring: lax.ppermute(array, ('core', 'ch'), pairs)  65.5 us
    all_to_all x1, starting transfers between devices, body(): every = lax.all_to_all(every, seq, split_axis=0, concat_axis=0, tiled=True)  11.1 us
    all_to_all x1, waiting for transfers between devices, body(): every = lax.all_to_all(every, seq, split_axis=0, concat_axis=0, tiled=True)  6.72 us
    ppermute x17, waiting for transfers between devices, body(): hop = lambda array, pairs=ring: lax.ppermute(array, ('core', 'ch'), pairs)  4.42 us
    dot_general x18, matrix products, project(): return jnp.dot(array, weight, preferred_element_type=F32)  4.27 us
    pallas_call x1, Pallas kernels, body(): kernel_call(states_kernel, 'states', 2 * work, out_shape=shape((devices,...  3.25 us
    pallas_call x1, Pallas kernels, body(): kernel_call(local_kernel, 'local_convolution', 6 * work, limit=8 << 20, o...  3.03 us
  transfers between devices with their start and end apart: 20, of which 5 were waited for; matrix products, arithmetic and copies ran while one was open for 4% of the time, Pallas kernels for 3%

profile of v6, /device:TPU:1, one launch (start us, length us, event | category | flops | bytes accessed | tf_op | source)
XLA Modules:
  0.0 106.2 jit_solution(15288220170213441756)
XLA Ops:
  0.0 3.3 %states.1 = f32[32,16,256]{2,1,0:T(8,128)} custom-call(bf16[512,256]{1,0:T(8,128)(2,1)} %k_hbm.3, bf16[512,256]{1,0:T(8,128)(2,1)} %v_hbm.3, f32[16,256]{1,0:T(8,128)} %rates_ref.1), custom_call_target="tpu_custom_call" | custom-call | flops 4194304 | bytes 1048576 | tf_op jit(solution)/shard_map/states/pallas_call | solution.py:197
  3.3 11.1 %all-to-all-start = ((f32[32,16,256]{2,1,0:T(8,128)}), f32[32,16,256]{2,1,0:T(8,128)}, u32[]{:S(2)}, u32[]{:S(2)}) async-start(f32[32,16,256]{2,1,0:T(8,128)} %states.1), calls=%async_computation | async-start | bytes 1048576 | tf_op jit(solution)/shard_map/all_to_all | solution.py:206
  14.4 0.0 copy-start.2
  14.4 0.9 copy-done.2
  15.4 0.9 copy-done.3
  16.3 3.0 %local_convolution.1.local_ref = f32[64,16,256]{2,1,0:T(8,128)S(1)} custom-call(bf16[512,256]{1,0:T(8,128)(2,1)S(1)} %copy-done.1, bf16[512,256]{1,0:T(8,128)(2,1)S(1)} %copy-done.2, bf16[512,256]{1,0:T(8,128)(2,1)S(1)} %copy-done.3, f32[16,256]{1,0:T(8,128)S(1)} %copy-done.4, f32[16,256]{1,0:T(8,128)S(1)} %copy-done.5, f32[1,256]{1,0:T(1,128)S(1)} %bitcast.20), custom_call_target="tpu_custom_call" | custom-call | flops 12582912 | bytes 1048576 | tf_op jit(solution)/shard_map/local_convolution/pallas_call | solution.py:207
  19.4 6.7 %all-to-all-done.all_hbm = f32[32,16,256]{2,1,0:T(8,128)} async-done(((f32[32,16,256]{2,1,0:T(8,128)}), f32[32,16,256]{2,1,0:T(8,128)}, u32[]{:S(2)}, u32[]{:S(2)}) %all-to-all-start) | async-done | bytes 524320 | tf_op jit(solution)/shard_map/all_to_all | solution.py:206
  26.1 1.9 %carry_and_gate.1 = bf16[512,256]{1,0:T(8,128)(2,1)S(1)} custom-call(s32[1]{0:T(128)} %bitcast.at_ref, f32[32,16,256]{2,1,0:T(8,128)} %all-to-all-done.all_hbm, f32[16,256]{1,0:T(8,128)S(1)} %copy-done.4, f32[16,256]{1,0:T(8,128)S(1)} %copy-done.5, f32[64,16,256]{2,1,0:T(8,128)S(1)} %local_convolution.1.local_ref), custom_call_target="tpu_custom_call" | custom-call | flops 4194304 | bytes 1048576 | tf_op jit(solution)/shard_map/carry_and_gate/pallas_call | solution.py:218
  28.0 8.6 %collective-permute-start = (bf16[512,256]{1,0:T(8,128)(2,1)S(1)}, bf16[512,256]{1,0:T(8,128)(2,1)S(1)}, u32[]{:S(2)}, u32[]{:S(2)}) collective-permute-start(bf16[512,256]{1,0:T(8,128)(2,1)S(1)} %carry_and_gate.1), channel_id=1, source_target_pairs={{0,1},{1,2},{2,3},{3,4},{4,5},{5,6},{6,7},{7,8},{8,9},{9,10},{10,1... | collective-permute-start | bytes 786440 | tf_op jit(solution)/shard_map/ppermute | solution.py:234
  36.6 1.9 %collective-permute-start.2 = (bf16[512,256]{1,0:T(8,128)(2,1)S(1)}, bf16[512,256]{1,0:T(8,128)(2,1)S(1)}, u32[]{:S(2)}, u32[]{:S(2)}) collective-permute-start(bf16[512,256]{1,0:T(8,128)(2,1)S(1)} %carry_and_gate.1), channel_id=1, source_target_pairs={{16,1},{17,2},{18,3},{19,4},{20,5},{21,6},{22,7},{23,8},{24,9},{25... | collective-permute-start | bytes 786440 | tf_op jit(solution)/shard_map/ppermute | solution.py:234
  38.5 1.4 %collective-permute-done = bf16[512,256]{1,0:T(8,128)(2,1)S(1)} collective-permute-done((bf16[512,256]{1,0:T(8,128)(2,1)S(1)}, bf16[512,256]{1,0:T(8,128)(2,1)S(1)}, u32[]{:S(2)}, u32[]{:S(2)}) %collective-permute-start) | collective-permute-done | bytes 262176 | tf_op jit(solution)/shard_map/ppermute | solution.py:234
  39.9 5.0 %collective-permute-start.1 = (bf16[512,256]{1,0:T(8,128)(2,1)S(1)}, bf16[512,256]{1,0:T(8,128)(2,1)S(1)}, u32[]{:S(2)}, u32[]{:S(2)}) collective-permute-start(bf16[512,256]{1,0:T(8,128)(2,1)S(1)} %collective-permute-done), channel_id=1, source_target_pairs={{0,1},{1,2},{2,3},{3,4},{4,5},{5,6},{6,7},{7,8},{8,9},{9,10},{10,1... | collective-permute-start | bytes 786440 | tf_op jit(solution)/shard_map/ppermute | solution.py:234
  44.9 0.0 collective-permute-done.2
  44.9 3.2 %collective-permute-start.4 = (bf16[512,256]{1,0:T(8,128)(2,1)S(1)}, bf16[512,256]{1,0:T(8,128)(2,1)S(1)}, u32[]{:S(2)}, u32[]{:S(2)}) collective-permute-start(bf16[512,256]{1,0:T(8,128)(2,1)S(1)} %collective-permute-done.2), channel_id=1, source_target_pairs={{0,1},{1,2},{2,3},{3,4},{4,5},{5,6},{6,7},{7,8},{8,9},{9,10},{10,1... | collective-permute-start | bytes 786440 | tf_op jit(solution)/shard_map/ppermute | solution.py:234
  48.2 0.2 fusion.13
  48.5 0.0 collective-permute-done.1
  48.5 4.8 %collective-permute-start.3 = (bf16[512,256]{1,0:T(8,128)(2,1)S(1)}, bf16[512,256]{1,0:T(8,128)(2,1)S(1)}, u32[]{:S(2)}, u32[]{:S(2)}) collective-permute-start(bf16[512,256]{1,0:T(8,128)(2,1)S(1)} %collective-permute-done.1), channel_id=1, source_target_pairs={{0,1},{1,2},{2,3},{3,4},{4,5},{5,6},{6,7},{7,8},{8,9},{9,10},{10,1... | collective-permute-start | bytes 786440 | tf_op jit(solution)/shard_map/ppermute | solution.py:234
  53.2 0.0 collective-permute-done.4
  53.2 3.2 %collective-permute-start.6 = (bf16[512,256]{1,0:T(8,128)(2,1)S(1)}, bf16[512,256]{1,0:T(8,128)(2,1)S(1)}, u32[]{:S(2)}, u32[]{:S(2)}) collective-permute-start(bf16[512,256]{1,0:T(8,128)(2,1)S(1)} %collective-permute-done.4), channel_id=1, source_target_pairs={{0,1},{1,2},{2,3},{3,4},{4,5},{5,6},{6,7},{7,8},{8,9},{9,10},{10,1... | collective-permute-start | bytes 786440 | tf_op jit(solution)/shard_map/ppermute | solution.py:234
  56.4 0.2 convolution_add_fusion.4
  56.7 0.2 fusion.37
  56.9 0.0 collective-permute-done.3
  56.9 4.6 %collective-permute-start.5 = (bf16[512,256]{1,0:T(8,128)(2,1)S(1)}, bf16[512,256]{1,0:T(8,128)(2,1)S(1)}, u32[]{:S(2)}, u32[]{:S(2)}) collective-permute-start(bf16[512,256]{1,0:T(8,128)(2,1)S(1)} %collective-permute-done.3), channel_id=1, source_target_pairs={{0,1},{1,2},{2,3},{3,4},{4,5},{5,6},{6,7},{7,8},{8,9},{9,10},{10,1... | collective-permute-start | bytes 786440 | tf_op jit(solution)/shard_map/ppermute | solution.py:234
  61.5 0.0 collective-permute-done.6
  61.6 3.2 %collective-permute-start.8 = (bf16[512,256]{1,0:T(8,128)(2,1)S(1)}, bf16[512,256]{1,0:T(8,128)(2,1)S(1)}, u32[]{:S(2)}, u32[]{:S(2)}) collective-permute-start(bf16[512,256]{1,0:T(8,128)(2,1)S(1)} %collective-permute-done.6), channel_id=1, source_target_pairs={{0,1},{1,2},{2,3},{3,4},{4,5},{5,6},{6,7},{7,8},{8,9},{9,10},{10,1... | collective-permute-start | bytes 786440 | tf_op jit(solution)/shard_map/ppermute | solution.py:234
  64.8 0.2 fusion.35
  65.0 0.2 fusion.33
  65.2 0.0 collective-permute-done.5
  65.2 4.6 %collective-permute-start.7 = (bf16[512,256]{1,0:T(8,128)(2,1)S(1)}, bf16[512,256]{1,0:T(8,128)(2,1)S(1)}, u32[]{:S(2)}, u32[]{:S(2)}) collective-permute-start(bf16[512,256]{1,0:T(8,128)(2,1)S(1)} %collective-permute-done.5), channel_id=1, source_target_pairs={{0,1},{1,2},{2,3},{3,4},{4,5},{5,6},{6,7},{7,8},{8,9},{9,10},{10,1... | collective-permute-start | bytes 786440 | tf_op jit(solution)/shard_map/ppermute | solution.py:234
  69.9 0.0 collective-permute-done.8
  69.9 3.2 %collective-permute-start.10 = (bf16[512,256]{1,0:T(8,128)(2,1)S(1)}, bf16[512,256]{1,0:T(8,128)(2,1)S(1)}, u32[]{:S(2)}, u32[]{:S(2)}) collective-permute-start(bf16[512,256]{1,0:T(8,128)(2,1)S(1)} %collective-permute-done.8), channel_id=1, source_target_pairs={{0,1},{1,2},{2,3},{3,4},{4,5},{5,6},{6,7},{7,8},{8,9},{9,10},{10,1... | collective-permute-start | bytes 786440 | tf_op jit(solution)/shard_map/ppermute | solution.py:234
  73.1 0.2 fusion.31
  73.3 0.2 fusion.29
  73.5 0.0 collective-permute-done.7
  73.6 4.6 %collective-permute-start.9 = (bf16[512,256]{1,0:T(8,128)(2,1)S(1)}, bf16[512,256]{1,0:T(8,128)(2,1)S(1)}, u32[]{:S(2)}, u32[]{:S(2)}) collective-permute-start(bf16[512,256]{1,0:T(8,128)(2,1)S(1)} %collective-permute-done.7), channel_id=1, source_target_pairs={{0,1},{1,2},{2,3},{3,4},{4,5},{5,6},{6,7},{7,8},{8,9},{9,10},{10,1... | collective-permute-start | bytes 786440 | tf_op jit(solution)/shard_map/ppermute | solution.py:234
  78.2 0.0 collective-permute-done.10
  78.2 3.2 %collective-permute-start.12 = (bf16[512,256]{1,0:T(8,128)(2,1)S(1)}, bf16[512,256]{1,0:T(8,128)(2,1)S(1)}, u32[]{:S(2)}, u32[]{:S(2)}) collective-permute-start(bf16[512,256]{1,0:T(8,128)(2,1)S(1)} %collective-permute-done.10), channel_id=1, source_target_pairs={{0,1},{1,2},{2,3},{3,4},{4,5},{5,6},{6,7},{7,8},{8,9},{9,10},{10,1... | collective-permute-start | bytes 786440 | tf_op jit(solution)/shard_map/ppermute | solution.py:234
  81.4 0.2 fusion.27
  81.6 0.2 fusion.25
  81.9 0.0 collective-permute-done.9
  81.9 4.6 %collective-permute-start.11 = (bf16[512,256]{1,0:T(8,128)(2,1)S(1)}, bf16[512,256]{1,0:T(8,128)(2,1)S(1)}, u32[]{:S(2)}, u32[]{:S(2)}) collective-permute-start(bf16[512,256]{1,0:T(8,128)(2,1)S(1)} %collective-permute-done.9), channel_id=1, source_target_pairs={{0,1},{1,2},{2,3},{3,4},{4,5},{5,6},{6,7},{7,8},{8,9},{9,10},{10,1... | collective-permute-start | bytes 786440 | tf_op jit(solution)/shard_map/ppermute | solution.py:234
  86.5 0.0 collective-permute-done.12
  86.5 3.2 %collective-permute-start.16 = (bf16[512,256]{1,0:T(8,128)(2,1)S(1)}, bf16[512,256]{1,0:T(8,128)(2,1)S(1)}, u32[]{:S(2)}, u32[]{:S(2)}) collective-permute-start(bf16[512,256]{1,0:T(8,128)(2,1)S(1)} %collective-permute-done.12), channel_id=1, source_target_pairs={{16,31},{17,16},{18,17},{19,18},{20,19},{21,20},{22,21},{23,22},{2... | collective-permute-start | bytes 786440 | tf_op jit(solution)/shard_map/ppermute | solution.py:234
  89.7 1.3 %collective-permute-start.13 = (bf16[512,256]{1,0:T(8,128)(2,1)S(1)}, bf16[512,256]{1,0:T(8,128)(2,1)S(1)}, u32[]{:S(2)}, u32[]{:S(2)}) collective-permute-start(bf16[512,256]{1,0:T(8,128)(2,1)S(1)} %collective-permute-done.12), channel_id=1, source_target_pairs={{0,17},{1,18},{2,19},{3,20},{4,21},{5,22},{6,23},{7,24},{8,25},{9,... | collective-permute-start | bytes 786440 | tf_op jit(solution)/shard_map/ppermute | solution.py:234
  91.0 0.2 fusion.21
  91.2 0.3 fusion.4
  91.5 0.2 fusion.23
  91.8 1.3 %collective-permute-start.15 = (f32[512,256]{1,0:T(8,128)S(1)}, f32[512,256]{1,0:T(8,128)S(1)}, u32[]{:S(2)}, u32[]{:S(2)}) collective-permute-start(f32[512,256]{1,0:T(8,128)S(1)} %fusion.4), channel_id=1, source_target_pairs={{0,16},{1,17},{2,18},{3,19},{4,20},{5,21},{6,22},{7,23},{8,24},{9,... | collective-permute-start | bytes 1572872 | tf_op jit(solution)/shard_map/ppermute | solution.py:260
  93.1 0.6 collective-permute-done.16
  93.6 0.0 collective-permute-done.11
  93.6 4.4 %collective-permute-start.17 = (bf16[512,256]{1,0:T(8,128)(2,1)S(1)}, bf16[512,256]{1,0:T(8,128)(2,1)S(1)}, u32[]{:S(2)}, u32[]{:S(2)}) collective-permute-start(bf16[512,256]{1,0:T(8,128)(2,1)S(1)} %collective-permute-done.16), channel_id=1, source_target_pairs={{16,31},{17,16},{18,17},{19,18},{20,19},{21,20},{22,21},{23,22},{2... | collective-permute-start | bytes 786440 | tf_op jit(solution)/shard_map/ppermute | solution.py:234
  98.0 1.9 %collective-permute-start.14 = (bf16[512,256]{1,0:T(8,128)(2,1)S(1)}, bf16[512,256]{1,0:T(8,128)(2,1)S(1)}, u32[]{:S(2)}, u32[]{:S(2)}) collective-permute-start(bf16[512,256]{1,0:T(8,128)(2,1)S(1)} %collective-permute-done.11), channel_id=1, source_target_pairs={{16,31},{17,16},{18,17},{19,18},{20,19},{21,20},{22,21},{23,22},{2... | collective-permute-start | bytes 786440 | tf_op jit(solution)/shard_map/ppermute | solution.py:234
  100.0 0.2 fusion.19
  100.2 1.1 %collective-permute-done.13 = bf16[512,256]{1,0:T(8,128)(2,1)S(1)} collective-permute-done((bf16[512,256]{1,0:T(8,128)(2,1)S(1)}, bf16[512,256]{1,0:T(8,128)(2,1)S(1)}, u32[]{:S(2)}, u32[]{:S(2)}) %collective-permute-start.13) | collective-permute-done | bytes 262176 | tf_op jit(solution)/shard_map/ppermute | solution.py:234
  101.3 0.2 fusion.11
  101.5 0.0 collective-permute-done.17
  101.5 0.2 fusion.15
  101.8 0.3 fusion
  102.0 1.4 %collective-permute-start.18 = (f32[512,256]{1,0:T(8,128)S(1)}, f32[512,256]{1,0:T(8,128)S(1)}, u32[]{:S(2)}, u32[]{:S(2)}) collective-permute-start(f32[512,256]{1,0:T(8,128)S(1)} %fusion), channel_id=1, source_target_pairs={{16,0},{17,1},{18,2},{19,3},{20,4},{21,5},{22,6},{23,7},{24,8},{25... | collective-permute-start | bytes 1572872 | tf_op jit(solution)/shard_map/ppermute | solution.py:267
  103.5 0.3 fusion.10
  103.8 1.4 %collective-permute-done.14 = bf16[512,256]{1,0:T(8,128)(2,1)S(1)} collective-permute-done((bf16[512,256]{1,0:T(8,128)(2,1)S(1)}, bf16[512,256]{1,0:T(8,128)(2,1)S(1)}, u32[]{:S(2)}, u32[]{:S(2)}) %collective-permute-start.14) | collective-permute-done | bytes 262176 | tf_op jit(solution)/shard_map/ppermute | solution.py:234
  105.1 0.2 convolution_add_fusion.2
  105.4 0.0 collective-permute-done.15
  105.4 0.8 add_convert_fusion
  (12 shorter events, 0.0 us)
Async XLA Ops:
  0.0 48.2 %copy-start = (bf16[4096,256]{1,0:T(8,128)(2,1)S(1)}, bf16[4096,256]{1,0:T(8,128)(2,1)}, u32[]{:S(2)}) copy-start(bf16[4096,256]{1,0:T(8,128)(2,1)} %param.13) | copy-start | bytes 6291460
  0.0 14.4 %copy-start.4 = (f32[16,256]{1,0:T(8,128)S(1)}, f32[16,256]{1,0:T(8,128)}, u32[]{:S(2)}) copy-start(f32[16,256]{1,0:T(8,128)} %rates_ref.1) | copy-start | bytes 49156
  0.0 14.4 %copy-start.1 = (bf16[512,256]{1,0:T(8,128)(2,1)S(1)}, bf16[512,256]{1,0:T(8,128)(2,1)}, u32[]{:S(2)}) copy-start(bf16[512,256]{1,0:T(8,128)(2,1)} %k_hbm.3) | copy-start | bytes 786436
  0.0 14.4 %copy-start.6 = (f32[256]{0:T(256)S(1)}, f32[256]{0:T(256)}, u32[]{:S(2)}) copy-start(f32[256]{0:T(256)} %param.12) | copy-start | bytes 3076
  0.0 14.4 %copy-start.5 = (f32[16,256]{1,0:T(8,128)S(1)}, f32[16,256]{1,0:T(8,128)}, u32[]{:S(2)}) copy-start(f32[16,256]{1,0:T(8,128)} %resid_ref.1) | copy-start | bytes 49156
  3.3 22.8 %all-to-all-start = ((f32[32,16,256]{2,1,0:T(8,128)}), f32[32,16,256]{2,1,0:T(8,128)}, u32[]{:S(2)}, u32[]{:S(2)}) async-start(f32[32,16,256]{2,1,0:T(8,128)} %states.1), calls=%async_computation | async-start | bytes 1048576 | tf_op jit(solution)/shard_map/all_to_all | solution.py:206
  14.4 1.0 copy-start.2
  15.4 0.9 copy-start.3
  28.0 11.9 %collective-permute-start = (bf16[512,256]{1,0:T(8,128)(2,1)S(1)}, bf16[512,256]{1,0:T(8,128)(2,1)S(1)}, u32[]{:S(2)}, u32[]{:S(2)}) collective-permute-start(bf16[512,256]{1,0:T(8,128)(2,1)S(1)} %carry_and_gate.1), channel_id=1, source_target_pairs={{0,1},{1,2},{2,3},{3,4},{4,5},{5,6},{6,7},{7,8},{8,9},{9,10},{10,1... | collective-permute-start | bytes 786440 | tf_op jit(solution)/shard_map/ppermute | solution.py:234
  36.6 8.3 %collective-permute-start.2 = (bf16[512,256]{1,0:T(8,128)(2,1)S(1)}, bf16[512,256]{1,0:T(8,128)(2,1)S(1)}, u32[]{:S(2)}, u32[]{:S(2)}) collective-permute-start(bf16[512,256]{1,0:T(8,128)(2,1)S(1)} %carry_and_gate.1), channel_id=1, source_target_pairs={{16,1},{17,2},{18,3},{19,4},{20,5},{21,6},{22,7},{23,8},{24,9},{25... | collective-permute-start | bytes 786440 | tf_op jit(solution)/shard_map/ppermute | solution.py:234
  39.9 8.6 %collective-permute-start.1 = (bf16[512,256]{1,0:T(8,128)(2,1)S(1)}, bf16[512,256]{1,0:T(8,128)(2,1)S(1)}, u32[]{:S(2)}, u32[]{:S(2)}) collective-permute-start(bf16[512,256]{1,0:T(8,128)(2,1)S(1)} %collective-permute-done), channel_id=1, source_target_pairs={{0,1},{1,2},{2,3},{3,4},{4,5},{5,6},{6,7},{7,8},{8,9},{9,10},{10,1... | collective-permute-start | bytes 786440 | tf_op jit(solution)/shard_map/ppermute | solution.py:234
  44.9 8.3 %collective-permute-start.4 = (bf16[512,256]{1,0:T(8,128)(2,1)S(1)}, bf16[512,256]{1,0:T(8,128)(2,1)S(1)}, u32[]{:S(2)}, u32[]{:S(2)}) collective-permute-start(bf16[512,256]{1,0:T(8,128)(2,1)S(1)} %collective-permute-done.2), channel_id=1, source_target_pairs={{0,1},{1,2},{2,3},{3,4},{4,5},{5,6},{6,7},{7,8},{8,9},{9,10},{10,1... | collective-permute-start | bytes 786440 | tf_op jit(solution)/shard_map/ppermute | solution.py:234
  48.5 8.5 %collective-permute-start.3 = (bf16[512,256]{1,0:T(8,128)(2,1)S(1)}, bf16[512,256]{1,0:T(8,128)(2,1)S(1)}, u32[]{:S(2)}, u32[]{:S(2)}) collective-permute-start(bf16[512,256]{1,0:T(8,128)(2,1)S(1)} %collective-permute-done.1), channel_id=1, source_target_pairs={{0,1},{1,2},{2,3},{3,4},{4,5},{5,6},{6,7},{7,8},{8,9},{9,10},{10,1... | collective-permute-start | bytes 786440 | tf_op jit(solution)/shard_map/ppermute | solution.py:234
  53.2 8.3 %collective-permute-start.6 = (bf16[512,256]{1,0:T(8,128)(2,1)S(1)}, bf16[512,256]{1,0:T(8,128)(2,1)S(1)}, u32[]{:S(2)}, u32[]{:S(2)}) collective-permute-start(bf16[512,256]{1,0:T(8,128)(2,1)S(1)} %collective-permute-done.4), channel_id=1, source_target_pairs={{0,1},{1,2},{2,3},{3,4},{4,5},{5,6},{6,7},{7,8},{8,9},{9,10},{10,1... | collective-permute-start | bytes 786440 | tf_op jit(solution)/shard_map/ppermute | solution.py:234
  56.9 8.3 %collective-permute-start.5 = (bf16[512,256]{1,0:T(8,128)(2,1)S(1)}, bf16[512,256]{1,0:T(8,128)(2,1)S(1)}, u32[]{:S(2)}, u32[]{:S(2)}) collective-permute-start(bf16[512,256]{1,0:T(8,128)(2,1)S(1)} %collective-permute-done.3), channel_id=1, source_target_pairs={{0,1},{1,2},{2,3},{3,4},{4,5},{5,6},{6,7},{7,8},{8,9},{9,10},{10,1... | collective-permute-start | bytes 786440 | tf_op jit(solution)/shard_map/ppermute | solution.py:234
  61.6 8.3 %collective-permute-start.8 = (bf16[512,256]{1,0:T(8,128)(2,1)S(1)}, bf16[512,256]{1,0:T(8,128)(2,1)S(1)}, u32[]{:S(2)}, u32[]{:S(2)}) collective-permute-start(bf16[512,256]{1,0:T(8,128)(2,1)S(1)} %collective-permute-done.6), channel_id=1, source_target_pairs={{0,1},{1,2},{2,3},{3,4},{4,5},{5,6},{6,7},{7,8},{8,9},{9,10},{10,1... | collective-permute-start | bytes 786440 | tf_op jit(solution)/shard_map/ppermute | solution.py:234
  65.2 8.3 %collective-permute-start.7 = (bf16[512,256]{1,0:T(8,128)(2,1)S(1)}, bf16[512,256]{1,0:T(8,128)(2,1)S(1)}, u32[]{:S(2)}, u32[]{:S(2)}) collective-permute-start(bf16[512,256]{1,0:T(8,128)(2,1)S(1)} %collective-permute-done.5), channel_id=1, source_target_pairs={{0,1},{1,2},{2,3},{3,4},{4,5},{5,6},{6,7},{7,8},{8,9},{9,10},{10,1... | collective-permute-start | bytes 786440 | tf_op jit(solution)/shard_map/ppermute | solution.py:234
  69.9 8.3 %collective-permute-start.10 = (bf16[512,256]{1,0:T(8,128)(2,1)S(1)}, bf16[512,256]{1,0:T(8,128)(2,1)S(1)}, u32[]{:S(2)}, u32[]{:S(2)}) collective-permute-start(bf16[512,256]{1,0:T(8,128)(2,1)S(1)} %collective-permute-done.8), channel_id=1, source_target_pairs={{0,1},{1,2},{2,3},{3,4},{4,5},{5,6},{6,7},{7,8},{8,9},{9,10},{10,1... | collective-permute-start | bytes 786440 | tf_op jit(solution)/shard_map/ppermute | solution.py:234
  73.6 8.3 %collective-permute-start.9 = (bf16[512,256]{1,0:T(8,128)(2,1)S(1)}, bf16[512,256]{1,0:T(8,128)(2,1)S(1)}, u32[]{:S(2)}, u32[]{:S(2)}) collective-permute-start(bf16[512,256]{1,0:T(8,128)(2,1)S(1)} %collective-permute-done.7), channel_id=1, source_target_pairs={{0,1},{1,2},{2,3},{3,4},{4,5},{5,6},{6,7},{7,8},{8,9},{9,10},{10,1... | collective-permute-start | bytes 786440 | tf_op jit(solution)/shard_map/ppermute | solution.py:234
  78.2 8.3 %collective-permute-start.12 = (bf16[512,256]{1,0:T(8,128)(2,1)S(1)}, bf16[512,256]{1,0:T(8,128)(2,1)S(1)}, u32[]{:S(2)}, u32[]{:S(2)}) collective-permute-start(bf16[512,256]{1,0:T(8,128)(2,1)S(1)} %collective-permute-done.10), channel_id=1, source_target_pairs={{0,1},{1,2},{2,3},{3,4},{4,5},{5,6},{6,7},{7,8},{8,9},{9,10},{10,1... | collective-permute-start | bytes 786440 | tf_op jit(solution)/shard_map/ppermute | solution.py:234
  81.9 11.8 %collective-permute-start.11 = (bf16[512,256]{1,0:T(8,128)(2,1)S(1)}, bf16[512,256]{1,0:T(8,128)(2,1)S(1)}, u32[]{:S(2)}, u32[]{:S(2)}) collective-permute-start(bf16[512,256]{1,0:T(8,128)(2,1)S(1)} %collective-permute-done.9), channel_id=1, source_target_pairs={{0,1},{1,2},{2,3},{3,4},{4,5},{5,6},{6,7},{7,8},{8,9},{9,10},{10,1... | collective-permute-start | bytes 786440 | tf_op jit(solution)/shard_map/ppermute | solution.py:234
  86.5 7.1 %collective-permute-start.16 = (bf16[512,256]{1,0:T(8,128)(2,1)S(1)}, bf16[512,256]{1,0:T(8,128)(2,1)S(1)}, u32[]{:S(2)}, u32[]{:S(2)}) collective-permute-start(bf16[512,256]{1,0:T(8,128)(2,1)S(1)} %collective-permute-done.12), channel_id=1, source_target_pairs={{16,31},{17,16},{18,17},{19,18},{20,19},{21,20},{22,21},{23,22},{2... | collective-permute-start | bytes 786440 | tf_op jit(solution)/shard_map/ppermute | solution.py:234
  89.7 11.6 %collective-permute-start.13 = (bf16[512,256]{1,0:T(8,128)(2,1)S(1)}, bf16[512,256]{1,0:T(8,128)(2,1)S(1)}, u32[]{:S(2)}, u32[]{:S(2)}) collective-permute-start(bf16[512,256]{1,0:T(8,128)(2,1)S(1)} %collective-permute-done.12), channel_id=1, source_target_pairs={{0,17},{1,18},{2,19},{3,20},{4,21},{5,22},{6,23},{7,24},{8,25},{9,... | collective-permute-start | bytes 786440 | tf_op jit(solution)/shard_map/ppermute | solution.py:234
  91.8 13.6 %collective-permute-start.15 = (f32[512,256]{1,0:T(8,128)S(1)}, f32[512,256]{1,0:T(8,128)S(1)}, u32[]{:S(2)}, u32[]{:S(2)}) collective-permute-start(f32[512,256]{1,0:T(8,128)S(1)} %fusion.4), channel_id=1, source_target_pairs={{0,16},{1,17},{2,18},{3,19},{4,20},{5,21},{6,22},{7,23},{8,24},{9,... | collective-permute-start | bytes 1572872 | tf_op jit(solution)/shard_map/ppermute | solution.py:260
  93.6 7.9 %collective-permute-start.17 = (bf16[512,256]{1,0:T(8,128)(2,1)S(1)}, bf16[512,256]{1,0:T(8,128)(2,1)S(1)}, u32[]{:S(2)}, u32[]{:S(2)}) collective-permute-start(bf16[512,256]{1,0:T(8,128)(2,1)S(1)} %collective-permute-done.16), channel_id=1, source_target_pairs={{16,31},{17,16},{18,17},{19,18},{20,19},{21,20},{22,21},{23,22},{2... | collective-permute-start | bytes 786440 | tf_op jit(solution)/shard_map/ppermute | solution.py:234
  98.0 7.1 %collective-permute-start.14 = (bf16[512,256]{1,0:T(8,128)(2,1)S(1)}, bf16[512,256]{1,0:T(8,128)(2,1)S(1)}, u32[]{:S(2)}, u32[]{:S(2)}) collective-permute-start(bf16[512,256]{1,0:T(8,128)(2,1)S(1)} %collective-permute-done.11), channel_id=1, source_target_pairs={{16,31},{17,16},{18,17},{19,18},{20,19},{21,20},{22,21},{23,22},{2... | collective-permute-start | bytes 786440 | tf_op jit(solution)/shard_map/ppermute | solution.py:234
  102.0 3.4 %collective-permute-start.18 = (f32[512,256]{1,0:T(8,128)S(1)}, f32[512,256]{1,0:T(8,128)S(1)}, u32[]{:S(2)}, u32[]{:S(2)}) collective-permute-start(f32[512,256]{1,0:T(8,128)S(1)} %fusion), channel_id=1, source_target_pairs={{16,0},{17,1},{18,2},{19,3},{20,4},{21,5},{22,6},{23,7},{24,8},{25... | collective-permute-start | bytes 1572872 | tf_op jit(solution)/shard_map/ppermute | solution.py:267

commit v7 on v5

--- a/solution.py
+++ b/solution.py
@@ -239,22 +239,20 @@
         sum_own = sum_own + project(own, distance)
         sum_oth = sum_oth + project(oth, distance)
     far = depth // 2
-    early = sum_oth
     last_own = own
     own = hop(own)
     oth, last_own = lax.optimization_barrier((oth, last_own))
     oth, from_up = hop(oth, ring[depth:]), hop(oth, across[:depth])
-    early = lax.ppermute(early, "core", [(0, 1)])
     sum_own = sum_own + project(own, far - 1)
     sum_oth = sum_oth + project(oth, far - 1)
     last_own, own = own, hop(own, ring[depth:])
     oth, last_own = lax.optimization_barrier((oth, last_own))
     oth = hop(oth, ring[depth:])
     sum_oth = sum_oth + project(oth, far)
-    late = lax.ppermute(sum_oth, "core", [(1, 0)])
+    swapped = lax.ppermute(sum_oth, "core", [(0, 1), (1, 0)])
     sum_own = sum_own + project(from_up, 1 - far) + project(own, far)
-    sum_own, early, late = lax.optimization_barrier((sum_own, early, late))
-    return (sum_own + (early + late)).astype(BF16)
+    sum_own, swapped = lax.optimization_barrier((sum_own, swapped))
+    return (sum_own + swapped).astype(BF16)
 
 
 def solution(mesh):

time: 107 us -> 109 us (1.019)
  waiting for transfers between devices: 11.1 us -> 13.5 us
    ppermute x17, waiting for transfers between devices: 4.4 us -> 6.49 us  [body(): hop = lambda array, pairs=ring: lax.ppermute(array, ('core', 'ch'), pairs)]
    ppermute x2 -> x1, starting transfers between devices: 2.72 us -> 1.92 us  [body(): swapped = lax.ppermute(sum_oth, 'core', [(0, 1), (1, 0)])]
  transfers between devices with their start and end apart: 20 -> 19, of which waited for: 5 -> 6; matrix products, arithmetic and copies ran while one was open for 4% -> 4% of each run, Pallas kernels for 3% -> 3%
where the time goes in v7:
time: 109 us; the launch traced here: 108 us
  starting transfers between devices  78.5 us (72%)
  waiting for transfers between devices  13.5 us (12%)
  Pallas kernels  8.23 us (8%)
  matrix products  4.28 us (4%)
  local copies, waits for them, and re-layouts  1.91 us (2%)
    ppermute x17, starting transfers between devices, body(): hop = lambda array, pairs=ring: lax.ppermute(array, ('core', 'ch'), pairs)  65.5 us
    all_to_all x1, starting transfers between devices, body(): every = lax.all_to_all(every, seq, split_axis=0, concat_axis=0, tiled=True)  11.1 us
    all_to_all x1, waiting for transfers between devices, body(): every = lax.all_to_all(every, seq, split_axis=0, concat_axis=0, tiled=True)  6.72 us
    ppermute x17, waiting for transfers between devices, body(): hop = lambda array, pairs=ring: lax.ppermute(array, ('core', 'ch'), pairs)  6.49 us
    dot_general x18, matrix products, project(): return jnp.dot(array, weight, preferred_element_type=F32)  4.28 us
    pallas_call x1, Pallas kernels, body(): kernel_call(states_kernel, 'states', 2 * work, out_shape=shape((devices,...  3.3 us
    pallas_call x1, Pallas kernels, body(): kernel_call(local_kernel, 'local_convolution', 6 * work, limit=8 << 20, o...  3.03 us
  transfers between devices with their start and end apart: 19, of which 6 were waited for; matrix products, arithmetic and copies ran while one was open for 4% of the time, Pallas kernels for 3%

profile of v7, /device:TPU:1, one launch (start us, length us, event | category | flops | bytes accessed | tf_op | source)
XLA Modules:
  0.0 107.8 jit_solution(13632353570879288785)
XLA Ops:
  0.0 3.3 %states.1 = f32[32,16,256]{2,1,0:T(8,128)} custom-call(bf16[512,256]{1,0:T(8,128)(2,1)} %k_hbm.3, bf16[512,256]{1,0:T(8,128)(2,1)} %v_hbm.3, f32[16,256]{1,0:T(8,128)} %rates_ref.1), custom_call_target="tpu_custom_call" | custom-call | flops 4194304 | bytes 1048576 | tf_op jit(solution)/shard_map/states/pallas_call | solution.py:184
  3.3 11.1 %all-to-all-start = ((f32[32,16,256]{2,1,0:T(8,128)}), f32[32,16,256]{2,1,0:T(8,128)}, u32[]{:S(2)}, u32[]{:S(2)}) async-start(f32[32,16,256]{2,1,0:T(8,128)} %states.1), calls=%async_computation | async-start | bytes 1048576 | tf_op jit(solution)/shard_map/all_to_all | solution.py:193
  14.4 0.0 copy-done.1
  14.5 0.0 copy-start.2
  14.5 0.9 copy-done.2
  15.4 0.9 copy-done.3
  16.4 3.0 %local_convolution.1.local_ref = f32[64,16,256]{2,1,0:T(8,128)S(1)} custom-call(bf16[512,256]{1,0:T(8,128)(2,1)S(1)} %copy-done.1, bf16[512,256]{1,0:T(8,128)(2,1)S(1)} %copy-done.2, bf16[512,256]{1,0:T(8,128)(2,1)S(1)} %copy-done.3, f32[16,256]{1,0:T(8,128)S(1)} %copy-done.4, f32[16,256]{1,0:T(8,128)S(1)} %copy-done.5, f32[1,256]{1,0:T(1,128)S(1)} %bitcast.20), custom_call_target="tpu_custom_call" | custom-call | flops 12582912 | bytes 1048576 | tf_op jit(solution)/shard_map/local_convolution/pallas_call | solution.py:194
  19.4 6.7 %all-to-all-done.all_hbm = f32[32,16,256]{2,1,0:T(8,128)} async-done(((f32[32,16,256]{2,1,0:T(8,128)}), f32[32,16,256]{2,1,0:T(8,128)}, u32[]{:S(2)}, u32[]{:S(2)}) %all-to-all-start) | async-done | bytes 524320 | tf_op jit(solution)/shard_map/all_to_all | solution.py:193
  26.1 1.9 %carry_and_gate.1 = bf16[512,256]{1,0:T(8,128)(2,1)S(1)} custom-call(s32[1]{0:T(128)} %bitcast.at_ref, f32[32,16,256]{2,1,0:T(8,128)} %all-to-all-done.all_hbm, f32[16,256]{1,0:T(8,128)S(1)} %copy-done.4, f32[16,256]{1,0:T(8,128)S(1)} %copy-done.5, f32[64,16,256]{2,1,0:T(8,128)S(1)} %local_convolution.1.local_ref), custom_call_target="tpu_custom_call" | custom-call | flops 4194304 | bytes 1048576 | tf_op jit(solution)/shard_map/carry_and_gate/pallas_call | solution.py:205
  28.0 8.6 %collective-permute-start = (bf16[512,256]{1,0:T(8,128)(2,1)S(1)}, bf16[512,256]{1,0:T(8,128)(2,1)S(1)}, u32[]{:S(2)}, u32[]{:S(2)}) collective-permute-start(bf16[512,256]{1,0:T(8,128)(2,1)S(1)} %carry_and_gate.1), channel_id=1, source_target_pairs={{0,1},{1,2},{2,3},{3,4},{4,5},{5,6},{6,7},{7,8},{8,9},{9,10},{10,1... | collective-permute-start | bytes 786440 | tf_op jit(solution)/shard_map/ppermute | solution.py:221
  36.6 1.9 %collective-permute-start.2 = (bf16[512,256]{1,0:T(8,128)(2,1)S(1)}, bf16[512,256]{1,0:T(8,128)(2,1)S(1)}, u32[]{:S(2)}, u32[]{:S(2)}) collective-permute-start(bf16[512,256]{1,0:T(8,128)(2,1)S(1)} %carry_and_gate.1), channel_id=1, source_target_pairs={{16,1},{17,2},{18,3},{19,4},{20,5},{21,6},{22,7},{23,8},{24,9},{25... | collective-permute-start | bytes 786440 | tf_op jit(solution)/shard_map/ppermute | solution.py:221
  38.6 1.4 %collective-permute-done = bf16[512,256]{1,0:T(8,128)(2,1)S(1)} collective-permute-done((bf16[512,256]{1,0:T(8,128)(2,1)S(1)}, bf16[512,256]{1,0:T(8,128)(2,1)S(1)}, u32[]{:S(2)}, u32[]{:S(2)}) %collective-permute-start) | collective-permute-done | bytes 262176 | tf_op jit(solution)/shard_map/ppermute | solution.py:221
  39.9 5.0 %collective-permute-start.1 = (bf16[512,256]{1,0:T(8,128)(2,1)S(1)}, bf16[512,256]{1,0:T(8,128)(2,1)S(1)}, u32[]{:S(2)}, u32[]{:S(2)}) collective-permute-start(bf16[512,256]{1,0:T(8,128)(2,1)S(1)} %collective-permute-done), channel_id=1, source_target_pairs={{0,1},{1,2},{2,3},{3,4},{4,5},{5,6},{6,7},{7,8},{8,9},{9,10},{10,1... | collective-permute-start | bytes 786440 | tf_op jit(solution)/shard_map/ppermute | solution.py:221
  45.0 0.0 collective-permute-done.2
  45.0 3.2 %collective-permute-start.4 = (bf16[512,256]{1,0:T(8,128)(2,1)S(1)}, bf16[512,256]{1,0:T(8,128)(2,1)S(1)}, u32[]{:S(2)}, u32[]{:S(2)}) collective-permute-start(bf16[512,256]{1,0:T(8,128)(2,1)S(1)} %collective-permute-done.2), channel_id=1, source_target_pairs={{0,1},{1,2},{2,3},{3,4},{4,5},{5,6},{6,7},{7,8},{8,9},{9,10},{10,1... | collective-permute-start | bytes 786440 | tf_op jit(solution)/shard_map/ppermute | solution.py:221
  48.3 0.2 fusion.14
  48.5 0.0 collective-permute-done.1
  48.5 4.8 %collective-permute-start.3 = (bf16[512,256]{1,0:T(8,128)(2,1)S(1)}, bf16[512,256]{1,0:T(8,128)(2,1)S(1)}, u32[]{:S(2)}, u32[]{:S(2)}) collective-permute-start(bf16[512,256]{1,0:T(8,128)(2,1)S(1)} %collective-permute-done.1), channel_id=1, source_target_pairs={{0,1},{1,2},{2,3},{3,4},{4,5},{5,6},{6,7},{7,8},{8,9},{9,10},{10,1... | collective-permute-start | bytes 786440 | tf_op jit(solution)/shard_map/ppermute | solution.py:221
  53.3 0.0 collective-permute-done.4
  53.3 3.2 %collective-permute-start.6 = (bf16[512,256]{1,0:T(8,128)(2,1)S(1)}, bf16[512,256]{1,0:T(8,128)(2,1)S(1)}, u32[]{:S(2)}, u32[]{:S(2)}) collective-permute-start(bf16[512,256]{1,0:T(8,128)(2,1)S(1)} %collective-permute-done.4), channel_id=1, source_target_pairs={{0,1},{1,2},{2,3},{3,4},{4,5},{5,6},{6,7},{7,8},{8,9},{9,10},{10,1... | collective-permute-start | bytes 786440 | tf_op jit(solution)/shard_map/ppermute | solution.py:221
  56.5 0.2 convolution_add_fusion.3
  56.7 0.2 fusion.39
  57.0 0.0 collective-permute-done.3
  57.0 4.6 %collective-permute-start.5 = (bf16[512,256]{1,0:T(8,128)(2,1)S(1)}, bf16[512,256]{1,0:T(8,128)(2,1)S(1)}, u32[]{:S(2)}, u32[]{:S(2)}) collective-permute-start(bf16[512,256]{1,0:T(8,128)(2,1)S(1)} %collective-permute-done.3), channel_id=1, source_target_pairs={{0,1},{1,2},{2,3},{3,4},{4,5},{5,6},{6,7},{7,8},{8,9},{9,10},{10,1... | collective-permute-start | bytes 786440 | tf_op jit(solution)/shard_map/ppermute | solution.py:221
  61.6 0.0 collective-permute-done.6
  61.6 3.2 %collective-permute-start.8 = (bf16[512,256]{1,0:T(8,128)(2,1)S(1)}, bf16[512,256]{1,0:T(8,128)(2,1)S(1)}, u32[]{:S(2)}, u32[]{:S(2)}) collective-permute-start(bf16[512,256]{1,0:T(8,128)(2,1)S(1)} %collective-permute-done.6), channel_id=1, source_target_pairs={{0,1},{1,2},{2,3},{3,4},{4,5},{5,6},{6,7},{7,8},{8,9},{9,10},{10,1... | collective-permute-start | bytes 786440 | tf_op jit(solution)/shard_map/ppermute | solution.py:221
  64.8 0.2 fusion.37
  65.0 0.2 fusion.35
  65.3 0.0 collective-permute-done.5
  65.3 4.6 %collective-permute-start.7 = (bf16[512,256]{1,0:T(8,128)(2,1)S(1)}, bf16[512,256]{1,0:T(8,128)(2,1)S(1)}, u32[]{:S(2)}, u32[]{:S(2)}) collective-permute-start(bf16[512,256]{1,0:T(8,128)(2,1)S(1)} %collective-permute-done.5), channel_id=1, source_target_pairs={{0,1},{1,2},{2,3},{3,4},{4,5},{5,6},{6,7},{7,8},{8,9},{9,10},{10,1... | collective-permute-start | bytes 786440 | tf_op jit(solution)/shard_map/ppermute | solution.py:221
  69.9 0.0 collective-permute-done.8
  69.9 3.2 %collective-permute-start.10 = (bf16[512,256]{1,0:T(8,128)(2,1)S(1)}, bf16[512,256]{1,0:T(8,128)(2,1)S(1)}, u32[]{:S(2)}, u32[]{:S(2)}) collective-permute-start(bf16[512,256]{1,0:T(8,128)(2,1)S(1)} %collective-permute-done.8), channel_id=1, source_target_pairs={{0,1},{1,2},{2,3},{3,4},{4,5},{5,6},{6,7},{7,8},{8,9},{9,10},{10,1... | collective-permute-start | bytes 786440 | tf_op jit(solution)/shard_map/ppermute | solution.py:221
  73.1 0.2 fusion.33
  73.4 0.2 fusion.31
  73.6 0.0 collective-permute-done.7
  73.6 4.6 %collective-permute-start.9 = (bf16[512,256]{1,0:T(8,128)(2,1)S(1)}, bf16[512,256]{1,0:T(8,128)(2,1)S(1)}, u32[]{:S(2)}, u32[]{:S(2)}) collective-permute-start(bf16[512,256]{1,0:T(8,128)(2,1)S(1)} %collective-permute-done.7), channel_id=1, source_target_pairs={{0,1},{1,2},{2,3},{3,4},{4,5},{5,6},{6,7},{7,8},{8,9},{9,10},{10,1... | collective-permute-start | bytes 786440 | tf_op jit(solution)/shard_map/ppermute | solution.py:221
  78.2 0.0 collective-permute-done.10
  78.2 3.2 %collective-permute-start.12 = (bf16[512,256]{1,0:T(8,128)(2,1)S(1)}, bf16[512,256]{1,0:T(8,128)(2,1)S(1)}, u32[]{:S(2)}, u32[]{:S(2)}) collective-permute-start(bf16[512,256]{1,0:T(8,128)(2,1)S(1)} %collective-permute-done.10), channel_id=1, source_target_pairs={{0,1},{1,2},{2,3},{3,4},{4,5},{5,6},{6,7},{7,8},{8,9},{9,10},{10,1... | collective-permute-start | bytes 786440 | tf_op jit(solution)/shard_map/ppermute | solution.py:221
  81.4 0.2 fusion.29
  81.7 0.2 fusion.27
  81.9 0.0 collective-permute-done.9
  81.9 4.6 %collective-permute-start.11 = (bf16[512,256]{1,0:T(8,128)(2,1)S(1)}, bf16[512,256]{1,0:T(8,128)(2,1)S(1)}, u32[]{:S(2)}, u32[]{:S(2)}) collective-permute-start(bf16[512,256]{1,0:T(8,128)(2,1)S(1)} %collective-permute-done.9), channel_id=1, source_target_pairs={{0,1},{1,2},{2,3},{3,4},{4,5},{5,6},{6,7},{7,8},{8,9},{9,10},{10,1... | collective-permute-start | bytes 786440 | tf_op jit(solution)/shard_map/ppermute | solution.py:221
  86.5 0.0 collective-permute-done.12
  86.5 1.3 %collective-permute-start.13 = (bf16[512,256]{1,0:T(8,128)(2,1)S(1)}, bf16[512,256]{1,0:T(8,128)(2,1)S(1)}, u32[]{:S(2)}, u32[]{:S(2)}) collective-permute-start(bf16[512,256]{1,0:T(8,128)(2,1)S(1)} %collective-permute-done.12), channel_id=1, source_target_pairs={{0,17},{1,18},{2,19},{3,20},{4,21},{5,22},{6,23},{7,24},{8,25},{9,... | collective-permute-start | bytes 786440 | tf_op jit(solution)/shard_map/ppermute | solution.py:221
  87.8 3.2 %collective-permute-start.15 = (bf16[512,256]{1,0:T(8,128)(2,1)S(1)}, bf16[512,256]{1,0:T(8,128)(2,1)S(1)}, u32[]{:S(2)}, u32[]{:S(2)}) collective-permute-start(bf16[512,256]{1,0:T(8,128)(2,1)S(1)} %collective-permute-done.12), channel_id=1, source_target_pairs={{16,31},{17,16},{18,17},{19,18},{20,19},{21,20},{22,21},{23,22},{2... | collective-permute-start | bytes 786440 | tf_op jit(solution)/shard_map/ppermute | solution.py:221
  91.1 0.2 fusion.25
  91.3 0.2 fusion.23
  91.5 0.0 collective-permute-done.11
  91.5 3.4 %collective-permute-done.15 = bf16[512,256]{1,0:T(8,128)(2,1)S(1)} collective-permute-done((bf16[512,256]{1,0:T(8,128)(2,1)S(1)}, bf16[512,256]{1,0:T(8,128)(2,1)S(1)}, u32[]{:S(2)}, u32[]{:S(2)}) %collective-permute-start.15) | collective-permute-done | bytes 262176 | tf_op jit(solution)/shard_map/ppermute | solution.py:221
  95.0 4.4 %collective-permute-start.16 = (bf16[512,256]{1,0:T(8,128)(2,1)S(1)}, bf16[512,256]{1,0:T(8,128)(2,1)S(1)}, u32[]{:S(2)}, u32[]{:S(2)}) collective-permute-start(bf16[512,256]{1,0:T(8,128)(2,1)S(1)} %collective-permute-done.15), channel_id=1, source_target_pairs={{16,31},{17,16},{18,17},{19,18},{20,19},{21,20},{22,21},{23,22},{2... | collective-permute-start | bytes 786440 | tf_op jit(solution)/shard_map/ppermute | solution.py:221
  99.4 1.9 %collective-permute-start.14 = (bf16[512,256]{1,0:T(8,128)(2,1)S(1)}, bf16[512,256]{1,0:T(8,128)(2,1)S(1)}, u32[]{:S(2)}, u32[]{:S(2)}) collective-permute-start(bf16[512,256]{1,0:T(8,128)(2,1)S(1)} %collective-permute-done.11), channel_id=1, source_target_pairs={{16,31},{17,16},{18,17},{19,18},{20,19},{21,20},{22,21},{23,22},{2... | collective-permute-start | bytes 786440 | tf_op jit(solution)/shard_map/ppermute | solution.py:221
  101.3 0.2 fusion.21
  101.5 0.2 fusion.19
  101.8 0.0 collective-permute-done.13
  101.8 0.2 fusion.12
  102.0 0.7 collective-permute-done.16
  102.7 0.2 fusion.16
  102.9 0.3 fusion.5
  103.2 1.9 %collective-permute-start.17 = (f32[512,256]{1,0:T(8,128)S(1)}, f32[512,256]{1,0:T(8,128)S(1)}, u32[]{:S(2)}, u32[]{:S(2)}) collective-permute-start(f32[512,256]{1,0:T(8,128)S(1)} %fusion.5), channel_id=1, source_target_pairs={{0,16},{16,0},{1,17},{17,1},{2,18},{18,2},{3,19},{19,3},{4,20},{20... | collective-permute-start | bytes 1572872 | tf_op jit(solution)/shard_map/ppermute | solution.py:252
  105.2 0.3 fusion.11
  105.5 1.0 collective-permute-done.14
  106.5 0.2 convolution_add_fusion.1
  106.7 0.3 collective-permute-done.17
  107.0 0.8 add_convert_fusion
  (10 shorter events, 0.0 us)
Async XLA Ops:
  0.0 48.3 %copy-start = (bf16[4096,256]{1,0:T(8,128)(2,1)S(1)}, bf16[4096,256]{1,0:T(8,128)(2,1)}, u32[]{:S(2)}) copy-start(bf16[4096,256]{1,0:T(8,128)(2,1)} %param.13) | copy-start | bytes 6291460
  0.0 14.4 %copy-start.1 = (bf16[512,256]{1,0:T(8,128)(2,1)S(1)}, bf16[512,256]{1,0:T(8,128)(2,1)}, u32[]{:S(2)}) copy-start(bf16[512,256]{1,0:T(8,128)(2,1)} %k_hbm.3) | copy-start | bytes 786436
  0.0 14.4 %copy-start.4 = (f32[16,256]{1,0:T(8,128)S(1)}, f32[16,256]{1,0:T(8,128)}, u32[]{:S(2)}) copy-start(f32[16,256]{1,0:T(8,128)} %rates_ref.1) | copy-start | bytes 49156
  0.0 14.4 %copy-start.5 = (f32[16,256]{1,0:T(8,128)S(1)}, f32[16,256]{1,0:T(8,128)}, u32[]{:S(2)}) copy-start(f32[16,256]{1,0:T(8,128)} %resid_ref.1) | copy-start | bytes 49156
  0.0 14.4 %copy-start.6 = (f32[256]{0:T(256)S(1)}, f32[256]{0:T(256)}, u32[]{:S(2)}) copy-start(f32[256]{0:T(256)} %param.12) | copy-start | bytes 3076
  3.3 22.8 %all-to-all-start = ((f32[32,16,256]{2,1,0:T(8,128)}), f32[32,16,256]{2,1,0:T(8,128)}, u32[]{:S(2)}, u32[]{:S(2)}) async-start(f32[32,16,256]{2,1,0:T(8,128)} %states.1), calls=%async_computation | async-start | bytes 1048576 | tf_op jit(solution)/shard_map/all_to_all | solution.py:193
  14.5 1.0 copy-start.2
  15.4 0.9 copy-start.3
  28.0 11.9 %collective-permute-start = (bf16[512,256]{1,0:T(8,128)(2,1)S(1)}, bf16[512,256]{1,0:T(8,128)(2,1)S(1)}, u32[]{:S(2)}, u32[]{:S(2)}) collective-permute-start(bf16[512,256]{1,0:T(8,128)(2,1)S(1)} %carry_and_gate.1), channel_id=1, source_target_pairs={{0,1},{1,2},{2,3},{3,4},{4,5},{5,6},{6,7},{7,8},{8,9},{9,10},{10,1... | collective-permute-start | bytes 786440 | tf_op jit(solution)/shard_map/ppermute | solution.py:221
  36.6 8.3 %collective-permute-start.2 = (bf16[512,256]{1,0:T(8,128)(2,1)S(1)}, bf16[512,256]{1,0:T(8,128)(2,1)S(1)}, u32[]{:S(2)}, u32[]{:S(2)}) collective-permute-start(bf16[512,256]{1,0:T(8,128)(2,1)S(1)} %carry_and_gate.1), channel_id=1, source_target_pairs={{16,1},{17,2},{18,3},{19,4},{20,5},{21,6},{22,7},{23,8},{24,9},{25... | collective-permute-start | bytes 786440 | tf_op jit(solution)/shard_map/ppermute | solution.py:221
  39.9 8.6 %collective-permute-start.1 = (bf16[512,256]{1,0:T(8,128)(2,1)S(1)}, bf16[512,256]{1,0:T(8,128)(2,1)S(1)}, u32[]{:S(2)}, u32[]{:S(2)}) collective-permute-start(bf16[512,256]{1,0:T(8,128)(2,1)S(1)} %collective-permute-done), channel_id=1, source_target_pairs={{0,1},{1,2},{2,3},{3,4},{4,5},{5,6},{6,7},{7,8},{8,9},{9,10},{10,1... | collective-permute-start | bytes 786440 | tf_op jit(solution)/shard_map/ppermute | solution.py:221
  45.0 8.3 %collective-permute-start.4 = (bf16[512,256]{1,0:T(8,128)(2,1)S(1)}, bf16[512,256]{1,0:T(8,128)(2,1)S(1)}, u32[]{:S(2)}, u32[]{:S(2)}) collective-permute-start(bf16[512,256]{1,0:T(8,128)(2,1)S(1)} %collective-permute-done.2), channel_id=1, source_target_pairs={{0,1},{1,2},{2,3},{3,4},{4,5},{5,6},{6,7},{7,8},{8,9},{9,10},{10,1... | collective-permute-start | bytes 786440 | tf_op jit(solution)/shard_map/ppermute | solution.py:221
  48.5 8.5 %collective-permute-start.3 = (bf16[512,256]{1,0:T(8,128)(2,1)S(1)}, bf16[512,256]{1,0:T(8,128)(2,1)S(1)}, u32[]{:S(2)}, u32[]{:S(2)}) collective-permute-start(bf16[512,256]{1,0:T(8,128)(2,1)S(1)} %collective-permute-done.1), channel_id=1, source_target_pairs={{0,1},{1,2},{2,3},{3,4},{4,5},{5,6},{6,7},{7,8},{8,9},{9,10},{10,1... | collective-permute-start | bytes 786440 | tf_op jit(solution)/shard_map/ppermute | solution.py:221
  53.3 8.3 %collective-permute-start.6 = (bf16[512,256]{1,0:T(8,128)(2,1)S(1)}, bf16[512,256]{1,0:T(8,128)(2,1)S(1)}, u32[]{:S(2)}, u32[]{:S(2)}) collective-permute-start(bf16[512,256]{1,0:T(8,128)(2,1)S(1)} %collective-permute-done.4), channel_id=1, source_target_pairs={{0,1},{1,2},{2,3},{3,4},{4,5},{5,6},{6,7},{7,8},{8,9},{9,10},{10,1... | collective-permute-start | bytes 786440 | tf_op jit(solution)/shard_map/ppermute | solution.py:221
  57.0 8.3 %collective-permute-start.5 = (bf16[512,256]{1,0:T(8,128)(2,1)S(1)}, bf16[512,256]{1,0:T(8,128)(2,1)S(1)}, u32[]{:S(2)}, u32[]{:S(2)}) collective-permute-start(bf16[512,256]{1,0:T(8,128)(2,1)S(1)} %collective-permute-done.3), channel_id=1, source_target_pairs={{0,1},{1,2},{2,3},{3,4},{4,5},{5,6},{6,7},{7,8},{8,9},{9,10},{10,1... | collective-permute-start | bytes 786440 | tf_op jit(solution)/shard_map/ppermute | solution.py:221
  61.6 8.3 %collective-permute-start.8 = (bf16[512,256]{1,0:T(8,128)(2,1)S(1)}, bf16[512,256]{1,0:T(8,128)(2,1)S(1)}, u32[]{:S(2)}, u32[]{:S(2)}) collective-permute-start(bf16[512,256]{1,0:T(8,128)(2,1)S(1)} %collective-permute-done.6), channel_id=1, source_target_pairs={{0,1},{1,2},{2,3},{3,4},{4,5},{5,6},{6,7},{7,8},{8,9},{9,10},{10,1... | collective-permute-start | bytes 786440 | tf_op jit(solution)/shard_map/ppermute | solution.py:221
  65.3 8.3 %collective-permute-start.7 = (bf16[512,256]{1,0:T(8,128)(2,1)S(1)}, bf16[512,256]{1,0:T(8,128)(2,1)S(1)}, u32[]{:S(2)}, u32[]{:S(2)}) collective-permute-start(bf16[512,256]{1,0:T(8,128)(2,1)S(1)} %collective-permute-done.5), channel_id=1, source_target_pairs={{0,1},{1,2},{2,3},{3,4},{4,5},{5,6},{6,7},{7,8},{8,9},{9,10},{10,1... | collective-permute-start | bytes 786440 | tf_op jit(solution)/shard_map/ppermute | solution.py:221
  69.9 8.3 %collective-permute-start.10 = (bf16[512,256]{1,0:T(8,128)(2,1)S(1)}, bf16[512,256]{1,0:T(8,128)(2,1)S(1)}, u32[]{:S(2)}, u32[]{:S(2)}) collective-permute-start(bf16[512,256]{1,0:T(8,128)(2,1)S(1)} %collective-permute-done.8), channel_id=1, source_target_pairs={{0,1},{1,2},{2,3},{3,4},{4,5},{5,6},{6,7},{7,8},{8,9},{9,10},{10,1... | collective-permute-start | bytes 786440 | tf_op jit(solution)/shard_map/ppermute | solution.py:221
  73.6 8.3 %collective-permute-start.9 = (bf16[512,256]{1,0:T(8,128)(2,1)S(1)}, bf16[512,256]{1,0:T(8,128)(2,1)S(1)}, u32[]{:S(2)}, u32[]{:S(2)}) collective-permute-start(bf16[512,256]{1,0:T(8,128)(2,1)S(1)} %collective-permute-done.7), channel_id=1, source_target_pairs={{0,1},{1,2},{2,3},{3,4},{4,5},{5,6},{6,7},{7,8},{8,9},{9,10},{10,1... | collective-permute-start | bytes 786440 | tf_op jit(solution)/shard_map/ppermute | solution.py:221
  78.2 8.3 %collective-permute-start.12 = (bf16[512,256]{1,0:T(8,128)(2,1)S(1)}, bf16[512,256]{1,0:T(8,128)(2,1)S(1)}, u32[]{:S(2)}, u32[]{:S(2)}) collective-permute-start(bf16[512,256]{1,0:T(8,128)(2,1)S(1)} %collective-permute-done.10), channel_id=1, source_target_pairs={{0,1},{1,2},{2,3},{3,4},{4,5},{5,6},{6,7},{7,8},{8,9},{9,10},{10,1... | collective-permute-start | bytes 786440 | tf_op jit(solution)/shard_map/ppermute | solution.py:221
  81.9 9.6 %collective-permute-start.11 = (bf16[512,256]{1,0:T(8,128)(2,1)S(1)}, bf16[512,256]{1,0:T(8,128)(2,1)S(1)}, u32[]{:S(2)}, u32[]{:S(2)}) collective-permute-start(bf16[512,256]{1,0:T(8,128)(2,1)S(1)} %collective-permute-done.9), channel_id=1, source_target_pairs={{0,1},{1,2},{2,3},{3,4},{4,5},{5,6},{6,7},{7,8},{8,9},{9,10},{10,1... | collective-permute-start | bytes 786440 | tf_op jit(solution)/shard_map/ppermute | solution.py:221
  86.5 15.2 %collective-permute-start.13 = (bf16[512,256]{1,0:T(8,128)(2,1)S(1)}, bf16[512,256]{1,0:T(8,128)(2,1)S(1)}, u32[]{:S(2)}, u32[]{:S(2)}) collective-permute-start(bf16[512,256]{1,0:T(8,128)(2,1)S(1)} %collective-permute-done.12), channel_id=1, source_target_pairs={{0,17},{1,18},{2,19},{3,20},{4,21},{5,22},{6,23},{7,24},{8,25},{9,... | collective-permute-start | bytes 786440 | tf_op jit(solution)/shard_map/ppermute | solution.py:221
  87.8 7.1 %collective-permute-start.15 = (bf16[512,256]{1,0:T(8,128)(2,1)S(1)}, bf16[512,256]{1,0:T(8,128)(2,1)S(1)}, u32[]{:S(2)}, u32[]{:S(2)}) collective-permute-start(bf16[512,256]{1,0:T(8,128)(2,1)S(1)} %collective-permute-done.12), channel_id=1, source_target_pairs={{16,31},{17,16},{18,17},{19,18},{20,19},{21,20},{22,21},{23,22},{2... | collective-permute-start | bytes 786440 | tf_op jit(solution)/shard_map/ppermute | solution.py:221
  95.0 7.7 %collective-permute-start.16 = (bf16[512,256]{1,0:T(8,128)(2,1)S(1)}, bf16[512,256]{1,0:T(8,128)(2,1)S(1)}, u32[]{:S(2)}, u32[]{:S(2)}) collective-permute-start(bf16[512,256]{1,0:T(8,128)(2,1)S(1)} %collective-permute-done.15), channel_id=1, source_target_pairs={{16,31},{17,16},{18,17},{19,18},{20,19},{21,20},{22,21},{23,22},{2... | collective-permute-start | bytes 786440 | tf_op jit(solution)/shard_map/ppermute | solution.py:221
  99.4 7.1 %collective-permute-start.14 = (bf16[512,256]{1,0:T(8,128)(2,1)S(1)}, bf16[512,256]{1,0:T(8,128)(2,1)S(1)}, u32[]{:S(2)}, u32[]{:S(2)}) collective-permute-start(bf16[512,256]{1,0:T(8,128)(2,1)S(1)} %collective-permute-done.11), channel_id=1, source_target_pairs={{16,31},{17,16},{18,17},{19,18},{20,19},{21,20},{22,21},{23,22},{2... | collective-permute-start | bytes 786440 | tf_op jit(solution)/shard_map/ppermute | solution.py:221
  103.2 3.8 %collective-permute-start.17 = (f32[512,256]{1,0:T(8,128)S(1)}, f32[512,256]{1,0:T(8,128)S(1)}, u32[]{:S(2)}, u32[]{:S(2)}) collective-permute-start(f32[512,256]{1,0:T(8,128)S(1)} %fusion.5), channel_id=1, source_target_pairs={{0,16},{16,0},{1,17},{17,1},{2,18},{18,2},{3,19},{19,3},{4,20},{20... | collective-permute-start | bytes 1572872 | tf_op jit(solution)/shard_map/ppermute | solution.py:252
